TPU v7x, 128 devices: a whole 4x4x4 slice. The times are simulated.
128 devices in a mesh: sec: 2 (over x_hi), row: 16 (over y, x_lo, core), col: 4 (over z).
Axes of the slice: x: 4 (x_hi: 2, x_lo: 2; x = x_hi * 2 + x_lo), y: 4, z: 4, core: 2. Of those that a mesh axis runs over, the one named last changes fastest.
Arguments:
- coarse_state: bfloat16 [720, 78, 1440], P('row', None, ('sec', 'col'))
- row_offset: int32 [1], replicated, may hold values from 1 to 703
- col_offset: int32 [1], replicated, may hold values from 1 to 1375
- fine_static: bfloat16 [256, 4, 1024], P('row', None, ('sec', 'col'))
- w_lift: bfloat16 [78, 256], replicated, may hold values from -0.625 to 0.625
- w_static: bfloat16 [4, 256], replicated, may hold values from -3 to 3
- norm_gains: float32 [4, 256], replicated, may hold values from 0.1 to 1.9
- kernels: bfloat16 [4, 3, 3, 256, 256], replicated, may hold values from -0.125 to 0.125
- w_head: bfloat16 [256, 78], replicated, may hold values from -0.375 to 0.375
- cotangent: bfloat16 [256, 78, 1024], P('row', None, ('sec', 'col')), may hold values from -6 to 6
Outputs:
- fine_out: bfloat16 [256, 78, 1024], P('row', None, ('sec', 'col'))
- coarse_grad: float32 [720, 78, 1440], P('row', None, ('sec', 'col'))
Inputs may be any that keep to these rules, and one draw needn't show every extreme that they name: The slab's coarse rows, one before row_offset to 16 after it, lie inside the grid. The slab's coarse columns, one before col_offset to 64 after it, lie inside the grid.
All inputs are finite; a program needn't handle non-finite values.
Results may differ from a plain program's by a relative error of at most 0.015.
Values may be sent and summed in bfloat16 or wider, within the bound.
No kernel may reach another device: no remote copies, remote signals or barrier semaphores. Data moves between devices by JAX's collectives and lax.ppermute only.
A program may use at most 128 MiB of HBM per device.

v0:
```python
import jax
import jax.numpy as jnp
from jax import lax
from jax.sharding import PartitionSpec as P

R = 16


def broadcast(x, axis, root):
    mine = lax.axis_index(axis) == root
    return lax.psum(jnp.where(mine, x, jnp.zeros_like(x)), axis)


def padded_2(x, sides, width):
    for axis, dim in sides:
        count, length = (lax.axis_size(axis), x.shape[dim])
        up = [(i, (i + 1) % count) for i in range(count - 1)]
        down = [(j, i) for i, j in up]
        last = lax.slice_in_dim(x, length - width, length, axis=dim)
        initial = lax.slice_in_dim(x, 0, width, axis=dim)
        before = lax.ppermute(last, axis, up)
        after = lax.ppermute(initial, axis, down)
        x = jnp.concatenate([before, x, after], axis=dim)
    return x


def interp_matrix(fine_len, ratio_cells):
    fine_idx = jnp.arange(fine_len, dtype=jnp.int32)
    numerator = 2 * fine_idx + 1 + ratio_cells
    lower_row = numerator // (2 * ratio_cells)
    weight_hi = (numerator % (2 * ratio_cells)).astype(jnp.float32) / (2.0 * ratio_cells)
    columns = jnp.arange(fine_len // ratio_cells + 2, dtype=jnp.int32)
    below_hot = (columns[None, :] == lower_row[:, None]).astype(jnp.float32)
    above_hot = (columns[None, :] == lower_row[:, None] + 1).astype(jnp.float32)
    return below_hot * (1.0 - weight_hi[:, None]) + above_hot * weight_hi[:, None]


def conv_sum(padded, kernel_set, row_count, col_count, transpose):
    width_out = kernel_set.shape[-1]
    accumulated = jnp.zeros((row_count * col_count, width_out), jnp.float32)
    for offset_dy in range(3):
        for offset_dx in range(3):
            if transpose:
                window = padded[
                    2 - offset_dy : 2 - offset_dy + row_count,
                    2 - offset_dx : 2 - offset_dx + col_count,
                    :,
                ]
                weight = kernel_set[offset_dy, offset_dx].T
            else:
                window = padded[
                    offset_dy : offset_dy + row_count, offset_dx : offset_dx + col_count, :
                ]
                weight = kernel_set[offset_dy, offset_dx]
            accumulated = accumulated + jnp.dot(
                window.reshape(row_count * col_count, -1),
                weight,
                preferred_element_type=jnp.float32,
            )
    return accumulated.reshape(row_count, col_count, -1)


def normalize(hidden, gain_row):
    hidden_f = hidden.astype(jnp.float32)
    inv_scale = lax.rsqrt(jnp.mean(hidden_f * hidden_f, axis=-1, keepdims=True) + 1e-06)
    return (hidden_f * inv_scale * gain_row[None, None, :], inv_scale)


def norm_backward(hidden, inv_scale, normed, gain_row, conv_back):
    hidden_f = hidden.astype(jnp.float32)
    sigmoid_val = jax.nn.sigmoid(normed)
    scaled_grad = (
        conv_back * sigmoid_val * (1.0 + normed * (1.0 - sigmoid_val)) * gain_row[None, None, :]
    )
    cubed = inv_scale * inv_scale * inv_scale
    return inv_scale * scaled_grad - hidden_f * cubed * jnp.mean(
        hidden_f * scaled_grad, axis=-1, keepdims=True
    )


def shards(
    coarse_state,
    row_offset,
    col_offset,
    fine_static,
    w_lift,
    w_static,
    norm_gains,
    kernels,
    w_head,
    cotangent,
):
    high = lax.Precision.HIGHEST
    lat_dev, channels, lon_dev = coarse_state.shape
    tile_rows = fine_static.shape[0]
    tile_cols = fine_static.shape[2]
    rows_size = lax.axis_size("row")
    cols_size = lax.axis_size(("sec", "col"))
    row_index = lax.axis_index("row")
    col_index = lax.axis_index(("sec", "col"))
    coarse_rows = tile_rows // R
    coarse_cols = tile_cols // R
    span_rows = rows_size * coarse_rows + 2
    span_cols = cols_size * coarse_cols + 2
    first_row = row_offset[0] - 1
    first_col = col_offset[0] - 1
    first_strip = first_row // lat_dev
    first_shard = first_col // lon_dev
    strip_count = (span_rows + 2 * lat_dev - 2) // lat_dev
    shard_count = (span_cols + 2 * lon_dev - 2) // lon_dev
    pieces = []
    for strip_k in range(strip_count):
        root_index = jnp.minimum(first_strip + strip_k, rows_size - 1)
        pieces.append(broadcast(coarse_state, "row", root_index))
    stacked = jnp.concatenate(pieces, 0)
    row_band = lax.dynamic_slice_in_dim(stacked, first_row - first_strip * lat_dev, span_rows, 0)
    pieces = []
    for shard_k in range(shard_count):
        root_index = jnp.minimum(first_shard + shard_k, cols_size - 1)
        pieces.append(broadcast(row_band, ("sec", "col"), root_index))
    stacked = jnp.concatenate(pieces, 2)
    footprint = lax.dynamic_slice_in_dim(stacked, first_col - first_shard * lon_dev, span_cols, 2)
    window = lax.dynamic_slice(
        footprint,
        (row_index * coarse_rows, jnp.int32(0), col_index * coarse_cols),
        (coarse_rows + 2, channels, coarse_cols + 2),
    )
    rows_mat = interp_matrix(tile_rows, R)
    cols_mat = interp_matrix(tile_cols, R)
    partial_up = jnp.einsum("yi,icj->ycj", rows_mat, window.astype(jnp.float32), precision=high)
    upsampled = jnp.einsum("ycj,xj->ycx", partial_up, cols_mat, precision=high).astype(jnp.bfloat16)
    hidden = (
        jnp.einsum("ycx,cw->yxw", upsampled, w_lift, preferred_element_type=jnp.float32)
        + jnp.einsum("ykx,kw->yxw", fine_static, w_static, preferred_element_type=jnp.float32)
    ).astype(jnp.bfloat16)
    saved_hidden = []
    for block_idx in range(kernels.shape[0]):
        saved_hidden.append(hidden)
        normed, inv_scale = normalize(hidden, norm_gains[block_idx])
        activated = (normed * jax.nn.sigmoid(normed)).astype(jnp.bfloat16)
        padded = padded_2(activated, (("row", 0), (("sec", "col"), 1)), 1)
        hidden = (
            hidden.astype(jnp.float32)
            + conv_sum(padded, kernels[block_idx], tile_rows, tile_cols, False)
        ).astype(jnp.bfloat16)
    fine_out = jnp.einsum("yxw,wc->ycx", hidden, w_head, preferred_element_type=jnp.float32).astype(
        jnp.bfloat16
    )
    grad_back = jnp.einsum("ycx,wc->yxw", cotangent, w_head, preferred_element_type=jnp.float32)
    for block_idx in reversed(range(kernels.shape[0])):
        sent = grad_back.astype(jnp.bfloat16)
        padded = padded_2(sent, (("row", 0), (("sec", "col"), 1)), 1)
        conv_back = conv_sum(padded, kernels[block_idx], tile_rows, tile_cols, True)
        normed, inv_scale = normalize(saved_hidden[block_idx], norm_gains[block_idx])
        grad_back = grad_back + norm_backward(
            saved_hidden[block_idx], inv_scale, normed, norm_gains[block_idx], conv_back
        )
    lifted_back = grad_back.astype(jnp.bfloat16)
    up_back = jnp.einsum("yxw,cw->ycx", lifted_back, w_lift, preferred_element_type=jnp.float32)
    window_back = jnp.einsum("yi,ycx->icx", rows_mat, up_back, precision=high)
    window_back = jnp.einsum("icx,xj->icj", window_back, cols_mat, precision=high)
    zero_grid = jnp.zeros((span_rows, channels, span_cols), jnp.float32)
    placed = lax.dynamic_update_slice(
        zero_grid, window_back, (row_index * coarse_rows, jnp.int32(0), col_index * coarse_cols)
    )
    summed = lax.psum(placed, ("sec", "row", "col"))
    row_global = row_index * lat_dev + jnp.arange(lat_dev, dtype=jnp.int32) - first_row
    row_valid = ((row_global >= 0) & (row_global < span_rows)).astype(jnp.float32)
    col_global = col_index * lon_dev + jnp.arange(lon_dev, dtype=jnp.int32) - first_col
    col_valid = ((col_global >= 0) & (col_global < span_cols)).astype(jnp.float32)
    picked = jnp.take(summed, jnp.clip(row_global, 0, span_rows - 1), axis=0)
    picked = jnp.take(picked, jnp.clip(col_global, 0, span_cols - 1), axis=2)
    coarse_grad = picked * row_valid[:, None, None] * col_valid[None, None, :]
    return (fine_out, coarse_grad)


def solution(mesh):
    in_specs = (
        P("row", None, ("sec", "col")),
        P(),
        P(),
        P("row", None, ("sec", "col")),
        P(),
        P(),
        P(),
        P(),
        P(),
        P("row", None, ("sec", "col")),
    )
    out_specs = (P("row", None, ("sec", "col")), P("row", None, ("sec", "col")))
    return jax.shard_map(shards, mesh=mesh, in_specs=in_specs, out_specs=out_specs, check_vma=False)
```

profile of v0, /device:TPU:0, one launch (start us, length us, event | category | flops | bytes accessed | tf_op | source)
XLA Modules:
  0.0 629.2 jit_solution(5450822614188079841)
XLA Ops:
  7.9 1.5 fusion.186
  9.4 1.3 collective-permute-start.16
  10.7 1.3 collective-permute-start.17
  12.7 4.7 copy.17
  17.4 4.0 broadcast_select_fusion
  24.1 4.2 slice_bitcast_fusion
  28.5 1.3 collective-permute-start.18
  29.8 5.0 collective-permute-start.19
  37.2 2.6 fusion.167
  40.3 1.8 convolution_add_fusion.26
  42.2 122.8 %all-reduce.8.cloned.1.call-done = (bf16[45,78,180]{1,0,2:T(8,128)(2,1)}, bf16[45,78,180]{1,0,2:T(8,128)(2,1)}) async-done(((bf16[45,78,180]{1,0,2:T(8,128)(2,1)}, bf16[45,78,180]{1,0,2:T(8,128)(2,1)}), (bf16[45,78,180]{1,0,2:T(8,128)(2,1)}, bf16[45,78,180]{1,0,2:T(8,128)(2,1)})) %all-reduce.8.cloned.1.call-update) | async-done | bytes 2527216 | tf_op jit(solution)/shard_map/psum | solution.py:11
  165.0 3.9 broadcast_select_fusion.2
  170.0 2.4 convolution_add_fusion.25
  172.4 1.5 convolution_add_fusion.24
  173.9 2.7 convolution_add_fusion.23
  176.6 87.3 %all-reduce.10.cloned.1.call-done = (bf16[18,78,180]{1,0,2:T(8,128)(2,1)}, bf16[18,78,180]{1,0,2:T(8,128)(2,1)}) async-done(((bf16[18,78,180]{1,0,2:T(8,128)(2,1)}, bf16[18,78,180]{1,0,2:T(8,128)(2,1)}), (bf16[18,78,180]{1,0,2:T(8,128)(2,1)}, bf16[18,78,180]{1,0,2:T(8,128)(2,1)})) %all-reduce.10.cloned.1.call-update) | async-done | bytes 1010896 | tf_op jit(solution)/shard_map/psum | solution.py:11
  268.7 1.3 collective-permute-start
  270.0 1.3 collective-permute-start.1
  271.8 2.1 collective-permute-done.1
  275.3 1.5 collective-permute-start.3
  277.4 3.5 collective-permute-done.3
  287.5 3.7 collective-permute-start.4
  291.2 1.3 collective-permute-start.5
  293.0 2.0 collective-permute-done.5
  295.0 3.2 collective-permute-start.6
  298.2 1.5 collective-permute-start.7
  300.4 4.4 collective-permute-done.7
  311.4 3.7 collective-permute-start.8
  315.1 1.3 collective-permute-start.9
  316.9 1.9 collective-permute-done.9
  318.9 7.5 %collective-permute-start.10 = (bf16[18,1,256]{2,1,0:T(2,128)(2,1)S(1)}, bf16[18,1,256]{2,1,0:T(2,128)(2,1)S(1)}, u32[]{:S(2)}, u32[]{:S(2)}) collective-permute-start(bf16[18,1,256]{2,1,0:T(2,128)(2,1)S(1)} %get-tuple-element.98), channel_id=1, source_target_pairs={{0,1},{1,2},{2,3},{3,64},{64,65},{65,66},{66,67},{4,5},{5,6},{6,7}... | collective-permute-start | bytes 27656 | tf_op jit(solution)/shard_map/ppermute | solution.py:21
  326.5 1.8 collective-permute-start.11
  328.8 3.3 collective-permute-done.11
  338.0 1.5 fusion.76
  339.5 1.6 fusion.87
  341.1 4.1 collective-permute-start.20
  345.2 1.3 collective-permute-start.21
  346.5 2.7 collective-permute-done.21
  349.3 1.3 collective-permute-start.22
  350.6 6.3 %collective-permute-start.23 = (bf16[18,1,256]{2,1,0:T(2,128)(2,1)S(1)}, bf16[18,1,256]{2,1,0:T(2,128)(2,1)S(1)}, u32[]{:S(2)}, u32[]{:S(2)}) collective-permute-start(bf16[18,1,256]{2,1,0:T(2,128)(2,1)S(1)} %get-tuple-element.87), channel_id=1, source_target_pairs={{0,1},{1,2},{2,3},{3,64},{64,65},{65,66},{66,67},{4,5},{5,6},{6,7}... | collective-permute-start | bytes 27656 | tf_op jit(solution)/shard_map/ppermute | solution.py:21
  364.0 1.5 fusion.59
  365.4 3.2 fusion.155
  368.7 4.9 collective-permute-start.24
  373.6 1.3 collective-permute-start.25
  374.9 3.4 collective-permute-start.12
  378.3 1.3 collective-permute-start.13
  380.2 1.3 collective-permute-start.26
  381.5 4.8 collective-permute-start.27
  387.0 5.3 collective-permute-start.14
  392.3 1.5 collective-permute-start.15
  399.5 1.5 fusion.42
  401.0 1.6 fusion.89
  402.6 4.9 collective-permute-start.28
  407.5 1.3 collective-permute-start.29
  414.4 1.3 collective-permute-start.30
  415.7 8.7 %collective-permute-start.31 = (bf16[18,1,256]{2,1,0:T(2,128)(2,1)S(1)}, bf16[18,1,256]{2,1,0:T(2,128)(2,1)S(1)}, u32[]{:S(2)}, u32[]{:S(2)}) collective-permute-start(bf16[18,1,256]{2,1,0:T(2,128)(2,1)S(1)} %get-tuple-element.79), channel_id=1, source_target_pairs={{0,1},{1,2},{2,3},{3,64},{64,65},{65,66},{66,67},{4,5},{5,6},{6,7}... | collective-permute-start | bytes 27656 | tf_op jit(solution)/shard_map/ppermute | solution.py:21
  431.6 1.5 fusion.25
  433.2 5.9 convolution_bitcast_fusion
  441.0 1.4 dynamic_update_slice.3
  443.7 161.6 %all-reduce.6.cloned.1.call-done = f32[18,78,66]{1,2,0:T(8,128)} async-done(((f32[18,78,66]{1,2,0:T(8,128)}), f32[18,78,66]{1,2,0:T(8,128)}) %all-reduce.6.cloned.1.call-update) | async-done | bytes 370672 | tf_op jit(solution)/shard_map/psum | solution.py:166
  605.3 1.9 gather_fusion
  607.7 3.2 gather_fusion.1
  610.9 5.2 multiply_bitcast_fusion
  616.1 6.2 copy.25
  (261 shorter events, 65.1 us)
Async XLA Ops:
  7.2 157.8 %all-reduce.8.cloned.1.call-start = ((), (), s32[]{:S(2)}) async-start(), calls=%async_computation.1 | async-start | bytes 8847360 | tf_op jit(solution)/shard_map/psum | solution.py:11
  9.4 19.0 %collective-permute-start.16 = (bf16[1,128,256]{2,1,0:T(8,128)(2,1)S(1)}, bf16[1,128,256]{2,1,0:T(8,128)(2,1)S(1)}, u32[]{:S(2)}, u32[]{:S(2)}) collective-permute-start(bf16[1,128,256]{2,1,0:T(8,128)(2,1)S(1)} %get-tuple-element.123), channel_id=1, source_target_pairs={{0,4},{4,8},{8,12},{12,16},{16,20},{20,24},{24,28},{28,32},{32,36}... | collective-permute-start | bytes 196616 | tf_op jit(solution)/shard_map/ppermute | solution.py:21
  10.7 17.7 %collective-permute-start.17 = (bf16[1,128,256]{2,1,0:T(8,128)(2,1)S(1)}, bf16[1,128,256]{2,1,0:T(8,128)(2,1)S(1)}, u32[]{:S(2)}, u32[]{:S(2)}) collective-permute-start(bf16[1,128,256]{2,1,0:T(8,128)(2,1)S(1)} %get-tuple-element.124), channel_id=1, source_target_pairs={{4,0},{8,4},{12,8},{16,12},{20,16},{24,20},{28,24},{32,28},{36,32}... | collective-permute-start | bytes 196616 | tf_op jit(solution)/shard_map/ppermute | solution.py:22
  21.5 242.4 %all-reduce.10.cloned.1.call-start = ((), (), s32[]{:S(2)}) async-start(), calls=%async_computation.2 | async-start | bytes 4423680 | tf_op jit(solution)/shard_map/psum | solution.py:11
  22.2 241.7 %copy-start.21 = (s32[16]{0:T(128)}, s32[16]{0:T(128)S(1)}, u32[]{:S(2)}) copy-start(s32[16]{0:T(128)S(1)} %get-tuple-element.163) | copy-start | bytes 196
  22.2 241.7 %copy-start.23 = (s32[16]{0:T(128)}, s32[16]{0:T(128)S(1)}, u32[]{:S(2)}) copy-start(s32[16]{0:T(128)S(1)} %get-tuple-element.164) | copy-start | bytes 196
  22.2 241.7 %copy-start.25 = (f32[16]{0:T(128)}, f32[16]{0:T(128)S(1)}, u32[]{:S(2)}) copy-start(f32[16]{0:T(128)S(1)} %get-tuple-element.165) | copy-start | bytes 196
  22.2 241.7 %copy-start.27 = (f32[16]{0:T(128)}, f32[16]{0:T(128)S(1)}, u32[]{:S(2)}) copy-start(f32[16]{0:T(128)S(1)} %get-tuple-element.166) | copy-start | bytes 196
  22.9 245.1 %copy-start.16 = (f32[1,256]{1,0:T(1,128)}, f32[1,256]{1,0:T(1,128)S(1)}, u32[]{:S(2)}) copy-start(f32[1,256]{1,0:T(1,128)S(1)} %get-tuple-element.151) | copy-start | bytes 3076
  24.1 240.9 %copy-start.29 = (s32[128]{0:T(128)}, s32[128]{0:T(128)S(1)}, u32[]{:S(2)}) copy-start(s32[128]{0:T(128)S(1)} %get-tuple-element.161) | copy-start | bytes 1540
  24.1 240.9 %copy-start.31 = (s32[128]{0:T(128)}, s32[128]{0:T(128)S(1)}, u32[]{:S(2)}) copy-start(s32[128]{0:T(128)S(1)} %get-tuple-element.162) | copy-start | bytes 1540
  28.4 12.0 %copy-start.2 = (bf16[3,3,256,256]{3,2,1,0:T(8,128)(2,1)}, bf16[3,3,256,256]{3,2,1,0:T(8,128)(2,1)S(1)}, u32[]{:S(2)}) copy-start(bf16[3,3,256,256]{3,2,1,0:T(8,128)(2,1)S(1)} %get-tuple-element.22) | copy-start | bytes 3538948
  28.4 236.6 %copy-start.33 = (f32[128]{0:T(128)}, f32[128]{0:T(128)S(1)}, u32[]{:S(2)}) copy-start(f32[128]{0:T(128)S(1)} %get-tuple-element.167) | copy-start | bytes 1540
  28.4 236.6 %copy-start.35 = (f32[128]{0:T(128)}, f32[128]{0:T(128)S(1)}, u32[]{:S(2)}) copy-start(f32[128]{0:T(128)S(1)} %get-tuple-element.168) | copy-start | bytes 1540
  28.5 7.9 %collective-permute-start.18 = (bf16[18,1,256]{2,1,0:T(2,128)(2,1)S(1)}, bf16[18,1,256]{2,1,0:T(2,128)(2,1)S(1)}, u32[]{:S(2)}, u32[]{:S(2)}) collective-permute-start(bf16[18,1,256]{2,1,0:T(2,128)(2,1)S(1)} %get-tuple-element.90), channel_id=1, source_target_pairs={{1,0},{2,1},{3,2},{64,3},{65,64},{66,65},{67,66},{5,4},{6,5},{7,6}... | collective-permute-start | bytes 27656 | tf_op jit(solution)/shard_map/ppermute | solution.py:22
  29.8 6.6 %collective-permute-start.19 = (bf16[18,1,256]{2,1,0:T(2,128)(2,1)S(1)}, bf16[18,1,256]{2,1,0:T(2,128)(2,1)S(1)}, u32[]{:S(2)}, u32[]{:S(2)}) collective-permute-start(bf16[18,1,256]{2,1,0:T(2,128)(2,1)S(1)} %get-tuple-element.91), channel_id=1, source_target_pairs={{0,1},{1,2},{2,3},{3,64},{64,65},{65,66},{66,67},{4,5},{5,6},{6,7}... | collective-permute-start | bytes 27656 | tf_op jit(solution)/shard_map/ppermute | solution.py:21
  169.9 435.4 %all-reduce.6.cloned.1.call-start = ((), (), s32[]{:S(2)}) async-start(), calls=%async_computation | async-start | bytes 1327104 | tf_op jit(solution)/shard_map/psum | solution.py:166
  176.6 89.6 %copy-start.13 = (bf16[78,256]{1,0:T(8,128)(2,1)S(1)}, bf16[78,256]{1,0:T(8,128)(2,1)}, u32[]{:S(2)}) copy-start(bf16[78,256]{1,0:T(8,128)(2,1)} %param.14) | copy-start | bytes 119812
  266.7 4.6 copy-start.3
  266.8 4.6 copy-start.6
  266.8 4.6 copy-start.9
  268.0 3.3 copy-start.11
  268.7 3.1 collective-permute-start
  270.0 4.0 collective-permute-start.1
  271.8 5.1 copy-start.1
  274.0 3.4 collective-permute-start.2
  275.3 5.7 collective-permute-start.3
  286.8 5.7 copy-start.8
  287.5 5.5 collective-permute-start.4
  291.2 3.8 collective-permute-start.5
  293.0 6.9 %copy-start.4 = (bf16[3,3,256,256]{3,2,1,0:T(8,128)(2,1)S(1)}, bf16[3,3,256,256]{3,2,1,0:T(8,128)(2,1)}, u32[]{:S(2)}) copy-start(bf16[3,3,256,256]{3,2,1,0:T(8,128)(2,1)} %get-tuple-element.23) | copy-start | bytes 3538948
  295.0 5.3 collective-permute-start.6
  298.2 6.6 %collective-permute-start.7 = (bf16[18,1,256]{2,1,0:T(2,128)(2,1)S(1)}, bf16[18,1,256]{2,1,0:T(2,128)(2,1)S(1)}, u32[]{:S(2)}, u32[]{:S(2)}) collective-permute-start(bf16[18,1,256]{2,1,0:T(2,128)(2,1)S(1)} %get-tuple-element.103), channel_id=1, source_target_pairs={{1,0},{2,1},{3,2},{64,3},{65,64},{66,65},{67,66},{5,4},{6,5},{7,6}... | collective-permute-start | bytes 27656 | tf_op jit(solution)/shard_map/ppermute | solution.py:22
  310.7 5.8 copy-start.7
  311.4 5.5 collective-permute-start.8
  315.1 3.7 collective-permute-start.9
  316.9 11.5 %copy-start.5 = (bf16[3,3,256,256]{3,2,1,0:T(8,128)(2,1)S(1)}, bf16[3,3,256,256]{3,2,1,0:T(8,128)(2,1)}, u32[]{:S(2)}) copy-start(bf16[3,3,256,256]{3,2,1,0:T(8,128)(2,1)} %get-tuple-element.25) | copy-start | bytes 3538948
  318.9 9.9 %collective-permute-start.10 = (bf16[18,1,256]{2,1,0:T(2,128)(2,1)S(1)}, bf16[18,1,256]{2,1,0:T(2,128)(2,1)S(1)}, u32[]{:S(2)}, u32[]{:S(2)}) collective-permute-start(bf16[18,1,256]{2,1,0:T(2,128)(2,1)S(1)} %get-tuple-element.98), channel_id=1, source_target_pairs={{0,1},{1,2},{2,3},{3,64},{64,65},{65,66},{66,67},{4,5},{5,6},{6,7}... | collective-permute-start | bytes 27656 | tf_op jit(solution)/shard_map/ppermute | solution.py:21
  326.5 5.7 collective-permute-start.11
  341.1 5.4 collective-permute-start.20
  345.2 4.0 collective-permute-start.21
  349.3 8.3 %collective-permute-start.22 = (bf16[18,1,256]{2,1,0:T(2,128)(2,1)S(1)}, bf16[18,1,256]{2,1,0:T(2,128)(2,1)S(1)}, u32[]{:S(2)}, u32[]{:S(2)}) collective-permute-start(bf16[18,1,256]{2,1,0:T(2,128)(2,1)S(1)} %get-tuple-element.86), channel_id=1, source_target_pairs={{1,0},{2,1},{3,2},{64,3},{65,64},{66,65},{67,66},{5,4},{6,5},{7,6}... | collective-permute-start | bytes 27656 | tf_op jit(solution)/shard_map/ppermute | solution.py:22
  350.6 7.6 %collective-permute-start.23 = (bf16[18,1,256]{2,1,0:T(2,128)(2,1)S(1)}, bf16[18,1,256]{2,1,0:T(2,128)(2,1)S(1)}, u32[]{:S(2)}, u32[]{:S(2)}) collective-permute-start(bf16[18,1,256]{2,1,0:T(2,128)(2,1)S(1)} %get-tuple-element.87), channel_id=1, source_target_pairs={{0,1},{1,2},{2,3},{3,64},{64,65},{65,66},{66,67},{4,5},{5,6},{6,7}... | collective-permute-start | bytes 27656 | tf_op jit(solution)/shard_map/ppermute | solution.py:21
  368.7 10.9 %collective-permute-start.24 = (bf16[1,128,256]{2,1,0:T(8,128)(2,1)S(1)}, bf16[1,128,256]{2,1,0:T(8,128)(2,1)S(1)}, u32[]{:S(2)}, u32[]{:S(2)}) collective-permute-start(bf16[1,128,256]{2,1,0:T(8,128)(2,1)S(1)} %get-tuple-element.115), channel_id=1, source_target_pairs={{0,4},{4,8},{8,12},{12,16},{16,20},{20,24},{24,28},{28,32},{32,36}... | collective-permute-start | bytes 196616 | tf_op jit(solution)/shard_map/ppermute | solution.py:21
  373.6 6.0 collective-permute-start.25
  374.9 11.5 %collective-permute-start.12 = (bf16[1,128,256]{2,1,0:T(8,128)(2,1)S(1)}, bf16[1,128,256]{2,1,0:T(8,128)(2,1)S(1)}, u32[]{:S(2)}, u32[]{:S(2)}) collective-permute-start(bf16[1,128,256]{2,1,0:T(8,128)(2,1)S(1)} %get-tuple-element.127), channel_id=1, source_target_pairs={{0,4},{4,8},{8,12},{12,16},{16,20},{20,24},{24,28},{28,32},{32,36}... | collective-permute-start | bytes 196616 | tf_op jit(solution)/shard_map/ppermute | solution.py:21
  378.3 8.1 %collective-permute-start.13 = (bf16[1,128,256]{2,1,0:T(8,128)(2,1)S(1)}, bf16[1,128,256]{2,1,0:T(8,128)(2,1)S(1)}, u32[]{:S(2)}, u32[]{:S(2)}) collective-permute-start(bf16[1,128,256]{2,1,0:T(8,128)(2,1)S(1)} %get-tuple-element.128), channel_id=1, source_target_pairs={{4,0},{8,4},{12,8},{16,12},{20,16},{24,20},{28,24},{32,28},{36,32}... | collective-permute-start | bytes 196616 | tf_op jit(solution)/shard_map/ppermute | solution.py:22
  380.2 13.6 %collective-permute-start.26 = (bf16[18,1,256]{2,1,0:T(2,128)(2,1)S(1)}, bf16[18,1,256]{2,1,0:T(2,128)(2,1)S(1)}, u32[]{:S(2)}, u32[]{:S(2)}) collective-permute-start(bf16[18,1,256]{2,1,0:T(2,128)(2,1)S(1)} %get-tuple-element.82), channel_id=1, source_target_pairs={{1,0},{2,1},{3,2},{64,3},{65,64},{66,65},{67,66},{5,4},{6,5},{7,6}... | collective-permute-start | bytes 27656 | tf_op jit(solution)/shard_map/ppermute | solution.py:22
  381.5 12.3 %collective-permute-start.27 = (bf16[18,1,256]{2,1,0:T(2,128)(2,1)S(1)}, bf16[18,1,256]{2,1,0:T(2,128)(2,1)S(1)}, u32[]{:S(2)}, u32[]{:S(2)}) collective-permute-start(bf16[18,1,256]{2,1,0:T(2,128)(2,1)S(1)} %get-tuple-element.83), channel_id=1, source_target_pairs={{0,1},{1,2},{2,3},{3,64},{64,65},{65,66},{66,67},{4,5},{5,6},{6,7}... | collective-permute-start | bytes 27656 | tf_op jit(solution)/shard_map/ppermute | solution.py:21
  387.0 21.8 %collective-permute-start.14 = (bf16[18,1,256]{2,1,0:T(2,128)(2,1)S(1)}, bf16[18,1,256]{2,1,0:T(2,128)(2,1)S(1)}, u32[]{:S(2)}, u32[]{:S(2)}) collective-permute-start(bf16[18,1,256]{2,1,0:T(2,128)(2,1)S(1)} %get-tuple-element.94), channel_id=1, source_target_pairs={{0,1},{1,2},{2,3},{3,64},{64,65},{65,66},{66,67},{4,5},{5,6},{6,7}... | collective-permute-start | bytes 27656 | tf_op jit(solution)/shard_map/ppermute | solution.py:21
  392.3 16.5 %collective-permute-start.15 = (bf16[18,1,256]{2,1,0:T(2,128)(2,1)S(1)}, bf16[18,1,256]{2,1,0:T(2,128)(2,1)S(1)}, u32[]{:S(2)}, u32[]{:S(2)}) collective-permute-start(bf16[18,1,256]{2,1,0:T(2,128)(2,1)S(1)} %get-tuple-element.95), channel_id=1, source_target_pairs={{1,0},{2,1},{3,2},{64,3},{65,64},{66,65},{67,66},{5,4},{6,5},{7,6}... | collective-permute-start | bytes 27656 | tf_op jit(solution)/shard_map/ppermute | solution.py:22
  402.6 11.8 %collective-permute-start.28 = (bf16[1,128,256]{2,1,0:T(8,128)(2,1)S(1)}, bf16[1,128,256]{2,1,0:T(8,128)(2,1)S(1)}, u32[]{:S(2)}, u32[]{:S(2)}) collective-permute-start(bf16[1,128,256]{2,1,0:T(8,128)(2,1)S(1)} %get-tuple-element.111), channel_id=1, source_target_pairs={{0,4},{4,8},{8,12},{12,16},{16,20},{20,24},{24,28},{28,32},{32,36}... | collective-permute-start | bytes 196616 | tf_op jit(solution)/shard_map/ppermute | solution.py:21
  407.5 6.9 %collective-permute-start.29 = (bf16[1,128,256]{2,1,0:T(8,128)(2,1)S(1)}, bf16[1,128,256]{2,1,0:T(8,128)(2,1)S(1)}, u32[]{:S(2)}, u32[]{:S(2)}) collective-permute-start(bf16[1,128,256]{2,1,0:T(8,128)(2,1)S(1)} %get-tuple-element.112), channel_id=1, source_target_pairs={{4,0},{8,4},{12,8},{16,12},{20,16},{24,20},{28,24},{32,28},{36,32}... | collective-permute-start | bytes 196616 | tf_op jit(solution)/shard_map/ppermute | solution.py:22
  414.4 10.6 %collective-permute-start.30 = (bf16[18,1,256]{2,1,0:T(2,128)(2,1)S(1)}, bf16[18,1,256]{2,1,0:T(2,128)(2,1)S(1)}, u32[]{:S(2)}, u32[]{:S(2)}) collective-permute-start(bf16[18,1,256]{2,1,0:T(2,128)(2,1)S(1)} %get-tuple-element.78), channel_id=1, source_target_pairs={{1,0},{2,1},{3,2},{64,3},{65,64},{66,65},{67,66},{5,4},{6,5},{7,6}... | collective-permute-start | bytes 27656 | tf_op jit(solution)/shard_map/ppermute | solution.py:22
  415.7 9.9 %collective-permute-start.31 = (bf16[18,1,256]{2,1,0:T(2,128)(2,1)S(1)}, bf16[18,1,256]{2,1,0:T(2,128)(2,1)S(1)}, u32[]{:S(2)}, u32[]{:S(2)}) collective-permute-start(bf16[18,1,256]{2,1,0:T(2,128)(2,1)S(1)} %get-tuple-element.79), channel_id=1, source_target_pairs={{0,1},{1,2},{2,3},{3,64},{64,65},{65,66},{66,67},{4,5},{5,6},{6,7}... | collective-permute-start | bytes 27656 | tf_op jit(solution)/shard_map/ppermute | solution.py:21
  433.1 6.0 copy-start.22
  433.1 6.0 copy-start.24
  433.1 6.0 copy-start.26
  433.1 6.0 copy-start.28
  433.1 6.6 %copy-start.30 = (s32[128]{0:T(128)S(1)}, s32[128]{0:T(128)}, u32[]{:S(2)}) copy-start(s32[128]{0:T(128)} %copy-done.29) | copy-start | bytes 1540
  433.1 6.6 %copy-start.32 = (s32[128]{0:T(128)S(1)}, s32[128]{0:T(128)}, u32[]{:S(2)}) copy-start(s32[128]{0:T(128)} %copy-done.31) | copy-start | bytes 1540
  433.2 6.6 %copy-start.34 = (f32[128]{0:T(128)S(1)}, f32[128]{0:T(128)}, u32[]{:S(2)}) copy-start(f32[128]{0:T(128)} %copy-done.33) | copy-start | bytes 1540
  433.2 6.6 %copy-start.36 = (f32[128]{0:T(128)S(1)}, f32[128]{0:T(128)}, u32[]{:S(2)}) copy-start(f32[128]{0:T(128)} %copy-done.35) | copy-start | bytes 1540
  607.7 3.2 copy-start.19
  (10 other events, 17.1 us)
Sparse Core Ops, SparseCore 0:
  21.6 143.3 all-reduce.7
  170.0 93.8 all-reduce.9
  442.6 162.7 all-reduce.5
where the time goes:
time: 641 us; the launch traced here: 629 us
  waiting for transfers between devices  393 us (61%)
  starting transfers between devices  91.3 us (14%)
  matrix products  51.9 us (8%)
  other arithmetic  41.5 us (6%)
  local copies, waits for them, and re-layouts  34.2 us (5%)
  between operations  17.4 us (3%)
    psum x2, waiting for transfers between devices, broadcast(): return lax.psum(jnp.where(mine, x, jnp.zeros_like(x)), axis)  210 us
    psum x1, waiting for transfers between devices, shards(): summed = lax.psum(placed, ('sec', 'row', 'col'))  162 us
    ppermute x16, starting transfers between devices, padded_2(): before = lax.ppermute(last, axis, up)  69.3 us
    dot_general x72, matrix products, conv_sum(): jnp.dot(window.reshape(row_count * col_count, -1), weight, preferred_elem...  39.9 us
    ppermute x16, starting transfers between devices, padded_2(): after = lax.ppermute(initial, axis, down)  21.8 us
    ppermute x16, waiting for transfers between devices, padded_2(): after = lax.ppermute(initial, axis, down)  19.9 us
  transfers between devices with their start and end apart: 35, of which 12 were waited for; matrix products, arithmetic and copies ran while one was open for 8% of the time, Pallas kernels for 0%

commit v1 on v0

v1 whole, which is shorter than its diff:
```python
import functools

import jax
import jax.numpy as jnp
from jax import lax
from jax.experimental import pallas as pl
from jax.experimental.pallas import tpu as pltpu
from jax.sharding import PartitionSpec as P

R = 16
CIN = 78
W = 256
BLOCKS = 4
TR = 16
TC = 128
LAT_DEV = 45
LON_DEV = 180
HR = 6
HC = 8
ER = TR + 2 * HR
L = 9
S = 16
EC = L * S
BF = jnp.bfloat16
F32 = jnp.float32
VM = pl.BlockSpec(memory_space=pltpu.VMEM)
SM = pl.BlockSpec(memory_space=pltpu.SMEM)
MB = 2**20
NT = (((1,), (1,)), ((), ()))
NN = (((1,), (0,)), ((), ()))
TN = (((0,), (0,)), ((), ()))


def dotf(a, b, dims=NN):
    return lax.dot_general(a, b, dims, preferred_element_type=F32)


def iota(shape, dim):
    return lax.broadcasted_iota(jnp.int32, shape, dim)


def ext_col(m):
    return (m & 15) * L + (m >> 4)


def one_hot(cond):
    return jnp.where(cond, 1.0, 0.0).astype(BF)


def col_weight(e, j):
    n = 2 * e + 1
    a = n >> 5
    t = (n & 31).astype(F32) * (1.0 / 32.0)
    return jnp.where(j == a, 1.0 - t, 0.0) + jnp.where(j == a + 1, t, 0.0)


def col_place():
    return lax.axis_index("sec") * 4 + lax.axis_index("col")


def pack_kernel(ro, co, coarse, static, cot, send, xown, pa, pb, prod):
    ri = lax.axis_index("row")
    ci = col_place()
    first_row = ro[0] - 1 - LAT_DEV * ri
    off = co[0] - 1 - LON_DEV * ci
    lj = iota((272, LON_DEV), 1)
    q = iota((272, LON_DEV), 0)
    tail = q - 80
    k = tail >> 6
    c = (tail & 63) >> 3
    s = (tail & 7) - 2 * k
    j_tail = jnp.where((s >= 0) & (s < 2), 8 * c + 8 + s, -100000)
    j = jnp.where(q < 80, jnp.where(q < 66, q, -100000), j_tail)
    sel = one_hot(lj == off + j)

    def row(i, _):
        li = first_row + i
        ok = ((li >= 0) & (li < LAT_DEV)).astype(F32)
        x = coarse[jnp.clip(li, 0, LAT_DEV - 1)]
        prod[i, :, :CIN] = dotf(sel, x, NT) * ok
        return 0

    lax.fori_loop(0, 18, row, 0)

    def dest(r, _):
        tails = prod[r, 80:144] + prod[r + 1, 144:208] + prod[r + 2, 208:272]
        for cc in range(8):
            d = (cc // 4) * 64 + r * 4 + cc % 4
            sl = slice(8 * cc, 8 * cc + 8)
            msg = jnp.concatenate([prod[r, sl], prod[r + 1, sl], prod[r + 2, sl], tails[sl]], axis=0)
            send[d] = msg.astype(BF)
        return 0

    lax.fori_loop(0, 16, dest, 0)
    xown[...] = jnp.zeros_like(xown)
    xown[:, :CIN, :] = cot[...]
    xown[:, 80:84, :] = static[...]
    odd = ri & 1
    pa[...] = xown[pl.ds(jnp.where(odd == 1, 0, TR - HR), HR)]
    pb[...] = xown[pl.ds(jnp.where(odd == 1, TR - HR, 0), HR)]


def pack(ro, co, coarse, static, cot):
    return pl.pallas_call(
        pack_kernel,
        out_shape=[
            jax.ShapeDtypeStruct((128, 32, 128), BF),
            jax.ShapeDtypeStruct((TR, 128, 128), BF),
            jax.ShapeDtypeStruct((HR, 128, 128), BF),
            jax.ShapeDtypeStruct((HR, 128, 128), BF),
        ],
        in_specs=[SM, SM, VM, VM, VM],
        out_specs=[VM] * 4,
        scratch_shapes=[pltpu.VMEM((18, 272, 128), F32)],
        compiler_params=pltpu.CompilerParams(vmem_limit_bytes=32 * MB),
        name="pack",
    )(ro, co, coarse, static, cot)


def edge_kernel(xown, ra, rb, ct, pc, pd, edge):
    ri = lax.axis_index("row")
    ci = col_place()
    m = iota((EC, 128), 0)
    perm = one_hot(ext_col(m) - HC == iota((EC, 128), 1))
    q = iota((16, 128), 0)
    sel = one_hot(iota((16, 128), 1) == jnp.where(q < 8, q, q + 112))
    both = jnp.concatenate([perm, sel], axis=0)

    def do(y, x):
        r = dotf(both, x, NT)
        ct[y] = r[:EC].astype(BF)
        edge[y] = r[EC:]

    def mid(y, _):
        do(y + HR, xown[y])
        return 0

    lax.fori_loop(0, TR, mid, 0)
    odd = (ri & 1) == 1

    def ends(y, _):
        a = ra[y]
        b = rb[y]
        do(y, jnp.where(odd, a, b))
        do(y + HR + TR, jnp.where(odd, b, a))
        return 0

    lax.fori_loop(0, HR, ends, 0)
    oddc = (ci & 1) == 1
    left = edge[:, :8, :].reshape(ER * 8, 128)
    right = edge[:, 8:, :].reshape(ER * 8, 128)
    pc[...] = jnp.where(oddc, left, right).astype(BF)
    pd[...] = jnp.where(oddc, right, left).astype(BF)


def edges(xown, ra, rb):
    return pl.pallas_call(
        edge_kernel,
        out_shape=[
            jax.ShapeDtypeStruct((ER, EC, 128), BF),
            jax.ShapeDtypeStruct((ER * 8, 128), BF),
            jax.ShapeDtypeStruct((ER * 8, 128), BF),
        ],
        in_specs=[VM] * 3,
        out_specs=[VM] * 3,
        scratch_shapes=[pltpu.VMEM((ER, 16, 128), F32)],
        compiler_params=pltpu.CompilerParams(vmem_limit_bytes=16 * MB),
        name="edges",
    )(xown, ra, rb)


def main_kernel(
    recv, ct, rc, rd, wbig, gains, kern, wht, wl, fine, msg,
    vup, hid, act, cv, hs_s, ds_s, back, gsum,
):
    ri = lax.axis_index("row")
    ci = col_place()
    oddc = (ci & 1) == 1

    win = jnp.sum(recv[...].astype(F32), axis=0)
    win = jnp.where(iota((32, 128), 1) < CIN, win, 0.0).astype(BF)
    m = iota((EC, 32), 0)
    q = iota((EC, 32), 1)
    for k in range(3):
        tail = q - 24 - 2 * k
        j = jnp.where((q >= 8 * k) & (q < 8 * k + 8), q - 8 * k, -10)
        j = jnp.where((tail >= 0) & (tail < 2), tail + 8, j)
        coef = col_weight(ext_col(m), j).astype(BF)
        vup[k] = dotf(coef, win)

    m4 = iota((4 * EC, 32), 0)
    q4 = iota((4 * EC, 32), 1)
    y4 = (
        (m4 >= EC).astype(jnp.int32) + (m4 >= 2 * EC).astype(jnp.int32) + (m4 >= 3 * EC).astype(jnp.int32)
    )
    e4 = ext_col(m4 - y4 * EC)
    same = y4 == (q4 >> 3)
    perm_l = one_hot(same & (e4 == (q4 & 7)))
    perm_r = one_hot(same & (e4 - (HC + TC) == (q4 & 7)))

    def lift(g, _):
        rows = pl.ds(pl.multiple_of(g * 32, 32), 32)
        c = rc[rows, :]
        d = rd[rows, :]
        halo = dotf(perm_l, jnp.where(oddc, c, d)) + dotf(perm_r, jnp.where(oddc, d, c))
        ups = []
        for k in range(4):
            n = 2 * (g * 4 + k) + 5
            a = n >> 5
            t = (n & 31).astype(F32) * (1.0 / 32.0)
            ups.append(((1.0 - t) * vup[a] + t * vup[a + 1]).astype(BF))
        up = jnp.concatenate(ups, axis=0)
        own = ct[pl.ds(g * 4, 4)].reshape(4 * EC, 128)
        both = (own.astype(F32) + halo).astype(BF)
        r = dotf(jnp.concatenate([up, both], axis=1), wbig[...])
        hid[pl.ds(g * 4, 4)] = r[:, :W].astype(BF).reshape(4, EC, W)
        back[pl.ds(g * 4, 4)] = r[:, W:].reshape(4, EC, W)
        return 0

    lax.fori_loop(0, ER // 4, lift, 0)

    CK = 48
    col_ok = []
    for ck in range(3):
        gc = ci * TC + ext_col(iota((CK, 1), 0) + ck * CK) - HC
        col_ok.append(jnp.where((gc >= 0) & (gc < 8 * TC), 1.0, 0.0))

    def put(y, ck, v):
        act[y, 1 + 3 * ck : 4 + 3 * ck] = v.astype(BF).reshape(3, S, W)
        if ck == 2:
            act[y, 0] = pltpu.roll(v[32:48], 1, 0).astype(BF)
        if ck == 0:
            act[y, L + 1] = pltpu.roll(v[:16], S - 1, 0).astype(BF)

    def activate(b, y):
        gr = ri * TR + y - HR
        ok = ((gr >= 0) & (gr < 16 * TR)).astype(F32)
        gain = gains[b : b + 1, :]
        for ck in range(3):
            h = hid[y, ck * CK : (ck + 1) * CK, :].astype(F32)
            s = lax.rsqrt(jnp.mean(h * h, axis=-1, keepdims=True) + 1e-06) * (col_ok[ck] * ok)
            hs = h * s
            n = hs * gain
            g = 0.5 * jnp.tanh(0.5 * n) + 0.5
            a = n * g
            put(y, ck, a)
            hs_s[b, y, ck * CK : (ck + 1) * CK, :] = hs.astype(BF)
            ds_s[b, y, ck * CK : (ck + 1) * CK, :] = ((g + a - a * g) * gain * s).astype(BF)

    def conv(b, y0, n, transpose):
        acc = None
        for p in range(3):
            for q in range(3):
                dy = 1 - p if transpose else p - 1
                dx = 2 - q if transpose else q
                x = act[pl.ds(y0 + dy, n), dx : dx + L].reshape(n * EC, W)
                r = dotf(x, kern[b, p, q], NT if transpose else NN)
                acc = r if acc is None else acc + r
        cv[:n] = acc.reshape(n, EC, W)

    def first(y, _):
        activate(0, y)
        return 0

    lax.fori_loop(0, ER, first, 0)

    for b in range(BLOCKS):
        lo, hi = (b + 1, ER - 1 - b) if b < 3 else (HR, HR + TR)
        n = (hi - lo) // 2
        for half in range(2):
            y0 = lo + half * n
            conv(b, y0, n, False)

            def resid(k, _, y0=y0):
                hid[y0 + k] = (hid[y0 + k].astype(F32) + cv[k]).astype(BF)
                return 0

            lax.fori_loop(0, n, resid, 0)
        if b < 3:

            def nxt(y, _, b=b):
                activate(b + 1, y)
                return 0

            lax.fori_loop(lo, hi, nxt, 0)

    perm = one_hot(ext_col(iota((EC, 128), 0)) - HC == iota((EC, 128), 1))

    def head(y, _):
        o = dotf(wht[...], hid[y + HR], NT).astype(BF)
        fine[y] = dotf(o, perm).astype(BF)[:CIN]
        return 0

    lax.fori_loop(0, TR, head, 0)

    def send4(y, _):
        for ck in range(3):
            put(y, ck, back[y, ck * CK : (ck + 1) * CK, :])
        return 0

    lax.fori_loop(2, ER - 2, send4, 0)
    for b in reversed(range(BLOCKS)):
        lo, hi = HR - b, HR + TR + b
        n = (hi - lo) // 2
        for half in range(2):
            y0 = lo + half * n
            conv(b, y0, n, True)

            def grad(k, _, y0=y0, b=b):
                y = y0 + k
                for ck in range(3):
                    sl = slice(ck * CK, (ck + 1) * CK)
                    u = cv[k, sl] * ds_s[b, y, sl].astype(F32)
                    hs = hs_s[b, y, sl].astype(F32)
                    mean = jnp.mean(u * hs, axis=-1, keepdims=True)
                    back[y, sl] = back[y, sl] + (u - hs * mean)
                return 0

            lax.fori_loop(0, n, grad, 0)
        if b > 0:
            lax.fori_loop(lo, hi, send4, 0)

    e = ext_col(iota((32, EC), 1))
    qq = iota((32, EC), 0)
    j = jnp.where(qq < 10, qq, jnp.where(qq < 20, qq - 10, -10))
    own = (e >= HC) & (e < HC + TC)
    cols_t = jnp.where(own, col_weight(e, j), 0.0).astype(BF)
    gsum[...] = jnp.zeros_like(gsum)

    def gather(y, _):
        t = dotf(cols_t, back[y + HR].astype(BF))
        n = 2 * (y + HR) + 5
        a = n >> 5
        w = (n & 31).astype(F32) * (1.0 / 32.0)
        gsum[a] = gsum[a] + (1.0 - w) * t
        gsum[a + 1] = gsum[a + 1] + w * t
        return 0

    lax.fori_loop(0, TR, gather, 0)
    g = jnp.concatenate([gsum[0], gsum[1], gsum[2]], axis=1)
    g_hi = g.astype(BF)
    g_lo = (g - g_hi.astype(F32)).astype(BF)
    o = dotf(g_hi, wl[...]) + dotf(g_lo, wl[...])
    o = jnp.where(iota((32, 128), 0) < 10, o[:, :128], o[:, 128:]).astype(BF)[:24]

    def spread(d, _):
        msg[d] = o
        return 0

    lax.fori_loop(0, 128, spread, 0)


def main(recv, ct, rc, rd, wbig, gains, kern, wht, wl):
    return pl.pallas_call(
        main_kernel,
        out_shape=[
            jax.ShapeDtypeStruct((TR, CIN, TC), BF),
            jax.ShapeDtypeStruct((128, 24, 128), BF),
        ],
        in_specs=[VM] * 9,
        out_specs=[VM] * 2,
        scratch_shapes=[
            pltpu.VMEM((3, EC, 128), F32),
            pltpu.VMEM((ER, EC, W), BF),
            pltpu.VMEM((ER, L + 2, S, W), BF),
            pltpu.VMEM((13, EC, W), F32),
            pltpu.VMEM((BLOCKS, ER, EC, W), BF),
            pltpu.VMEM((BLOCKS, ER, EC, W), BF),
            pltpu.VMEM((ER, EC, W), F32),
            pltpu.VMEM((3, 32, W), F32),
        ],
        compiler_params=pltpu.CompilerParams(vmem_limit_bytes=56 * MB),
        name="main",
    )(recv, ct, rc, rd, wbig, gains, kern, wht, wl)


def place_kernel(ro, co, recv, out, acc):
    first_row = ro[0] - 1 - LAT_DEV * lax.axis_index("row")
    off = co[0] - 1 - LON_DEV * col_place()
    q = iota((192, 512), 0)
    lane = iota((192, 512), 1)
    h = lane >> 8
    lj = lane & 255
    c = q // 24
    j = q - c * 24 - 10 * h
    sel = one_hot((j >= 0) & (j < 10) & (lj == off + 8 * c + j) & (lj < LON_DEV))
    acc[...] = jnp.zeros_like(acc)

    def row(r, _):
        a = recv[:, r].astype(F32).reshape(192, 128).astype(BF)
        o = dotf(a, sel, TN)
        for k in range(3):
            acc[r + k, :40] = acc[r + k, :40] + o[40 * k : 40 * k + 40, :256]
            acc[r + k, 40:] = acc[r + k, 40:] + o[40 * k : 40 * k + 40, 256:]
        return 0

    lax.fori_loop(0, 16, row, 0)
    out[...] = jnp.zeros_like(out)

    def store(i, _):
        li = first_row + i

        @pl.when((li >= 0) & (li < LAT_DEV))
        def _():
            out[jnp.clip(li, 0, LAT_DEV - 1)] = acc[i, :CIN, :LON_DEV]

        return 0

    lax.fori_loop(0, 18, store, 0)


def place(ro, co, recv):
    return pl.pallas_call(
        place_kernel,
        out_shape=jax.ShapeDtypeStruct((LAT_DEV, CIN, LON_DEV), F32),
        in_specs=[SM, SM, VM],
        out_specs=VM,
        scratch_shapes=[pltpu.VMEM((18, 80, 256), F32)],
        compiler_params=pltpu.CompilerParams(vmem_limit_bytes=32 * MB),
        name="place",
    )(ro, co, recv)


def shards(coarse, ro, co, static, w_lift, w_static, gains, kern, w_head, cot):
    send, xown, pa, pb = pack(ro, co, coarse, static, cot)
    recv = lax.all_to_all(send, ("sec", "row", "col"), 0, 0, tiled=True)
    near = [(i, i ^ 1) for i in range(16)]
    far = [(i, j) for i in range(16) for j in [i + 1 if i & 1 else i - 1] if 0 <= j < 16]
    ra = lax.ppermute(pa, "row", near)
    rb = lax.ppermute(pb, "row", far)
    ct, pc, pd = edges(xown, ra, rb)
    near = [(i, i ^ 1) for i in range(8)]
    far = [(i, j) for i in range(8) for j in [i + 1 if i & 1 else i - 1] if 0 <= j < 8]
    rc = lax.ppermute(pc, ("sec", "col"), near)
    rd = lax.ppermute(pd, ("sec", "col"), far)

    wht = w_head.T
    zero = jnp.zeros
    wbig = jnp.concatenate(
        [
            jnp.concatenate([w_lift, zero((50, W), BF), zero((80, W), BF), w_static, zero((44, W), BF)], 0),
            jnp.concatenate([zero((128, W), BF), wht, zero((50, W), BF)], 0),
        ],
        1,
    )
    wht80 = jnp.concatenate([wht, zero((2, W), BF)], 0)
    wl = jnp.concatenate([w_lift, zero((2, W), BF)], 0).reshape(2, 40, W).transpose(2, 0, 1)
    wl = jnp.concatenate(
        [jnp.pad(wl, ((0, 0), (0, 0), (40 * k, 88 - 40 * k))).reshape(W, 256) for k in range(3)], 0
    )
    fine, msg = main(recv, ct, rc, rd, wbig, gains, kern, wht80, wl)
    back = lax.all_to_all(msg, ("sec", "row", "col"), 0, 0, tiled=True)
    return fine, place(ro, co, back.reshape(2, 16, 4, 24, 128))


def solution(mesh):
    tile = P("row", None, ("sec", "col"))
    in_specs = (tile, P(), P(), tile, P(), P(), P(), P(), P(), tile)
    return jax.shard_map(shards, mesh=mesh, in_specs=in_specs, out_specs=(tile, tile), check_vma=False)
```

time: 641 us -> 191 us (0.30); the launches traced: 629 us -> 188 us
  waiting for transfers between devices: 393 us -> 23.1 us
  Pallas kernels: 0 us -> 118 us
  starting transfers between devices: 91.3 us -> 34.2 us
  matrix products: 51.9 us -> 0 us
  other arithmetic: 41.5 us -> 1.49 us
  local copies, waits for them, and re-layouts: 34.2 us -> 8.68 us
  between operations: 17.4 us -> 2.4 us
    psum x3 -> x0, waiting for transfers between devices: 372 us -> none  [the longest x2 210 us: broadcast(): return lax.psum(jnp.where(mine, x, jnp.zeros_like(x)), axis)]
    pallas_call x0 -> x4, Pallas kernels: none -> 118 us  [the longest x1 103 us: main(): pl.pallas_call(main_kernel, out_shape=[jax.ShapeDtypeStruct((TR, CIN, TC)...]
    ppermute x32 -> x4, starting transfers between devices: 91.1 us -> 3.13 us  [the longest x1 1.2 us: shards(): rc = lax.ppermute(pc, ('sec', 'col'), near)]
    dot_general x81 -> x0, matrix products: 51.9 us -> none  [the longest x72 39.9 us: conv_sum(): jnp.dot(window.reshape(row_count * col_count, -1), weight, preferred_elem...]
    all_to_all x0 -> x2, starting transfers between devices: none -> 31.1 us  [the longest x1 19.9 us: shards(): back = lax.all_to_all(msg, ('sec', 'row', 'col'), 0, 0, tiled=True)]
    all_to_all x0 -> x2, waiting for transfers between devices: none -> 20.7 us  [the longest x1 14.7 us: shards(): back = lax.all_to_all(msg, ('sec', 'row', 'col'), 0, 0, tiled=True)]
    ppermute x32 -> x4, waiting for transfers between devices: 21.2 us -> 2.35 us  [the longest x1 2.34 us: shards(): rc = lax.ppermute(pc, ('sec', 'col'), near)]
    slice x24 -> x0, local copies, waits for them, and re-layouts: 9.63 us -> none  [the longest x7 5.55 us: conv_sum(): padded[2 - offset_dy:2 - offset_dy + row_count, 2 - offset_dx:2 - offset_...]
  transfers between devices with their start and end apart: 35 -> 6, of which waited for: 12 -> 3; matrix products, arithmetic and copies ran while one was open for 8% -> 3% of each run, Pallas kernels for 0% -> 2%
where the time goes in v1:
time: 191 us; the launch traced here: 188 us
  Pallas kernels  118 us (62%)
  starting transfers between devices  34.2 us (18%)
  waiting for transfers between devices  23.1 us (12%)
  local copies, waits for them, and re-layouts  8.68 us (5%)
  between operations  2.4 us (1%)
    pallas_call x1, Pallas kernels, main(): pl.pallas_call(main_kernel, out_shape=[jax.ShapeDtypeStruct((TR, CIN, TC)...  103 us
    all_to_all x1, starting transfers between devices, shards(): back = lax.all_to_all(msg, ('sec', 'row', 'col'), 0, 0, tiled=True)  19.9 us
    all_to_all x1, waiting for transfers between devices, shards(): back = lax.all_to_all(msg, ('sec', 'row', 'col'), 0, 0, tiled=True)  14.7 us
    all_to_all x1, starting transfers between devices, shards(): recv = lax.all_to_all(send, ('sec', 'row', 'col'), 0, 0, tiled=True)  11.1 us
    unnamed x21, local copies, waits for them, and re-layouts  7.03 us
    all_to_all x1, waiting for transfers between devices, shards(): recv = lax.all_to_all(send, ('sec', 'row', 'col'), 0, 0, tiled=True)  6.05 us
    pallas_call x1, Pallas kernels, place(): pl.pallas_call(place_kernel, out_shape=jax.ShapeDtypeStruct((LAT_DEV, CIN...  6.02 us
    pallas_call x1, Pallas kernels, pack(): pl.pallas_call(pack_kernel, out_shape=[jax.ShapeDtypeStruct((128, 32, 128...  4.71 us
  transfers between devices with their start and end apart: 6, of which 3 were waited for; matrix products, arithmetic and copies ran while one was open for 3% of the time, Pallas kernels for 2%

profile of v1, /device:TPU:0, one launch (start us, length us, event | category | flops | bytes accessed | tf_op | source)
XLA Modules:
  0.0 187.5 jit_solution(13048231494925243893)
XLA Ops:
  0.6 0.0 copy-start.5
  0.6 0.0 copy-start.8
  2.0 1.1 copy.12.cot
  3.0 0.0 copy-start
  3.0 1.5 copy-done
  4.5 0.0 copy-start.2
  4.5 0.7 copy-done.2
  5.2 0.0 copy-start.4
  5.2 4.7 %pack.1 = (bf16[128,32,128]{2,1,0:T(8,128)(2,1)}, bf16[16,128,128]{2,1,0:T(8,128)(2,1)S(1)}, bf16[6,128,128]{2,1,0:T(8,128)(2,1)S(1)}, bf16[6,128,128]{2,1,0:T(8,128)(2,1)S(1)}) custom-call(s32[1]{0:T(128)S(6)} %copy.22.ro, s32[1]{0:T(128)S(6)} %copy.23.co, bf16[45,78,180]{2,1,0:T(8,128)(2,1)S(1)} %copy-done, bf16[16,4,128]{2,1,0:T(4,128)(2,1)S(1)} %copy-done.2, ...), custom_call_target="tpu_custom_call" | custom-call | tf_op jit(solution)/shard_map/pack/pallas_call | solution.py:104
  10.0 11.1 %all-to-all-start = ((bf16[128,32,128]{2,1,0:T(8,128)(2,1)}), bf16[128,32,128]{2,1,0:T(8,128)(2,1)S(1)}, u32[]{:S(2)}, u32[]{:S(2)}) async-start(bf16[128,32,128]{2,1,0:T(8,128)(2,1)} %get-tuple-element.11), calls=%async_computation | async-start | bytes 2097152 | tf_op jit(solution)/shard_map/all_to_all | solution.py:426
  21.1 0.1 collective-permute-start
  21.2 0.7 collective-permute-start.1
  21.9 0.0 copy-done.5
  21.9 0.1 copy.13
  22.0 0.5 fusion
  22.6 0.0 copy-done.8
  22.6 0.4 concatenate.18
  23.0 0.8 pad_maximum_fusion.wl
  23.8 0.0 collective-permute-done.ra
  23.8 0.0 collective-permute-done.1.rb
  23.8 3.7 %edges.1 = (bf16[28,144,128]{2,1,0:T(8,128)(2,1)S(1)}, bf16[224,128]{1,0:T(8,128)(2,1)S(1)}, bf16[224,128]{1,0:T(8,128)(2,1)S(1)}) custom-call(bf16[16,128,128]{2,1,0:T(8,128)(2,1)S(1)} %get-tuple-element.12.xown, bf16[6,128,128]{2,1,0:T(8,128)(2,1)S(1)} %collective-permute-done.ra, bf16[6,128,128]{2,1,0:T(8,128)(2,1)S(1)} %collective-permute-done.1.rb), custom_call_target="tpu_custom_call" | custom-call | tf_op jit(solution)/shard_map/edges/pallas_call | solution.py:157
  27.5 0.0 copy-start.1
  27.5 1.0 copy-done.1
  28.5 1.2 collective-permute-start.2
  29.6 1.2 collective-permute-start.3
  30.8 0.0 copy-done.4
  30.9 0.7 maximum_maximum_fusion.wbig
  31.6 0.6 concatenate.21.wht
  32.2 2.3 %collective-permute-done.2.rc = bf16[224,128]{1,0:T(8,128)(2,1)S(1)} collective-permute-done((bf16[224,128]{1,0:T(8,128)(2,1)S(1)}, bf16[224,128]{1,0:T(8,128)(2,1)S(1)}, u32[]{:S(2)}, u32[]{:S(2)}) %collective-permute-start.2) | collective-permute-done | bytes 57376 | tf_op jit(solution)/shard_map/ppermute | solution.py:434
  34.5 0.0 copy-start.6
  34.5 0.0 collective-permute-done.3.rd
  34.6 0.0 copy-start.7
  34.6 6.1 %all-to-all-done.recv = bf16[128,32,128]{2,1,0:T(8,128)(2,1)S(1)} async-done(((bf16[128,32,128]{2,1,0:T(8,128)(2,1)}), bf16[128,32,128]{2,1,0:T(8,128)(2,1)S(1)}, u32[]{:S(2)}, u32[]{:S(2)}) %all-to-all-start) | async-done | bytes 1048608 | tf_op jit(solution)/shard_map/all_to_all | solution.py:426
  40.6 0.0 copy-start.3
  40.6 0.0 copy-done.6
  40.6 0.0 copy-done.7
  40.6 1.0 copy-done.3
  41.6 103.3 %main.1 = (bf16[16,78,128]{2,1,0:T(8,128)(2,1)}, bf16[128,24,128]{2,1,0:T(8,128)(2,1)}) custom-call(bf16[128,32,128]{2,1,0:T(8,128)(2,1)} %copy-done.3, bf16[28,144,128]{2,1,0:T(8,128)(2,1)} %copy-done.1, bf16[224,128]{1,0:T(8,128)(2,1)} %copy-done.6, bf16[224,128]{1,0:T(8,128)(2,1)} %copy-done.7, bf16[256,512]{1,0:T(8,128)(2,1)} %maximum_maximum_fusion.wbig, ...), custom_call_target="tpu_custom_call" | custom-call | tf_op jit(solution)/shard_map/main/pallas_call | solution.py:354
  144.9 19.9 %all-to-all-start.1 = ((bf16[128,24,128]{2,1,0:T(8,128)(2,1)}), bf16[128,24,128]{2,1,0:T(8,128)(2,1)S(1)}, u32[]{:S(2)}, u32[]{:S(2)}) async-start(bf16[128,24,128]{2,1,0:T(8,128)(2,1)} %get-tuple-element.19), calls=%async_computation.1 | async-start | bytes 1572864 | tf_op jit(solution)/shard_map/all_to_all | solution.py:452
  164.8 1.8 copy.14
  166.6 14.7 %all-to-all-done.1 = bf16[128,24,128]{2,1,0:T(8,128)(2,1)S(1)} async-done(((bf16[128,24,128]{2,1,0:T(8,128)(2,1)}), bf16[128,24,128]{2,1,0:T(8,128)(2,1)S(1)}, u32[]{:S(2)}, u32[]{:S(2)}) %all-to-all-start.1) | async-done | bytes 786464 | tf_op jit(solution)/shard_map/all_to_all | solution.py:452
  181.2 6.0 %place.1 = f32[45,78,180]{2,1,0:T(8,128)} custom-call(s32[1]{0:T(128)S(6)} %copy.22.ro, s32[1]{0:T(128)S(6)} %copy.23.co, bf16[2,16,4,24,128]{4,3,2,1,0:T(8,128)(2,1)S(1)} %bitcast.14), custom_call_target="tpu_custom_call" | custom-call | tf_op jit(solution)/shard_map/place/pallas_call | solution.py:413
  (7 shorter events, 0.1 us)
Async XLA Ops:
  0.6 21.3 %copy-start.5 = (bf16[78,256]{1,0:T(8,128)(2,1)S(1)}, bf16[78,256]{1,0:T(8,128)(2,1)}, u32[]{:S(2)}) copy-start(bf16[78,256]{1,0:T(8,128)(2,1)} %param.14) | copy-start | bytes 119812
  0.6 22.0 %copy-start.8 = (bf16[4,256]{1,0:T(4,128)(2,1)S(1)}, bf16[4,256]{1,0:T(4,128)(2,1)}, u32[]{:S(2)}) copy-start(bf16[4,256]{1,0:T(4,128)(2,1)} %param.15) | copy-start | bytes 6148
  3.0 1.5 copy-start
  4.5 0.7 copy-start.2
  5.2 25.6 %copy-start.4 = (bf16[256,78]{0,1:T(8,128)(2,1)S(1)}, bf16[256,78]{0,1:T(8,128)(2,1)}, u32[]{:S(2)}) copy-start(bf16[256,78]{0,1:T(8,128)(2,1)} %param.18) | copy-start | bytes 119812
  10.0 30.6 %all-to-all-start = ((bf16[128,32,128]{2,1,0:T(8,128)(2,1)}), bf16[128,32,128]{2,1,0:T(8,128)(2,1)S(1)}, u32[]{:S(2)}, u32[]{:S(2)}) async-start(bf16[128,32,128]{2,1,0:T(8,128)(2,1)} %get-tuple-element.11), calls=%async_computation | async-start | bytes 2097152 | tf_op jit(solution)/shard_map/all_to_all | solution.py:426
  21.1 2.7 %collective-permute-start = (bf16[6,128,128]{2,1,0:T(8,128)(2,1)S(1)}, bf16[6,128,128]{2,1,0:T(8,128)(2,1)S(1)}, u32[]{:S(2)}, u32[]{:S(2)}) collective-permute-start(bf16[6,128,128]{2,1,0:T(8,128)(2,1)S(1)} %get-tuple-element.13), channel_id=1, source_target_pairs={{0,4},{4,0},{8,12},{12,8},{16,20},{20,16},{24,28},{28,24},{32,36},... | collective-permute-start | bytes 589832 | tf_op jit(solution)/shard_map/ppermute | solution.py:429
  21.2 2.6 %collective-permute-start.1 = (bf16[6,128,128]{2,1,0:T(8,128)(2,1)S(1)}, bf16[6,128,128]{2,1,0:T(8,128)(2,1)S(1)}, u32[]{:S(2)}, u32[]{:S(2)}) collective-permute-start(bf16[6,128,128]{2,1,0:T(8,128)(2,1)S(1)} %get-tuple-element.14), channel_id=1, source_target_pairs={{4,8},{8,4},{12,16},{16,12},{20,24},{24,20},{28,32},{32,28},{36,40... | collective-permute-start | bytes 589832 | tf_op jit(solution)/shard_map/ppermute | solution.py:430
  27.5 1.0 copy-start.1
  28.5 6.1 %collective-permute-start.2 = (bf16[224,128]{1,0:T(8,128)(2,1)S(1)}, bf16[224,128]{1,0:T(8,128)(2,1)S(1)}, u32[]{:S(2)}, u32[]{:S(2)}) collective-permute-start(bf16[224,128]{1,0:T(8,128)(2,1)S(1)} %get-tuple-element.16), channel_id=1, source_target_pairs={{0,1},{1,0},{2,3},{3,2},{64,65},{65,64},{66,67},{67,66},{4,5},{5,4... | collective-permute-start | bytes 172040 | tf_op jit(solution)/shard_map/ppermute | solution.py:434
  29.6 4.9 %collective-permute-start.3 = (bf16[224,128]{1,0:T(8,128)(2,1)S(1)}, bf16[224,128]{1,0:T(8,128)(2,1)S(1)}, u32[]{:S(2)}, u32[]{:S(2)}) collective-permute-start(bf16[224,128]{1,0:T(8,128)(2,1)S(1)} %get-tuple-element.17), channel_id=1, source_target_pairs={{1,2},{2,1},{3,64},{64,3},{65,66},{66,65},{5,6},{6,5},{7,68},{68,7... | collective-permute-start | bytes 172040 | tf_op jit(solution)/shard_map/ppermute | solution.py:435
  34.5 6.1 %copy-start.6 = (bf16[224,128]{1,0:T(8,128)(2,1)}, bf16[224,128]{1,0:T(8,128)(2,1)S(1)}, u32[]{:S(2)}) copy-start(bf16[224,128]{1,0:T(8,128)(2,1)S(1)} %collective-permute-done.2.rc) | copy-start | bytes 172036
  34.6 6.1 %copy-start.7 = (bf16[224,128]{1,0:T(8,128)(2,1)}, bf16[224,128]{1,0:T(8,128)(2,1)S(1)}, u32[]{:S(2)}) copy-start(bf16[224,128]{1,0:T(8,128)(2,1)S(1)} %collective-permute-done.3.rd) | copy-start | bytes 172036
  40.6 1.0 copy-start.3
  144.9 36.4 %all-to-all-start.1 = ((bf16[128,24,128]{2,1,0:T(8,128)(2,1)}), bf16[128,24,128]{2,1,0:T(8,128)(2,1)S(1)}, u32[]{:S(2)}, u32[]{:S(2)}) async-start(bf16[128,24,128]{2,1,0:T(8,128)(2,1)} %get-tuple-element.19), calls=%async_computation.1 | async-start | bytes 1572864 | tf_op jit(solution)/shard_map/all_to_all | solution.py:452

commit v2 on v1

--- a/solution.py
+++ b/solution.py
@@ -213,11 +213,12 @@
         own = ct[pl.ds(g * 4, 4)].reshape(4 * EC, 128)
         both = (own.astype(F32) + halo).astype(BF)
         r = dotf(jnp.concatenate([up, both], axis=1), wbig[...])
-        hid[pl.ds(g * 4, 4)] = r[:, :W].astype(BF).reshape(4, EC, W)
+        cv[pl.ds(g * 4, 4)] = r[:, :W].reshape(4, EC, W)
         back[pl.ds(g * 4, 4)] = r[:, W:].reshape(4, EC, W)
         return 0
 
     lax.fori_loop(0, ER // 4, lift, 0)
+    hid[...] = jnp.zeros_like(hid)
 
     CK = 48
     col_ok = []
@@ -232,57 +233,77 @@
         if ck == 0:
             act[y, L + 1] = pltpu.roll(v[:16], S - 1, 0).astype(BF)
 
+    def rows_of(lo, hi, f):
+        def two(i, _):
+            f(lo + 2 * i)
+            f(lo + 2 * i + 1)
+            return 0
+
+        lax.fori_loop(0, (hi - lo) >> 1, two, 0)
+
+    def resid(y, ck):
+        sl = slice(ck * CK, (ck + 1) * CK)
+        h = (hid[y, sl].astype(F32) + cv[y, sl]).astype(BF)
+        hid[y, sl] = h
+        return h.astype(F32)
+
     def activate(b, y):
         gr = ri * TR + y - HR
-        ok = ((gr >= 0) & (gr < 16 * TR)).astype(F32)
-        gain = gains[b : b + 1, :]
+        ok = jnp.where((gr >= 0) & (gr < 16 * TR), 1.0, 0.0)
+        gain = gains[pl.ds(b, 1), :]
         for ck in range(3):
-            h = hid[y, ck * CK : (ck + 1) * CK, :].astype(F32)
+            sl = slice(ck * CK, (ck + 1) * CK)
+            h = resid(y, ck)
             s = lax.rsqrt(jnp.mean(h * h, axis=-1, keepdims=True) + 1e-06) * (col_ok[ck] * ok)
             hs = h * s
             n = hs * gain
             g = 0.5 * jnp.tanh(0.5 * n) + 0.5
             a = n * g
             put(y, ck, a)
-            hs_s[b, y, ck * CK : (ck + 1) * CK, :] = hs.astype(BF)
-            ds_s[b, y, ck * CK : (ck + 1) * CK, :] = ((g + a - a * g) * gain * s).astype(BF)
-
-    def conv(b, y0, n, transpose):
-        acc = None
-        for p in range(3):
-            for q in range(3):
-                dy = 1 - p if transpose else p - 1
-                dx = 2 - q if transpose else q
-                x = act[pl.ds(y0 + dy, n), dx : dx + L].reshape(n * EC, W)
-                r = dotf(x, kern[b, p, q], NT if transpose else NN)
-                acc = r if acc is None else acc + r
-        cv[:n] = acc.reshape(n, EC, W)
-
-    def first(y, _):
-        activate(0, y)
-        return 0
-
-    lax.fori_loop(0, ER, first, 0)
-
-    for b in range(BLOCKS):
-        lo, hi = (b + 1, ER - 1 - b) if b < 3 else (HR, HR + TR)
-        n = (hi - lo) // 2
-        for half in range(2):
-            y0 = lo + half * n
-            conv(b, y0, n, False)
-
-            def resid(k, _, y0=y0):
-                hid[y0 + k] = (hid[y0 + k].astype(F32) + cv[k]).astype(BF)
-                return 0
-
-            lax.fori_loop(0, n, resid, 0)
-        if b < 3:
-
-            def nxt(y, _, b=b):
-                activate(b + 1, y)
-                return 0
-
-            lax.fori_loop(lo, hi, nxt, 0)
+            hs_s[b, y, sl] = hs.astype(BF)
+            ds_s[b, y, sl] = ((g + a - a * g) * gain * s).astype(BF)
+
+    def conv(b, lo, hi, transpose):
+        dims = NT if transpose else NN
+
+        def unit(i, _):
+            y0 = jnp.minimum(lo + 8 * i, hi - 8)
+
+            def rows(k):
+                return jnp.concatenate([act[pl.ds(y0 - 1 + k + 2 * u, 1)] for u in range(4)], axis=0)
+
+            d0, d1, d2, d3 = rows(0), rows(1), rows(2), rows(3)
+            ms = []
+            for k, t in enumerate((d0 - d2, d1 + d2, d2 - d1, d1 - d3)):
+                acc = None
+                for q in range(3):
+                    dx = 2 - q if transpose else q
+                    kk = (3, 1, 2, 0)[k] if transpose else k
+                    r = dotf(t[:, dx : dx + L].reshape(4 * EC, W), kern[b, kk, q], dims)
+                    acc = r if acc is None else acc + r
+                ms.append(acc)
+            e = (ms[0] + ms[1] + ms[2]).reshape(4, EC, W)
+            o = (ms[1] - ms[2] - ms[3]).reshape(4, EC, W)
+            for u in range(4):
+                cv[y0 + 2 * u] = e[u]
+                cv[y0 + 2 * u + 1] = o[u]
+            return 0
+
+        lax.fori_loop(0, (hi - lo + 7) >> 3, unit, 0)
+
+    def forward(b, _):
+        deep = b == 3
+        rows_of(jnp.where(deep, 3, b), jnp.where(deep, ER - 3, ER - b), functools.partial(activate, b))
+        conv(b, jnp.where(deep, HR, b + 1), jnp.where(deep, HR + TR, ER - 1 - b), False)
+        return 0
+
+    lax.fori_loop(0, BLOCKS, forward, 0)
+
+    def last(y):
+        for ck in range(3):
+            resid(y, ck)
+
+    rows_of(HR, HR + TR, last)
 
     perm = one_hot(ext_col(iota((EC, 128), 0)) - HC == iota((EC, 128), 1))
 
@@ -293,32 +314,29 @@
 
     lax.fori_loop(0, TR, head, 0)
 
-    def send4(y, _):
+    def send4(y):
         for ck in range(3):
             put(y, ck, back[y, ck * CK : (ck + 1) * CK, :])
-        return 0
-
-    lax.fori_loop(2, ER - 2, send4, 0)
-    for b in reversed(range(BLOCKS)):
-        lo, hi = HR - b, HR + TR + b
-        n = (hi - lo) // 2
-        for half in range(2):
-            y0 = lo + half * n
-            conv(b, y0, n, True)
-
-            def grad(k, _, y0=y0, b=b):
-                y = y0 + k
-                for ck in range(3):
-                    sl = slice(ck * CK, (ck + 1) * CK)
-                    u = cv[k, sl] * ds_s[b, y, sl].astype(F32)
-                    hs = hs_s[b, y, sl].astype(F32)
-                    mean = jnp.mean(u * hs, axis=-1, keepdims=True)
-                    back[y, sl] = back[y, sl] + (u - hs * mean)
-                return 0
-
-            lax.fori_loop(0, n, grad, 0)
-        if b > 0:
-            lax.fori_loop(lo, hi, send4, 0)
+
+    rows_of(2, ER - 2, send4)
+
+    def grad(b, y):
+        for ck in range(3):
+            sl = slice(ck * CK, (ck + 1) * CK)
+            u = cv[y, sl] * ds_s[b, y, sl].astype(F32)
+            hs = hs_s[b, y, sl].astype(F32)
+            mean = jnp.mean(u * hs, axis=-1, keepdims=True)
+            new = back[y, sl] + (u - hs * mean)
+            back[y, sl] = new
+            put(y, ck, new)
+
+    def backward(i, _):
+        b = 3 - i
+        conv(b, HR - b, HR + TR + b, True)
+        rows_of(HR - b, HR + TR + b, functools.partial(grad, b))
+        return 0
+
+    lax.fori_loop(0, BLOCKS, backward, 0)
 
     e = ext_col(iota((32, EC), 1))
     qq = iota((32, EC), 0)
@@ -363,7 +381,7 @@
             pltpu.VMEM((3, EC, 128), F32),
             pltpu.VMEM((ER, EC, W), BF),
             pltpu.VMEM((ER, L + 2, S, W), BF),
-            pltpu.VMEM((13, EC, W), F32),
+            pltpu.VMEM((ER, EC, W), F32),
             pltpu.VMEM((BLOCKS, ER, EC, W), BF),
             pltpu.VMEM((BLOCKS, ER, EC, W), BF),
             pltpu.VMEM((ER, EC, W), F32),
@@ -448,7 +466,9 @@
     wl = jnp.concatenate(
         [jnp.pad(wl, ((0, 0), (0, 0), (40 * k, 88 - 40 * k))).reshape(W, 256) for k in range(3)], 0
     )
-    fine, msg = main(recv, ct, rc, rd, wbig, gains, kern, wht80, wl)
+    k0, k1, k2 = (kern[:, p].astype(F32) for p in range(3))
+    wino = jnp.stack([k0, 0.5 * (k0 + k1 + k2), 0.5 * (k0 - k1 + k2), k2], axis=1).astype(BF)
+    fine, msg = main(recv, ct, rc, rd, wbig, gains, wino, wht80, wl)
     back = lax.all_to_all(msg, ("sec", "row", "col"), 0, 0, tiled=True)
     return fine, place(ro, co, back.reshape(2, 16, 4, 24, 128))
 

time: 191 us -> 146 us (0.76); the launches traced: 188 us -> 146 us
  Pallas kernels: 118 us -> 75.1 us
  other arithmetic: 1.49 us -> 10.1 us
  waiting for transfers between devices: 23.1 us -> 15.7 us
  starting transfers between devices: 34.2 us -> 30.5 us
  local copies, waits for them, and re-layouts: 8.68 us -> 12 us
    pallas_call x1, Pallas kernels: 103 us -> 60.7 us  [main(): pl.pallas_call(main_kernel, out_shape=[jax.ShapeDtypeStruct((TR, CIN, TC)...]
    another operation x0 -> x2, other arithmetic: none -> 8.56 us  [the longest x1 5.81 us: shards(): jnp.stack([k0, 0.5 * (k0 + k1 + k2), 0.5 * (k0 - k1 + k2), k2], axis=1)]
    all_to_all x1, waiting for transfers between devices: 6.05 us -> 0.01 us  [shards(): recv = lax.all_to_all(send, ('sec', 'row', 'col'), 0, 0, tiled=True)]
    all_to_all x1, starting transfers between devices: 19.9 us -> 16.2 us  [shards(): back = lax.all_to_all(msg, ('sec', 'row', 'col'), 0, 0, tiled=True)]
    slice x0 -> x1, local copies, waits for them, and re-layouts: none -> 3.69 us  [shards(): k0, k1, k2 = (kern[:, p].astype(F32) for p in range(3))]
  transfers between devices with their start and end apart: 6 -> 6, of which waited for: 3 -> 2; matrix products, arithmetic and copies ran while one was open for 3% -> 12% of each run, Pallas kernels for 2% -> 3%
where the time goes in v2:
time: 146 us
  Pallas kernels  75.1 us (51%)
  starting transfers between devices  30.5 us (21%)
  waiting for transfers between devices  15.7 us (11%)
  local copies, waits for them, and re-layouts  12 us (8%)
  other arithmetic  10.1 us (7%)
  between operations  2.11 us (1%)
    pallas_call x1, Pallas kernels, main(): pl.pallas_call(main_kernel, out_shape=[jax.ShapeDtypeStruct((TR, CIN, TC)...  60.7 us
    all_to_all x1, starting transfers between devices, shards(): back = lax.all_to_all(msg, ('sec', 'row', 'col'), 0, 0, tiled=True)  16.2 us
    all_to_all x1, waiting for transfers between devices, shards(): back = lax.all_to_all(msg, ('sec', 'row', 'col'), 0, 0, tiled=True)  14.7 us
    all_to_all x1, starting transfers between devices, shards(): recv = lax.all_to_all(send, ('sec', 'row', 'col'), 0, 0, tiled=True)  11.7 us
    unnamed x21, local copies, waits for them, and re-layouts  6.67 us
    pallas_call x1, Pallas kernels, place(): pl.pallas_call(place_kernel, out_shape=jax.ShapeDtypeStruct((LAT_DEV, CIN...  6.02 us
    another operation x1, other arithmetic, shards(): jnp.stack([k0, 0.5 * (k0 + k1 + k2), 0.5 * (k0 - k1 + k2), k2], axis=1)  5.81 us
    pallas_call x1, Pallas kernels, pack(): pl.pallas_call(pack_kernel, out_shape=[jax.ShapeDtypeStruct((128, 32, 128...  4.72 us
  transfers between devices with their start and end apart: 6, of which 2 were waited for; matrix products, arithmetic and copies ran while one was open for 12% of the time, Pallas kernels for 3%

profile of v2, /device:TPU:0, one launch (start us, length us, event | category | flops | bytes accessed | tf_op | source)
XLA Modules:
  0.0 145.5 jit_solution(5794935745140364516)
XLA Ops:
  1.9 1.1 copy.12.cot
  3.0 0.0 copy-start
  3.0 1.5 %copy-done = bf16[45,78,180]{2,1,0:T(8,128)(2,1)S(1)} copy-done((bf16[45,78,180]{2,1,0:T(8,128)(2,1)S(1)}, bf16[45,78,180]{2,1,0:T(8,128)(2,1)}, u32[]{:S(2)}) %copy-start) | copy-done | bytes 1263624
  4.5 0.0 copy-start.2
  4.5 0.7 copy-done.2
  5.2 4.7 %pack.1 = (bf16[128,32,128]{2,1,0:T(8,128)(2,1)}, bf16[16,128,128]{2,1,0:T(8,128)(2,1)S(1)}, bf16[6,128,128]{2,1,0:T(8,128)(2,1)S(1)}, bf16[6,128,128]{2,1,0:T(8,128)(2,1)S(1)}) custom-call(s32[1]{0:T(128)S(6)} %copy.22.ro, s32[1]{0:T(128)S(6)} %copy.23.co, bf16[45,78,180]{2,1,0:T(8,128)(2,1)S(1)} %copy-done, bf16[16,4,128]{2,1,0:T(4,128)(2,1)S(1)} %copy-done.2, ...), custom_call_target="tpu_custom_call" | custom-call | tf_op jit(solution)/shard_map/pack/pallas_call | solution.py:104
  9.9 11.7 %all-to-all-start = ((bf16[128,32,128]{2,1,0:T(8,128)(2,1)}), bf16[128,32,128]{2,1,0:T(8,128)(2,1)}, u32[]{:S(2)}, u32[]{:S(2)}) async-start(bf16[128,32,128]{2,1,0:T(8,128)(2,1)} %get-tuple-element.11), calls=%async_computation | async-start | bytes 2097152 | tf_op jit(solution)/shard_map/all_to_all | solution.py:444
  21.6 0.1 collective-permute-start
  21.7 0.0 copy-start.3
  21.7 0.8 collective-permute-start.1
  22.5 3.7 %fusion.4 = (bf16[4,1,3,256,256]{4,3,2,1,0:T(8,128)(2,1)S(1)}, bf16[4,1,3,256,256]{4,3,2,1,0:T(8,128)(2,1)}) fusion(bf16[4,3,3,256,256]{4,3,2,1,0:T(8,128)(2,1)} %param.17), kind=kLoop, calls=%fused_computation.14 | loop fusion | bytes 6291456 | tf_op jit(solution)/shard_map/slice | solution.py:469
  26.2 0.0 copy-done.3
  26.2 0.0 copy-start.5
  26.2 2.8 %fusion.1 = (bf16[4,1,3,256,256]{4,3,2,1,0:T(8,128)(2,1)}, bf16[4,1,3,256,256]{4,3,2,1,0:T(8,128)(2,1)}) fusion(bf16[4,3,3,256,256]{4,3,2,1,0:T(8,128)(2,1)S(1)} %copy-done.3), kind=kLoop, calls=%fused_computation.6 | loop fusion | flops 8650752 | bytes 7864320 | tf_op jit(solution)/shard_map/convert.1
  29.0 0.0 copy-done.5
  29.0 0.1 copy.13
  29.1 0.5 fusion.5
  29.6 0.0 copy-start.8
  29.6 0.0 copy-start.4
  29.6 5.8 %pad_maximum_fusion.kern = bf16[4,4,3,256,256]{4,3,2,1,0:T(8,128)(2,1)} fusion(bf16[4,1,3,256,256]{4,3,2,1,0:T(8,128)(2,1)} %get-tuple-element.23, bf16[4,1,3,256,256]{4,3,2,1,0:T(8,128)(2,1)} %get-tuple-element.25, bf16[4,1,3,256,256]{4,3,2,1,0:T(8,128)(2,1)} %get-tuple-element.24, bf16[4,1,3,256,256]{4,3,2,1,0:T(8,128)(2,1)S(1)} %get-tuple-element.22), kind=kLoop, calls=%fused_computation | loop fusion | flops 9437184 | bytes 12582912 | tf_op jit(solution)/shard_map/stack | solution.py:470
  35.5 0.0 copy-done.8
  35.5 0.4 concatenate.18
  35.9 0.8 pad_maximum_fusion.1.wl
  36.7 0.0 collective-permute-done.ra
  36.7 0.0 collective-permute-done.1.rb
  36.7 3.7 %edges.1 = (bf16[28,144,128]{2,1,0:T(8,128)(2,1)S(1)}, bf16[224,128]{1,0:T(8,128)(2,1)S(1)}, bf16[224,128]{1,0:T(8,128)(2,1)S(1)}) custom-call(bf16[16,128,128]{2,1,0:T(8,128)(2,1)S(1)} %get-tuple-element.12.xown, bf16[6,128,128]{2,1,0:T(8,128)(2,1)S(1)} %collective-permute-done.ra, bf16[6,128,128]{2,1,0:T(8,128)(2,1)S(1)} %collective-permute-done.1.rb), custom_call_target="tpu_custom_call" | custom-call | tf_op jit(solution)/shard_map/edges/pallas_call | solution.py:157
  40.4 0.0 copy-start.1
  40.4 1.0 copy-done.1
  41.3 1.1 collective-permute-start.2
  42.5 0.7 collective-permute-start.3
  43.1 0.0 copy-done.4
  43.1 0.7 maximum_maximum_fusion.wbig
  43.9 0.6 concatenate.21.wht
  44.5 1.0 collective-permute-done.2.rc
  45.5 0.0 copy-start.6
  45.5 0.0 collective-permute-done.3.rd
  45.5 0.0 copy-start.7
  45.5 0.0 all-to-all-done.recv
  45.5 0.6 copy-done.6
  46.1 0.0 copy-done.7
  46.2 60.7 %main.1 = (bf16[16,78,128]{2,1,0:T(8,128)(2,1)}, bf16[128,24,128]{2,1,0:T(8,128)(2,1)}) custom-call(bf16[128,32,128]{2,1,0:T(8,128)(2,1)} %all-to-all-done.recv, bf16[28,144,128]{2,1,0:T(8,128)(2,1)} %copy-done.1, bf16[224,128]{1,0:T(8,128)(2,1)} %copy-done.6, bf16[224,128]{1,0:T(8,128)(2,1)} %copy-done.7, bf16[256,512]{1,0:T(8,128)(2,1)} %maximum_maximum_fusion.wbig, ...), custom_call_target="tpu_custom_call" | custom-call | tf_op jit(solution)/shard_map/main/pallas_call | solution.py:372
  106.9 16.2 %all-to-all-start.1 = ((bf16[128,24,128]{2,1,0:T(8,128)(2,1)}), bf16[128,24,128]{2,1,0:T(8,128)(2,1)S(1)}, u32[]{:S(2)}, u32[]{:S(2)}) async-start(bf16[128,24,128]{2,1,0:T(8,128)(2,1)} %get-tuple-element.19), calls=%async_computation.1 | async-start | bytes 1572864 | tf_op jit(solution)/shard_map/all_to_all | solution.py:472
  123.1 1.8 %copy.14 = bf16[16,78,128]{2,0,1:T(8,128)(2,1)} copy(bf16[16,78,128]{2,1,0:T(8,128)(2,1)} %get-tuple-element.20) | data formatting | bytes 638976
  124.9 14.7 %all-to-all-done.1 = bf16[128,24,128]{2,1,0:T(8,128)(2,1)S(1)} async-done(((bf16[128,24,128]{2,1,0:T(8,128)(2,1)}), bf16[128,24,128]{2,1,0:T(8,128)(2,1)S(1)}, u32[]{:S(2)}, u32[]{:S(2)}) %all-to-all-start.1) | async-done | bytes 786464 | tf_op jit(solution)/shard_map/all_to_all | solution.py:472
  139.5 6.0 %place.1 = f32[45,78,180]{2,1,0:T(8,128)} custom-call(s32[1]{0:T(128)S(6)} %copy.22.ro, s32[1]{0:T(128)S(6)} %copy.23.co, bf16[2,16,4,24,128]{4,3,2,1,0:T(8,128)(2,1)S(1)} %bitcast.14), custom_call_target="tpu_custom_call" | custom-call | tf_op jit(solution)/shard_map/place/pallas_call | solution.py:431
  (7 shorter events, 0.1 us)
Async XLA Ops:
  3.0 1.5 %copy-start = (bf16[45,78,180]{2,1,0:T(8,128)(2,1)S(1)}, bf16[45,78,180]{2,1,0:T(8,128)(2,1)}, u32[]{:S(2)}) copy-start(bf16[45,78,180]{2,1,0:T(8,128)(2,1)} %coarse.1) | copy-start | bytes 3790804
  4.5 0.7 copy-start.2
  9.9 35.6 %all-to-all-start = ((bf16[128,32,128]{2,1,0:T(8,128)(2,1)}), bf16[128,32,128]{2,1,0:T(8,128)(2,1)}, u32[]{:S(2)}, u32[]{:S(2)}) async-start(bf16[128,32,128]{2,1,0:T(8,128)(2,1)} %get-tuple-element.11), calls=%async_computation | async-start | bytes 2097152 | tf_op jit(solution)/shard_map/all_to_all | solution.py:444
  21.6 15.1 %collective-permute-start = (bf16[6,128,128]{2,1,0:T(8,128)(2,1)S(1)}, bf16[6,128,128]{2,1,0:T(8,128)(2,1)S(1)}, u32[]{:S(2)}, u32[]{:S(2)}) collective-permute-start(bf16[6,128,128]{2,1,0:T(8,128)(2,1)S(1)} %get-tuple-element.13), channel_id=1, source_target_pairs={{0,4},{4,0},{8,12},{12,8},{16,20},{20,16},{24,28},{28,24},{32,36},... | collective-permute-start | bytes 589832 | tf_op jit(solution)/shard_map/ppermute | solution.py:447
  21.7 4.5 %copy-start.3 = (bf16[4,3,3,256,256]{4,3,2,1,0:T(8,128)(2,1)S(1)}, bf16[4,3,3,256,256]{4,3,2,1,0:T(8,128)(2,1)}, u32[]{:S(2)}) copy-start(bf16[4,3,3,256,256]{4,3,2,1,0:T(8,128)(2,1)} %param.17) | copy-start | bytes 14155780
  21.7 15.0 %collective-permute-start.1 = (bf16[6,128,128]{2,1,0:T(8,128)(2,1)S(1)}, bf16[6,128,128]{2,1,0:T(8,128)(2,1)S(1)}, u32[]{:S(2)}, u32[]{:S(2)}) collective-permute-start(bf16[6,128,128]{2,1,0:T(8,128)(2,1)S(1)} %get-tuple-element.14), channel_id=1, source_target_pairs={{4,8},{8,4},{12,16},{16,12},{20,24},{24,20},{28,32},{32,28},{36,40... | collective-permute-start | bytes 589832 | tf_op jit(solution)/shard_map/ppermute | solution.py:448
  26.2 2.8 %copy-start.5 = (bf16[78,256]{1,0:T(8,128)(2,1)S(1)}, bf16[78,256]{1,0:T(8,128)(2,1)}, u32[]{:S(2)}) copy-start(bf16[78,256]{1,0:T(8,128)(2,1)} %param.14) | copy-start | bytes 119812
  29.6 5.9 %copy-start.8 = (bf16[4,256]{1,0:T(4,128)(2,1)S(1)}, bf16[4,256]{1,0:T(4,128)(2,1)}, u32[]{:S(2)}) copy-start(bf16[4,256]{1,0:T(4,128)(2,1)} %param.15) | copy-start | bytes 6148
  29.6 13.5 %copy-start.4 = (bf16[256,78]{0,1:T(8,128)(2,1)S(1)}, bf16[256,78]{0,1:T(8,128)(2,1)}, u32[]{:S(2)}) copy-start(bf16[256,78]{0,1:T(8,128)(2,1)} %param.18) | copy-start | bytes 119812
  40.4 1.0 copy-start.1
  41.3 4.2 %collective-permute-start.2 = (bf16[224,128]{1,0:T(8,128)(2,1)S(1)}, bf16[224,128]{1,0:T(8,128)(2,1)S(1)}, u32[]{:S(2)}, u32[]{:S(2)}) collective-permute-start(bf16[224,128]{1,0:T(8,128)(2,1)S(1)} %get-tuple-element.16), channel_id=1, source_target_pairs={{0,1},{1,0},{2,3},{3,2},{64,65},{65,64},{66,67},{67,66},{4,5},{5,4... | collective-permute-start | bytes 172040 | tf_op jit(solution)/shard_map/ppermute | solution.py:452
  42.5 3.1 %collective-permute-start.3 = (bf16[224,128]{1,0:T(8,128)(2,1)S(1)}, bf16[224,128]{1,0:T(8,128)(2,1)S(1)}, u32[]{:S(2)}, u32[]{:S(2)}) collective-permute-start(bf16[224,128]{1,0:T(8,128)(2,1)S(1)} %get-tuple-element.17), channel_id=1, source_target_pairs={{1,2},{2,1},{3,64},{64,3},{65,66},{66,65},{5,6},{6,5},{7,68},{68,7... | collective-permute-start | bytes 172040 | tf_op jit(solution)/shard_map/ppermute | solution.py:453
  45.5 0.6 copy-start.6
  45.5 0.6 copy-start.7
  106.9 32.6 %all-to-all-start.1 = ((bf16[128,24,128]{2,1,0:T(8,128)(2,1)}), bf16[128,24,128]{2,1,0:T(8,128)(2,1)S(1)}, u32[]{:S(2)}, u32[]{:S(2)}) async-start(bf16[128,24,128]{2,1,0:T(8,128)(2,1)} %get-tuple-element.19), calls=%async_computation.1 | async-start | bytes 1572864 | tf_op jit(solution)/shard_map/all_to_all | solution.py:472

commit v3 on v2

--- a/solution.py
+++ b/solution.py
@@ -58,11 +58,39 @@
     return lax.axis_index("sec") * 4 + lax.axis_index("col")
 
 
-def pack_kernel(ro, co, coarse, static, cot, send, xown, pa, pb, prod):
+def rows_kernel(static, cot, xown, pa, pb):
+    xown[...] = jnp.zeros_like(xown)
+    xown[:, :CIN, :] = cot[...]
+    xown[:, 80:84, :] = static[...]
+    odd = (lax.axis_index("row") & 1) == 1
+    pa[...] = xown[pl.ds(jnp.where(odd, 0, TR - HR), HR)]
+    pb[...] = xown[pl.ds(jnp.where(odd, TR - HR, 0), HR)]
+
+
+def own_rows(static, cot):
+    return pl.pallas_call(
+        rows_kernel,
+        out_shape=[
+            jax.ShapeDtypeStruct((TR, 128, 128), BF),
+            jax.ShapeDtypeStruct((HR, 128, 128), BF),
+            jax.ShapeDtypeStruct((HR, 128, 128), BF),
+        ],
+        in_specs=[VM] * 2,
+        out_specs=[VM] * 3,
+        cost_estimate=pl.CostEstimate(flops=0, bytes_accessed=2 * MB, transcendentals=0),
+        compiler_params=pltpu.CompilerParams(vmem_limit_bytes=8 * MB),
+        name="own_rows",
+    )(static, cot)
+
+
+def pack_kernel(ro, co, coarse, after, send, xs, prod, sem):
     ri = lax.axis_index("row")
     ci = col_place()
     first_row = ro[0] - 1 - LAT_DEV * ri
     off = co[0] - 1 - LON_DEV * ci
+    start = jnp.clip(first_row, 0, LAT_DEV - 18)
+    copy = pltpu.make_async_copy(coarse.at[pl.ds(start, 18)], xs, sem)
+    copy.start()
     lj = iota((272, LON_DEV), 1)
     q = iota((272, LON_DEV), 0)
     tail = q - 80
@@ -72,15 +100,17 @@
     j_tail = jnp.where((s >= 0) & (s < 2), 8 * c + 8 + s, -100000)
     j = jnp.where(q < 80, jnp.where(q < 66, q, -100000), j_tail)
     sel = one_hot(lj == off + j)
-
-    def row(i, _):
-        li = first_row + i
-        ok = ((li >= 0) & (li < LAT_DEV)).astype(F32)
-        x = coarse[jnp.clip(li, 0, LAT_DEV - 1)]
-        prod[i, :, :CIN] = dotf(sel, x, NT) * ok
-        return 0
-
-    lax.fori_loop(0, 18, row, 0)
+    copy.wait()
+
+    def rows(g, _):
+        for k in range(6):
+            i = 6 * g + k
+            li = first_row + i
+            ok = jnp.where((li >= 0) & (li < LAT_DEV), 1.0, 0.0)
+            prod[i, :, :CIN] = dotf(sel, xs[jnp.clip(li - start, 0, 17)], NT) * ok
+        return 0
+
+    lax.fori_loop(0, 3, rows, 0)
 
     def dest(r, _):
         tails = prod[r, 80:144] + prod[r + 1, 144:208] + prod[r + 2, 208:272]
@@ -92,61 +122,42 @@
         return 0
 
     lax.fori_loop(0, 16, dest, 0)
-    xown[...] = jnp.zeros_like(xown)
-    xown[:, :CIN, :] = cot[...]
-    xown[:, 80:84, :] = static[...]
-    odd = ri & 1
-    pa[...] = xown[pl.ds(jnp.where(odd == 1, 0, TR - HR), HR)]
-    pb[...] = xown[pl.ds(jnp.where(odd == 1, TR - HR, 0), HR)]
-
-
-def pack(ro, co, coarse, static, cot):
+
+
+def pack(ro, co, coarse, after):
     return pl.pallas_call(
         pack_kernel,
-        out_shape=[
-            jax.ShapeDtypeStruct((128, 32, 128), BF),
-            jax.ShapeDtypeStruct((TR, 128, 128), BF),
-            jax.ShapeDtypeStruct((HR, 128, 128), BF),
-            jax.ShapeDtypeStruct((HR, 128, 128), BF),
+        out_shape=jax.ShapeDtypeStruct((128, 32, 128), BF),
+        in_specs=[SM, SM, pl.BlockSpec(memory_space=pltpu.HBM), pl.BlockSpec(memory_space=pl.ANY)],
+        out_specs=VM,
+        scratch_shapes=[
+            pltpu.VMEM((18, CIN, LON_DEV), BF),
+            pltpu.VMEM((18, 272, 128), F32),
+            pltpu.SemaphoreType.DMA(()),
         ],
-        in_specs=[SM, SM, VM, VM, VM],
-        out_specs=[VM] * 4,
-        scratch_shapes=[pltpu.VMEM((18, 272, 128), F32)],
-        compiler_params=pltpu.CompilerParams(vmem_limit_bytes=32 * MB),
+        cost_estimate=pl.CostEstimate(flops=0, bytes_accessed=8 * MB, transcendentals=0),
+        compiler_params=pltpu.CompilerParams(vmem_limit_bytes=16 * MB),
         name="pack",
-    )(ro, co, coarse, static, cot)
-
-
-def edge_kernel(xown, ra, rb, ct, pc, pd, edge):
-    ri = lax.axis_index("row")
-    ci = col_place()
-    m = iota((EC, 128), 0)
-    perm = one_hot(ext_col(m) - HC == iota((EC, 128), 1))
+    )(ro, co, coarse, after)
+
+
+def edge_kernel(xown, ra, rb, pc, pd, edge):
+    odd = (lax.axis_index("row") & 1) == 1
+    oddc = (col_place() & 1) == 1
     q = iota((16, 128), 0)
     sel = one_hot(iota((16, 128), 1) == jnp.where(q < 8, q, q + 112))
-    both = jnp.concatenate([perm, sel], axis=0)
-
-    def do(y, x):
-        r = dotf(both, x, NT)
-        ct[y] = r[:EC].astype(BF)
-        edge[y] = r[EC:]
-
-    def mid(y, _):
-        do(y + HR, xown[y])
-        return 0
-
-    lax.fori_loop(0, TR, mid, 0)
-    odd = (ri & 1) == 1
-
-    def ends(y, _):
-        a = ra[y]
-        b = rb[y]
-        do(y, jnp.where(odd, a, b))
-        do(y + HR + TR, jnp.where(odd, b, a))
-        return 0
-
-    lax.fori_loop(0, HR, ends, 0)
-    oddc = (ci & 1) == 1
+
+    def do(y0, x):
+        n = x.shape[0]
+        r = dotf(sel, x.reshape(n * 128, 128), NT)
+        for k in range(n):
+            edge[y0 + k] = r[:, k * 128 : (k + 1) * 128]
+
+    do(HR, xown[...])
+    a = ra[...]
+    b = rb[...]
+    do(0, jnp.where(odd, a, b))
+    do(HR + TR, jnp.where(odd, b, a))
     left = edge[:, :8, :].reshape(ER * 8, 128)
     right = edge[:, 8:, :].reshape(ER * 8, 128)
     pc[...] = jnp.where(oddc, left, right).astype(BF)
@@ -157,25 +168,93 @@
     return pl.pallas_call(
         edge_kernel,
         out_shape=[
-            jax.ShapeDtypeStruct((ER, EC, 128), BF),
             jax.ShapeDtypeStruct((ER * 8, 128), BF),
             jax.ShapeDtypeStruct((ER * 8, 128), BF),
         ],
         in_specs=[VM] * 3,
-        out_specs=[VM] * 3,
+        out_specs=[VM] * 2,
         scratch_shapes=[pltpu.VMEM((ER, 16, 128), F32)],
-        compiler_params=pltpu.CompilerParams(vmem_limit_bytes=16 * MB),
+        cost_estimate=pl.CostEstimate(flops=0, bytes_accessed=4 * MB, transcendentals=0),
+        compiler_params=pltpu.CompilerParams(vmem_limit_bytes=8 * MB),
         name="edges",
     )(xown, ra, rb)
 
 
+def cells_kernel(xown, ra, rb, rc, rd, ct):
+    odd = (lax.axis_index("row") & 1) == 1
+    oddc = (col_place() & 1) == 1
+    perm = one_hot(ext_col(iota((EC, 128), 0)) - HC == iota((EC, 128), 1))
+    m = iota((2 * EC, 16), 0)
+    q = iota((2 * EC, 16), 1)
+    y2 = (m >= EC).astype(jnp.int32)
+    e2 = ext_col(m - y2 * EC)
+    same = y2 == (q >> 3)
+    perm_l = one_hot(same & (e2 == (q & 7)))
+    perm_r = one_hot(same & (e2 - (HC + TC) == (q & 7)))
+
+    def do(y, x):
+        rows = pl.ds(pl.multiple_of(y * 8, 16), 16)
+        c = rc[rows, :]
+        d = rd[rows, :]
+        halo = dotf(perm_l, jnp.where(oddc, c, d)) + dotf(perm_r, jnp.where(oddc, d, c))
+        for k in range(2):
+            ct[y + k] = (dotf(perm, x[k], NT) + halo[k * EC : (k + 1) * EC]).astype(BF)
+
+    def mid(i, _):
+        for k in range(2):
+            y = 4 * i + 2 * k
+            do(y + HR, xown[pl.ds(y, 2)])
+        return 0
+
+    lax.fori_loop(0, TR // 4, mid, 0)
+    for y in range(0, HR, 2):
+        a = ra[y : y + 2]
+        b = rb[y : y + 2]
+        do(y, jnp.where(odd, a, b))
+        do(y + HR + TR, jnp.where(odd, b, a))
+
+
+def cells(xown, ra, rb, rc, rd):
+    return pl.pallas_call(
+        cells_kernel,
+        out_shape=jax.ShapeDtypeStruct((ER, EC, 128), BF),
+        in_specs=[VM] * 5,
+        out_specs=VM,
+        cost_estimate=pl.CostEstimate(flops=0, bytes_accessed=8 * MB, transcendentals=0),
+        compiler_params=pltpu.CompilerParams(vmem_limit_bytes=8 * MB),
+        name="cells",
+    )(xown, ra, rb, rc, rd)
+
+
+def pairs_kernel(kern, out):
+    k0, k1, k2 = (kern[p].astype(F32) for p in range(3))
+    out[0] = kern[0]
+    out[1] = (0.5 * (k0 + k1 + k2)).astype(BF)
+    out[2] = (0.5 * (k0 - k1 + k2)).astype(BF)
+    out[3] = kern[2]
+
+
+def pairs(kern):
+    return pl.pallas_call(
+        pairs_kernel,
+        out_shape=jax.ShapeDtypeStruct((BLOCKS, 4, 3, W, W), BF),
+        grid=(BLOCKS, 3),
+        in_specs=[pl.BlockSpec((None, 3, None, W, W), lambda b, q: (b, 0, q, 0, 0))],
+        out_specs=pl.BlockSpec((None, 4, None, W, W), lambda b, q: (b, 0, q, 0, 0)),
+        cost_estimate=pl.CostEstimate(flops=0, bytes_accessed=12 * MB, transcendentals=0),
+        compiler_params=pltpu.CompilerParams(vmem_limit_bytes=8 * MB),
+        name="pairs",
+    )(kern)
+
+
 def main_kernel(
-    recv, ct, rc, rd, wbig, gains, kern, wht, wl, fine, msg,
-    vup, hid, act, cv, hs_s, ds_s, back, gsum,
+    recv, ct, wbig, gains, kern_hbm, wht, wl, fine, msg,
+    vup, hid, act, cv, hs_s, ds_s, back, gsum, kern, sem,
 ):
     ri = lax.axis_index("row")
     ci = col_place()
-    oddc = (ci & 1) == 1
+    load = pltpu.make_async_copy(kern_hbm, kern, sem)
+    load.start()
 
     win = jnp.sum(recv[...].astype(F32), axis=0)
     win = jnp.where(iota((32, 128), 1) < CIN, win, 0.0).astype(BF)
@@ -188,21 +267,7 @@
         coef = col_weight(ext_col(m), j).astype(BF)
         vup[k] = dotf(coef, win)
 
-    m4 = iota((4 * EC, 32), 0)
-    q4 = iota((4 * EC, 32), 1)
-    y4 = (
-        (m4 >= EC).astype(jnp.int32) + (m4 >= 2 * EC).astype(jnp.int32) + (m4 >= 3 * EC).astype(jnp.int32)
-    )
-    e4 = ext_col(m4 - y4 * EC)
-    same = y4 == (q4 >> 3)
-    perm_l = one_hot(same & (e4 == (q4 & 7)))
-    perm_r = one_hot(same & (e4 - (HC + TC) == (q4 & 7)))
-
     def lift(g, _):
-        rows = pl.ds(pl.multiple_of(g * 32, 32), 32)
-        c = rc[rows, :]
-        d = rd[rows, :]
-        halo = dotf(perm_l, jnp.where(oddc, c, d)) + dotf(perm_r, jnp.where(oddc, d, c))
         ups = []
         for k in range(4):
             n = 2 * (g * 4 + k) + 5
@@ -211,8 +276,7 @@
             ups.append(((1.0 - t) * vup[a] + t * vup[a + 1]).astype(BF))
         up = jnp.concatenate(ups, axis=0)
         own = ct[pl.ds(g * 4, 4)].reshape(4 * EC, 128)
-        both = (own.astype(F32) + halo).astype(BF)
-        r = dotf(jnp.concatenate([up, both], axis=1), wbig[...])
+        r = dotf(jnp.concatenate([up, own], axis=1), wbig[...])
         cv[pl.ds(g * 4, 4)] = r[:, :W].reshape(4, EC, W)
         back[pl.ds(g * 4, 4)] = r[:, W:].reshape(4, EC, W)
         return 0
@@ -297,6 +361,7 @@
         conv(b, jnp.where(deep, HR, b + 1), jnp.where(deep, HR + TR, ER - 1 - b), False)
         return 0
 
+    load.wait()
     lax.fori_loop(0, BLOCKS, forward, 0)
 
     def last(y):
@@ -368,14 +433,14 @@
     lax.fori_loop(0, 128, spread, 0)
 
 
-def main(recv, ct, rc, rd, wbig, gains, kern, wht, wl):
+def main(recv, ct, wbig, gains, kern, wht, wl):
     return pl.pallas_call(
         main_kernel,
         out_shape=[
             jax.ShapeDtypeStruct((TR, CIN, TC), BF),
             jax.ShapeDtypeStruct((128, 24, 128), BF),
         ],
-        in_specs=[VM] * 9,
+        in_specs=[VM] * 4 + [pl.BlockSpec(memory_space=pltpu.HBM)] + [VM] * 2,
         out_specs=[VM] * 2,
         scratch_shapes=[
             pltpu.VMEM((3, EC, 128), F32),
@@ -386,13 +451,32 @@
             pltpu.VMEM((BLOCKS, ER, EC, W), BF),
             pltpu.VMEM((ER, EC, W), F32),
             pltpu.VMEM((3, 32, W), F32),
+            pltpu.VMEM((BLOCKS, 4, 3, W, W), BF),
+            pltpu.SemaphoreType.DMA(()),
         ],
-        compiler_params=pltpu.CompilerParams(vmem_limit_bytes=56 * MB),
+        compiler_params=pltpu.CompilerParams(vmem_limit_bytes=58 * MB),
         name="main",
-    )(recv, ct, rc, rd, wbig, gains, kern, wht, wl)
-
-
-def place_kernel(ro, co, recv, out, acc):
+    )(recv, ct, wbig, gains, kern, wht, wl)
+
+
+def blank_kernel(after, out):
+    out[...] = jnp.zeros_like(out)
+
+
+def blank(after):
+    return pl.pallas_call(
+        blank_kernel,
+        out_shape=jax.ShapeDtypeStruct((LAT_DEV, CIN, LON_DEV), F32),
+        grid=(5,),
+        in_specs=[pl.BlockSpec(memory_space=pl.ANY)],
+        out_specs=pl.BlockSpec((9, CIN, LON_DEV), lambda i: (i, 0, 0)),
+        cost_estimate=pl.CostEstimate(flops=0, bytes_accessed=4 * MB, transcendentals=0),
+        compiler_params=pltpu.CompilerParams(vmem_limit_bytes=8 * MB),
+        name="blank",
+    )(after)
+
+
+def place_kernel(ro, co, recv, zero, out, acc, sem):
     first_row = ro[0] - 1 - LAT_DEV * lax.axis_index("row")
     off = co[0] - 1 - LON_DEV * col_place()
     q = iota((192, 512), 0)
@@ -404,53 +488,65 @@
     sel = one_hot((j >= 0) & (j < 10) & (lj == off + 8 * c + j) & (lj < LON_DEV))
     acc[...] = jnp.zeros_like(acc)
 
-    def row(r, _):
-        a = recv[:, r].astype(F32).reshape(192, 128).astype(BF)
-        o = dotf(a, sel, TN)
-        for k in range(3):
-            acc[r + k, :40] = acc[r + k, :40] + o[40 * k : 40 * k + 40, :256]
-            acc[r + k, 40:] = acc[r + k, 40:] + o[40 * k : 40 * k + 40, 256:]
-        return 0
-
-    lax.fori_loop(0, 16, row, 0)
-    out[...] = jnp.zeros_like(out)
-
-    def store(i, _):
-        li = first_row + i
-
-        @pl.when((li >= 0) & (li < LAT_DEV))
-        def _():
-            out[jnp.clip(li, 0, LAT_DEV - 1)] = acc[i, :CIN, :LON_DEV]
-
-        return 0
-
-    lax.fori_loop(0, 18, store, 0)
-
-
-def place(ro, co, recv):
+    def rows(g, _):
+        for u in range(4):
+            r = 4 * g + u
+            a = recv[:, r].astype(F32).reshape(192, 128).astype(BF)
+            o = dotf(a, sel, TN)
+            for k in range(3):
+                acc[r + k, :40] = acc[r + k, :40] + o[40 * k : 40 * k + 40, :LON_DEV]
+                acc[r + k, 40:] = acc[r + k, 40:] + o[40 * k : 40 * k + 38, 256 : 256 + LON_DEV]
+        return 0
+
+    lax.fori_loop(0, 4, rows, 0)
+    lo = jnp.clip(-first_row, 0, 18)
+    hi = jnp.clip(LAT_DEV - first_row, lo, 18)
+
+    def copy(i):
+        li = jnp.clip(first_row + i, 0, LAT_DEV - 1)
+        return pltpu.make_async_copy(acc.at[i], out.at[li], sem)
+
+    def start(i, _):
+        copy(i).start()
+        return 0
+
+    def wait(i, _):
+        copy(i).wait()
+        return 0
+
+    lax.fori_loop(lo, hi, start, 0)
+    lax.fori_loop(lo, hi, wait, 0)
+
+
+def place(ro, co, recv, zero):
+    hbm = pl.BlockSpec(memory_space=pltpu.HBM)
     return pl.pallas_call(
         place_kernel,
         out_shape=jax.ShapeDtypeStruct((LAT_DEV, CIN, LON_DEV), F32),
-        in_specs=[SM, SM, VM],
-        out_specs=VM,
-        scratch_shapes=[pltpu.VMEM((18, 80, 256), F32)],
-        compiler_params=pltpu.CompilerParams(vmem_limit_bytes=32 * MB),
+        in_specs=[SM, SM, VM, hbm],
+        out_specs=hbm,
+        input_output_aliases={3: 0},
+        scratch_shapes=[pltpu.VMEM((18, CIN, LON_DEV), F32), pltpu.SemaphoreType.DMA(())],
+        compiler_params=pltpu.CompilerParams(vmem_limit_bytes=16 * MB),
         name="place",
-    )(ro, co, recv)
+    )(ro, co, recv, zero)
 
 
 def shards(coarse, ro, co, static, w_lift, w_static, gains, kern, w_head, cot):
-    send, xown, pa, pb = pack(ro, co, coarse, static, cot)
-    recv = lax.all_to_all(send, ("sec", "row", "col"), 0, 0, tiled=True)
+    xown, pa, pb = own_rows(static, cot)
     near = [(i, i ^ 1) for i in range(16)]
     far = [(i, j) for i in range(16) for j in [i + 1 if i & 1 else i - 1] if 0 <= j < 16]
     ra = lax.ppermute(pa, "row", near)
     rb = lax.ppermute(pb, "row", far)
-    ct, pc, pd = edges(xown, ra, rb)
+    send = pack(ro, co, coarse, pa)
+    pc, pd = edges(xown, ra, rb)
     near = [(i, i ^ 1) for i in range(8)]
     far = [(i, j) for i in range(8) for j in [i + 1 if i & 1 else i - 1] if 0 <= j < 8]
+    send, pc, pd = lax.optimization_barrier((send, pc, pd))
     rc = lax.ppermute(pc, ("sec", "col"), near)
     rd = lax.ppermute(pd, ("sec", "col"), far)
+    recv = lax.all_to_all(send, ("sec", "row", "col"), 0, 0, tiled=True)
+    ct = cells(xown, ra, rb, rc, rd)
 
     wht = w_head.T
     zero = jnp.zeros
@@ -466,11 +562,9 @@
     wl = jnp.concatenate(
         [jnp.pad(wl, ((0, 0), (0, 0), (40 * k, 88 - 40 * k))).reshape(W, 256) for k in range(3)], 0
     )
-    k0, k1, k2 = (kern[:, p].astype(F32) for p in range(3))
-    wino = jnp.stack([k0, 0.5 * (k0 + k1 + k2), 0.5 * (k0 - k1 + k2), k2], axis=1).astype(BF)
-    fine, msg = main(recv, ct, rc, rd, wbig, gains, wino, wht80, wl)
+    fine, msg = main(recv, ct, wbig, gains, pairs(kern), wht80, wl)
     back = lax.all_to_all(msg, ("sec", "row", "col"), 0, 0, tiled=True)
-    return fine, place(ro, co, back.reshape(2, 16, 4, 24, 128))
+    return fine, place(ro, co, back.reshape(2, 16, 4, 24, 128), blank(msg))
 
 
 def solution(mesh):

time: 146 us -> 128 us (0.88)
  other arithmetic: 10.1 us -> 1.55 us
  starting transfers between devices: 30.5 us -> 24.3 us
  Pallas kernels: 75.1 us -> 69.8 us
  local copies, waits for them, and re-layouts: 12 us -> 13.8 us
    another operation x2 -> x0, other arithmetic: 8.56 us -> none  [the longest x1 5.81 us: shards(): jnp.stack([k0, 0.5 * (k0 + k1 + k2), 0.5 * (k0 - k1 + k2), k2], axis=1)]
    all_to_all x1, starting transfers between devices: 16.2 us -> 7.84 us  [shards(): back = lax.all_to_all(msg, ('sec', 'row', 'col'), 0, 0, tiled=True)]
    unnamed x21 -> x25, local copies, waits for them, and re-layouts: 6.67 us -> 12.2 us
    pallas_call x1, Pallas kernels: 6.02 us -> 1.62 us  [place(): pl.pallas_call(place_kernel, out_shape=jax.ShapeDtypeStruct((LAT_DEV, CIN...]
    slice x1 -> x0, local copies, waits for them, and re-layouts: 3.69 us -> none  [shards(): k0, k1, k2 = (kern[:, p].astype(F32) for p in range(3))]
    all_to_all x1, waiting for transfers between devices: 0.01 us -> 3.57 us  [shards(): recv = lax.all_to_all(send, ('sec', 'row', 'col'), 0, 0, tiled=True)]
    all_to_all x1, waiting for transfers between devices: 14.7 us -> 11.7 us  [shards(): back = lax.all_to_all(msg, ('sec', 'row', 'col'), 0, 0, tiled=True)]
    ppermute x1, starting transfers between devices: 0.09 us -> 3 us  [shards(): ra = lax.ppermute(pa, 'row', near)]
  transfers between devices with their start and end apart: 6 -> 6, of which waited for: 2 -> 3; matrix products, arithmetic and copies ran while one was open for 12% -> 3% of each run, Pallas kernels for 3% -> 8%
where the time goes in v3:
time: 128 us; the launch traced here: 127 us
  Pallas kernels  69.8 us (55%)
  starting transfers between devices  24.3 us (19%)
  waiting for transfers between devices  15.5 us (12%)
  local copies, waits for them, and re-layouts  13.8 us (11%)
  between operations  2.19 us (2%)
  other arithmetic  1.55 us (1%)
    pallas_call x1, Pallas kernels, main(): pl.pallas_call(main_kernel, out_shape=[jax.ShapeDtypeStruct((TR, CIN, TC)...  57.9 us
    unnamed x25, local copies, waits for them, and re-layouts  12.2 us
    all_to_all x1, waiting for transfers between devices, shards(): back = lax.all_to_all(msg, ('sec', 'row', 'col'), 0, 0, tiled=True)  11.7 us
    all_to_all x1, starting transfers between devices, shards(): recv = lax.all_to_all(send, ('sec', 'row', 'col'), 0, 0, tiled=True)  11 us
    all_to_all x1, starting transfers between devices, shards(): back = lax.all_to_all(msg, ('sec', 'row', 'col'), 0, 0, tiled=True)  7.84 us
    all_to_all x1, waiting for transfers between devices, shards(): recv = lax.all_to_all(send, ('sec', 'row', 'col'), 0, 0, tiled=True)  3.57 us
    ppermute x1, starting transfers between devices, shards(): ra = lax.ppermute(pa, 'row', near)  3 us
    pallas_call x1, Pallas kernels, blank(): pl.pallas_call(blank_kernel, out_shape=jax.ShapeDtypeStruct((LAT_DEV, CIN...  2.75 us
  transfers between devices with their start and end apart: 6, of which 3 were waited for; matrix products, arithmetic and copies ran while one was open for 3% of the time, Pallas kernels for 8%

profile of v3, /device:TPU:0, one launch (start us, length us, event | category | flops | bytes accessed | tf_op | source)
XLA Modules:
  0.0 127.2 jit_solution(2686515841847746390)
XLA Ops:
  0.6 0.0 copy-start.9
  0.6 1.1 copy.13.cot
  1.7 0.0 copy-start.5
  1.7 0.7 copy-done.5
  2.4 0.1 own_rows.1
  2.6 0.0 copy-start.10
  2.6 0.7 collective-permute-start.1
  3.3 3.0 %collective-permute-start = (bf16[6,128,128]{2,1,0:T(8,128)(2,1)S(1)}, bf16[6,128,128]{2,1,0:T(8,128)(2,1)S(1)}, u32[]{:S(2)}, u32[]{:S(2)}) collective-permute-start(bf16[6,128,128]{2,1,0:T(8,128)(2,1)S(1)} %get-tuple-element.12.after), channel_id=1, source_target_pairs={{0,4},{4,0},{8,12},{12,8},{16,20},{20,16},{24,28},{28,24},{32,36},... | collective-permute-start | bytes 589832 | tf_op jit(solution)/shard_map/ppermute | solution.py:539
  7.6 0.0 copy-start.4
  7.6 1.5 %copy-done.4 = bf16[45,78,180]{2,1,0:T(8,128)(2,1)S(1)} copy-done((bf16[45,78,180]{2,1,0:T(8,128)(2,1)S(1)}, bf16[45,78,180]{2,1,0:T(8,128)(2,1)}, u32[]{:S(2)}) %copy-start.4) | copy-done | bytes 1263624
  9.1 0.0 copy-start.8
  9.1 2.7 %pack.1 = bf16[128,32,128]{2,1,0:T(8,128)(2,1)} custom-call(s32[1]{0:T(128)S(6)} %copy.24.ro, s32[1]{0:T(128)S(6)} %copy.25.co, bf16[45,78,180]{2,1,0:T(8,128)(2,1)S(1)} %copy-done.4, bf16[6,128,128]{2,1,0:T(8,128)(2,1)S(1)} %get-tuple-element.12.after), custom_call_target="tpu_custom_call" | custom-call | bytes 8388608 | tf_op jit(solution)/shard_map/pack/pallas_call | solution.py:128
  11.8 0.0 collective-permute-done.1.rb
  11.8 0.0 collective-permute-done.ra
  11.8 0.3 edges.1
  12.2 11.0 %all-to-all-start = ((bf16[128,32,128]{2,1,0:T(8,128)(2,1)}), bf16[128,32,128]{2,1,0:T(8,128)(2,1)S(1)}, u32[]{:S(2)}, u32[]{:S(2)}) async-start(bf16[128,32,128]{2,1,0:T(8,128)(2,1)} %pack.1), calls=%async_computation | async-start | bytes 2097152 | tf_op jit(solution)/shard_map/all_to_all | solution.py:548
  23.2 0.0 copy-done.9
  23.2 0.1 copy.14
  23.3 0.5 fusion
  23.9 0.0 copy-done.10
  23.9 0.4 concatenate.18
  24.3 0.8 pad_maximum_fusion.wl
  25.1 1.1 collective-permute-start.2
  26.2 0.7 collective-permute-start.3
  26.9 0.0 copy-done.8
  26.9 0.7 maximum_maximum_fusion.wbig
  27.6 0.6 concatenate.21.wht
  28.3 0.0 copy-start.1
  28.3 2.3 %copy-done.1 = bf16[4,3,3,256,256]{4,3,2,1,0:T(8,128)(2,1)S(1)} copy-done((bf16[4,3,3,256,256]{4,3,2,1,0:T(8,128)(2,1)S(1)}, bf16[4,3,3,256,256]{4,3,2,1,0:T(8,128)(2,1)}, u32[]{:S(2)}) %copy-start.1) | copy-done | bytes 4718616
  30.6 2.5 %pairs.1.kern_hbm = bf16[4,4,3,256,256]{4,3,2,1,0:T(8,128)(2,1)S(1)} custom-call(bf16[4,3,3,256,256]{4,3,2,1,0:T(8,128)(2,1)S(1)} %copy-done.1), custom_call_target="tpu_custom_call" | custom-call | bytes 12582912 | tf_op jit(solution)/shard_map/pairs/pallas_call | solution.py:238
  33.1 0.0 copy-start
  33.1 2.6 %copy-done = bf16[4,4,3,256,256]{4,3,2,1,0:T(8,128)(2,1)} copy-done((bf16[4,4,3,256,256]{4,3,2,1,0:T(8,128)(2,1)}, bf16[4,4,3,256,256]{4,3,2,1,0:T(8,128)(2,1)S(1)}, u32[]{:S(2)}) %copy-start) | copy-done | bytes 6291480
  35.7 0.2 collective-permute-done.2.rc
  35.9 0.0 collective-permute-done.3.rd
  36.0 1.9 %cells.1.ct = bf16[28,144,128]{2,1,0:T(8,128)(2,1)S(1)} custom-call(bf16[16,128,128]{2,1,0:T(8,128)(2,1)S(1)} %get-tuple-element.13.xown, bf16[6,128,128]{2,1,0:T(8,128)(2,1)S(1)} %collective-permute-done.ra, bf16[6,128,128]{2,1,0:T(8,128)(2,1)S(1)} %collective-permute-done.1.rb, bf16[224,128]{1,0:T(8,128)(2,1)S(1)} %collective-permute-done.2.rc, ...), custom_call_target="tpu_custom_call" | custom-call | bytes 8388608 | tf_op jit(solution)/shard_map/cells/pallas_call | solution.py:218
  37.8 0.0 copy-start.2
  37.9 1.0 copy-done.2
  38.8 3.6 %all-to-all-done.recv = bf16[128,32,128]{2,1,0:T(8,128)(2,1)S(1)} async-done(((bf16[128,32,128]{2,1,0:T(8,128)(2,1)}), bf16[128,32,128]{2,1,0:T(8,128)(2,1)S(1)}, u32[]{:S(2)}, u32[]{:S(2)}) %all-to-all-start) | async-done | bytes 1048608 | tf_op jit(solution)/shard_map/all_to_all | solution.py:548
  42.4 0.0 copy-start.6
  42.4 1.0 copy-done.6
  43.4 57.9 %main.1 = (bf16[16,78,128]{2,1,0:T(8,128)(2,1)}, bf16[128,24,128]{2,1,0:T(8,128)(2,1)}) custom-call(bf16[128,32,128]{2,1,0:T(8,128)(2,1)} %copy-done.6, bf16[28,144,128]{2,1,0:T(8,128)(2,1)} %copy-done.2, bf16[256,512]{1,0:T(8,128)(2,1)} %maximum_maximum_fusion.wbig, f32[4,256]{1,0:T(4,128)} %gains.1, bf16[4,4,3,256,256]{4,3,2,1,0:T(8,128)(2,1)} %copy-done, ...), custom_call_target="tpu_custom_call" | custom-call | tf_op jit(solution)/shard_map/main/pallas_call | solution.py:437
  101.3 0.0 copy-start.7
  101.3 7.8 %all-to-all-start.1 = ((bf16[128,24,128]{2,1,0:T(8,128)(2,1)}), bf16[128,24,128]{2,1,0:T(8,128)(2,1)S(1)}, u32[]{:S(2)}, u32[]{:S(2)}) async-start(bf16[128,24,128]{2,1,0:T(8,128)(2,1)} %get-tuple-element.21.after), calls=%async_computation.1 | async-start | bytes 1572864 | tf_op jit(solution)/shard_map/all_to_all | solution.py:566
  109.1 0.0 copy-start.3
  109.1 1.2 copy-done.3
  110.3 2.7 %blank.1.zero = f32[45,78,180]{2,1,0:T(8,128)} custom-call(bf16[128,24,128]{2,1,0:T(8,128)(2,1)S(1)} %copy-done.3), custom_call_target="tpu_custom_call" | custom-call | bytes 4194304 | tf_op jit(solution)/shard_map/blank/pallas_call | solution.py:467
  113.0 0.0 copy-done.7
  113.0 0.8 copy.15
  113.8 11.7 %all-to-all-done.1 = bf16[128,24,128]{2,1,0:T(8,128)(2,1)S(1)} async-done(((bf16[128,24,128]{2,1,0:T(8,128)(2,1)}), bf16[128,24,128]{2,1,0:T(8,128)(2,1)S(1)}, u32[]{:S(2)}, u32[]{:S(2)}) %all-to-all-start.1) | async-done | bytes 786464 | tf_op jit(solution)/shard_map/all_to_all | solution.py:566
  125.6 1.6 %place.1 = f32[45,78,180]{2,1,0:T(8,128)} custom-call(s32[1]{0:T(128)S(6)} %copy.24.ro, s32[1]{0:T(128)S(6)} %copy.25.co, bf16[2,16,4,24,128]{4,3,2,1,0:T(8,128)(2,1)S(1)} %bitcast.14, f32[45,78,180]{2,1,0:T(8,128)} %blank.1.zero), custom_call_target="tpu_custom_call", output_to_operand_aliasing={{}: (3, {})} | custom-call | tf_op jit(solution)/shard_map/place/pallas_call | solution.py:523
  (7 shorter events, 0.1 us)
Async XLA Ops:
  0.6 22.6 %copy-start.9 = (bf16[78,256]{1,0:T(8,128)(2,1)S(1)}, bf16[78,256]{1,0:T(8,128)(2,1)}, u32[]{:S(2)}) copy-start(bf16[78,256]{1,0:T(8,128)(2,1)} %param.14) | copy-start | bytes 119812
  1.7 0.7 copy-start.5
  2.6 21.3 %copy-start.10 = (bf16[4,256]{1,0:T(4,128)(2,1)S(1)}, bf16[4,256]{1,0:T(4,128)(2,1)}, u32[]{:S(2)}) copy-start(bf16[4,256]{1,0:T(4,128)(2,1)} %param.15) | copy-start | bytes 6148
  2.6 9.2 %collective-permute-start.1 = (bf16[6,128,128]{2,1,0:T(8,128)(2,1)S(1)}, bf16[6,128,128]{2,1,0:T(8,128)(2,1)S(1)}, u32[]{:S(2)}, u32[]{:S(2)}) collective-permute-start(bf16[6,128,128]{2,1,0:T(8,128)(2,1)S(1)} %get-tuple-element.14), channel_id=1, source_target_pairs={{4,8},{8,4},{12,16},{16,12},{20,24},{24,20},{28,32},{32,28},{36,40... | collective-permute-start | bytes 589832 | tf_op jit(solution)/shard_map/ppermute | solution.py:540
  3.3 8.6 %collective-permute-start = (bf16[6,128,128]{2,1,0:T(8,128)(2,1)S(1)}, bf16[6,128,128]{2,1,0:T(8,128)(2,1)S(1)}, u32[]{:S(2)}, u32[]{:S(2)}) collective-permute-start(bf16[6,128,128]{2,1,0:T(8,128)(2,1)S(1)} %get-tuple-element.12.after), channel_id=1, source_target_pairs={{0,4},{4,0},{8,12},{12,8},{16,20},{20,16},{24,28},{28,24},{32,36},... | collective-permute-start | bytes 589832 | tf_op jit(solution)/shard_map/ppermute | solution.py:539
  7.6 1.5 %copy-start.4 = (bf16[45,78,180]{2,1,0:T(8,128)(2,1)S(1)}, bf16[45,78,180]{2,1,0:T(8,128)(2,1)}, u32[]{:S(2)}) copy-start(bf16[45,78,180]{2,1,0:T(8,128)(2,1)} %coarse.1) | copy-start | bytes 3790804
  9.1 17.8 %copy-start.8 = (bf16[256,78]{0,1:T(8,128)(2,1)S(1)}, bf16[256,78]{0,1:T(8,128)(2,1)}, u32[]{:S(2)}) copy-start(bf16[256,78]{0,1:T(8,128)(2,1)} %param.18) | copy-start | bytes 119812
  12.2 30.2 %all-to-all-start = ((bf16[128,32,128]{2,1,0:T(8,128)(2,1)}), bf16[128,32,128]{2,1,0:T(8,128)(2,1)S(1)}, u32[]{:S(2)}, u32[]{:S(2)}) async-start(bf16[128,32,128]{2,1,0:T(8,128)(2,1)} %pack.1), calls=%async_computation | async-start | bytes 2097152 | tf_op jit(solution)/shard_map/all_to_all | solution.py:548
  25.1 10.8 %collective-permute-start.2 = (bf16[224,128]{1,0:T(8,128)(2,1)S(1)}, bf16[224,128]{1,0:T(8,128)(2,1)S(1)}, u32[]{:S(2)}, u32[]{:S(2)}) collective-permute-start(bf16[224,128]{1,0:T(8,128)(2,1)S(1)} %get-tuple-element.18), channel_id=1, source_target_pairs={{0,1},{1,0},{2,3},{3,2},{64,65},{65,64},{66,67},{67,66},{4,5},{5,4... | collective-permute-start | bytes 172040 | tf_op jit(solution)/shard_map/ppermute | solution.py:546
  26.2 9.7 %collective-permute-start.3 = (bf16[224,128]{1,0:T(8,128)(2,1)S(1)}, bf16[224,128]{1,0:T(8,128)(2,1)S(1)}, u32[]{:S(2)}, u32[]{:S(2)}) collective-permute-start(bf16[224,128]{1,0:T(8,128)(2,1)S(1)} %get-tuple-element.19), channel_id=1, source_target_pairs={{1,2},{2,1},{3,64},{64,3},{65,66},{66,65},{5,6},{6,5},{7,68},{68,7... | collective-permute-start | bytes 172040 | tf_op jit(solution)/shard_map/ppermute | solution.py:547
  28.3 2.3 %copy-start.1 = (bf16[4,3,3,256,256]{4,3,2,1,0:T(8,128)(2,1)S(1)}, bf16[4,3,3,256,256]{4,3,2,1,0:T(8,128)(2,1)}, u32[]{:S(2)}) copy-start(bf16[4,3,3,256,256]{4,3,2,1,0:T(8,128)(2,1)} %kern.1) | copy-start | bytes 14155780
  33.1 2.7 %copy-start = (bf16[4,4,3,256,256]{4,3,2,1,0:T(8,128)(2,1)}, bf16[4,4,3,256,256]{4,3,2,1,0:T(8,128)(2,1)S(1)}, u32[]{:S(2)}) copy-start(bf16[4,4,3,256,256]{4,3,2,1,0:T(8,128)(2,1)S(1)} %pairs.1.kern_hbm) | copy-start | bytes 18874372
  37.8 1.0 copy-start.2
  42.4 1.0 copy-start.6
  101.3 11.8 %copy-start.7 = (bf16[16,78,128]{2,1,0:T(8,128)(2,1)S(1)}, bf16[16,78,128]{2,1,0:T(8,128)(2,1)}, u32[]{:S(2)}) copy-start(bf16[16,78,128]{2,1,0:T(8,128)(2,1)} %get-tuple-element.22) | copy-start | bytes 958468
  101.3 24.3 %all-to-all-start.1 = ((bf16[128,24,128]{2,1,0:T(8,128)(2,1)}), bf16[128,24,128]{2,1,0:T(8,128)(2,1)S(1)}, u32[]{:S(2)}, u32[]{:S(2)}) async-start(bf16[128,24,128]{2,1,0:T(8,128)(2,1)} %get-tuple-element.21.after), calls=%async_computation.1 | async-start | bytes 1572864 | tf_op jit(solution)/shard_map/all_to_all | solution.py:566
  109.1 1.2 copy-start.3

commit v4 on v3

--- a/solution.py
+++ b/solution.py
@@ -249,7 +249,7 @@
 
 def main_kernel(
     recv, ct, wbig, gains, kern_hbm, wht, wl, fine, msg,
-    vup, hid, act, cv, hs_s, ds_s, back, gsum, kern, sem,
+    vup, hid_a, hid_b, act_a, act_b, act_c, cv, hs_s, ds_s, gsum, kern, sem,
 ):
     ri = lax.axis_index("row")
     ci = col_place()
@@ -267,7 +267,48 @@
         coef = col_weight(ext_col(m), j).astype(BF)
         vup[k] = dotf(coef, win)
 
-    def lift(g, _):
+    CK = 48
+    col_ok = []
+    for ck in range(3):
+        gc = ci * TC + ext_col(iota((CK, 1), 0) + ck * CK) - HC
+        col_ok.append(jnp.where((gc >= 0) & (gc < 8 * TC), 1.0, 0.0))
+
+    def put(act, y, ck, v):
+        act[y, 1 + 3 * ck : 4 + 3 * ck] = v.reshape(3, S, W)
+        if ck == 2:
+            act[y, 0] = pltpu.roll(v[32:48].astype(F32), 1, 0).astype(BF)
+        if ck == 0:
+            act[y, L + 1] = pltpu.roll(v[:16].astype(F32), S - 1, 0).astype(BF)
+
+    def lane_mean(v):
+        half = (v[:, :128] + v[:, 128:]).astype(F32)
+        return jnp.sum(half, axis=-1, keepdims=True) * (1.0 / W)
+
+    def over_lanes(v):
+        half = jnp.broadcast_to(v, (v.shape[0], 128)).astype(BF)
+        return jnp.concatenate([half, half], axis=1)
+
+    def activate(b, y, ck, before, after, act):
+        gr = ri * TR + y - HR
+        ok = jnp.where((gr >= 0) & (gr < 16 * TR), 1.0, 0.0)
+        gain = gains[pl.ds(jnp.minimum(b, BLOCKS - 1), 1), :].astype(BF)
+        keep = jnp.clip(y - 3, 0, 21)
+        sl = slice(ck * CK, (ck + 1) * CK)
+        h = cv[y, sl]
+        if before is not None:
+            h = h + before[y, sl]
+        after[y, sl] = h
+        s = over_lanes(lax.rsqrt(lane_mean(h * h) + 1e-06) * (col_ok[ck] * ok))
+        hs = h * s
+        n = hs * gain
+        half = BF(0.5)
+        g = half * jnp.tanh(half * n) + half
+        a = n * g
+        put(act, y, ck, a)
+        hs_s[b, keep, sl] = hs
+        ds_s[b, keep, sl] = (g + a - a * g) * (gain * s)
+
+    def lift(g):
         ups = []
         for k in range(4):
             n = 2 * (g * 4 + k) + 5
@@ -277,131 +318,113 @@
         up = jnp.concatenate(ups, axis=0)
         own = ct[pl.ds(g * 4, 4)].reshape(4 * EC, 128)
         r = dotf(jnp.concatenate([up, own], axis=1), wbig[...])
+        r = r.astype(BF)
         cv[pl.ds(g * 4, 4)] = r[:, :W].reshape(4, EC, W)
-        back[pl.ds(g * 4, 4)] = r[:, W:].reshape(4, EC, W)
-        return 0
-
-    lax.fori_loop(0, ER // 4, lift, 0)
-    hid[...] = jnp.zeros_like(hid)
-
-    CK = 48
-    col_ok = []
-    for ck in range(3):
-        gc = ci * TC + ext_col(iota((CK, 1), 0) + ck * CK) - HC
-        col_ok.append(jnp.where((gc >= 0) & (gc < 8 * TC), 1.0, 0.0))
-
-    def put(y, ck, v):
-        act[y, 1 + 3 * ck : 4 + 3 * ck] = v.astype(BF).reshape(3, S, W)
-        if ck == 2:
-            act[y, 0] = pltpu.roll(v[32:48], 1, 0).astype(BF)
-        if ck == 0:
-            act[y, L + 1] = pltpu.roll(v[:16], S - 1, 0).astype(BF)
-
-    def rows_of(lo, hi, f):
-        def two(i, _):
-            f(lo + 2 * i)
-            f(lo + 2 * i + 1)
+        for k in range(4):
+            for ck in range(3):
+                put(act_c, g * 4 + k, ck, r[k * EC + ck * CK : k * EC + (ck + 1) * CK, W:])
+
+    def start4(g):
+        for k in range(4):
+            for ck in range(3):
+                activate(0, g * 4 + k, ck, None, hid_a, act_a)
+
+    def lift_on(g, _):
+        start4(g - 1)
+        lift(jnp.minimum(g, ER // 4 - 1))
+        return 0
+
+    lift(jnp.int32(0))
+    lax.fori_loop(1, ER // 4 + 1, lift_on, 0)
+
+    def conv(b, act, y0, transpose, between=()):
+        between = list(between)
+        dims = NT if transpose else NN
+
+        def rows(k):
+            return jnp.concatenate([act[pl.ds(y0 - 1 + k + 2 * u, 1)] for u in range(4)], axis=0)
+
+        d0, d1, d2, d3 = rows(0), rows(1), rows(2), rows(3)
+        ms = []
+        for k, t in enumerate((d0 - d2, d1 + d2, d2 - d1, d1 - d3)):
+            acc = None
+            for q in range(3):
+                dx = 2 - q if transpose else q
+                kk = (3, 1, 2, 0)[k] if transpose else k
+                r = dotf(t[:, dx : dx + L].reshape(4 * EC, W), kern[b, kk, q], dims)
+                acc = r if acc is None else acc + r
+                for job in between[:2]:
+                    job()
+                between = between[2:]
+            ms.append(acc)
+        e = (ms[0] + ms[1] + ms[2]).reshape(4, EC, W)
+        o = (ms[1] - ms[2] - ms[3]).reshape(4, EC, W)
+        for u in range(4):
+            cv[y0 + 2 * u] = e[u].astype(BF)
+            cv[y0 + 2 * u + 1] = o[u].astype(BF)
+
+    def layer(b, lo, hi, act, transpose, after):
+        def place(i):
+            return jnp.minimum(lo + 8 * i, hi - 8)
+
+        def rest(i):
+            y0 = place(i)
+            return [functools.partial(after, y0 + k, ck) for k in range(8) for ck in range(3)]
+
+        def unit(i, _):
+            conv(b, act, place(i), transpose, rest(i - 1))
             return 0
 
-        lax.fori_loop(0, (hi - lo) >> 1, two, 0)
-
-    def resid(y, ck):
+        n = (hi - lo + 7) >> 3
+        conv(b, act, place(0), transpose)
+        lax.fori_loop(1, n, unit, 0)
+        for job in rest(n - 1):
+            job()
+
+    load.wait()
+
+    def forward(i, _):
+        for b, src, dst in ((2 * i, (hid_a, act_a), (hid_b, act_b)), (2 * i + 1, (hid_b, act_b), (hid_a, act_a))):
+            deep = b == 3
+            lo = jnp.where(deep, HR, b + 1)
+            hi = jnp.where(deep, HR + TR, ER - 1 - b)
+
+            def after(y, ck, b=b, src=src, dst=dst):
+                activate(b + 1, y, ck, src[0], *dst)
+
+            layer(b, lo, hi, src[1], False, after)
+        return 0
+
+    lax.fori_loop(0, 2, forward, 0)
+
+    perm = one_hot(ext_col(iota((EC, 128), 0)) - HC == iota((EC, 128), 1))
+
+    def head(g, _):
+        for k in range(4):
+            y = 4 * g + k
+            o = dotf(wht[...], hid_a[y + HR], NT).astype(BF)
+            fine[y] = dotf(o, perm).astype(BF)[:CIN]
+        return 0
+
+    lax.fori_loop(0, TR // 4, head, 0)
+
+    def grad(b, y, ck, before, act):
         sl = slice(ck * CK, (ck + 1) * CK)
-        h = (hid[y, sl].astype(F32) + cv[y, sl]).astype(BF)
-        hid[y, sl] = h
-        return h.astype(F32)
-
-    def activate(b, y):
-        gr = ri * TR + y - HR
-        ok = jnp.where((gr >= 0) & (gr < 16 * TR), 1.0, 0.0)
-        gain = gains[pl.ds(b, 1), :]
-        for ck in range(3):
-            sl = slice(ck * CK, (ck + 1) * CK)
-            h = resid(y, ck)
-            s = lax.rsqrt(jnp.mean(h * h, axis=-1, keepdims=True) + 1e-06) * (col_ok[ck] * ok)
-            hs = h * s
-            n = hs * gain
-            g = 0.5 * jnp.tanh(0.5 * n) + 0.5
-            a = n * g
-            put(y, ck, a)
-            hs_s[b, y, sl] = hs.astype(BF)
-            ds_s[b, y, sl] = ((g + a - a * g) * gain * s).astype(BF)
-
-    def conv(b, lo, hi, transpose):
-        dims = NT if transpose else NN
-
-        def unit(i, _):
-            y0 = jnp.minimum(lo + 8 * i, hi - 8)
-
-            def rows(k):
-                return jnp.concatenate([act[pl.ds(y0 - 1 + k + 2 * u, 1)] for u in range(4)], axis=0)
-
-            d0, d1, d2, d3 = rows(0), rows(1), rows(2), rows(3)
-            ms = []
-            for k, t in enumerate((d0 - d2, d1 + d2, d2 - d1, d1 - d3)):
-                acc = None
-                for q in range(3):
-                    dx = 2 - q if transpose else q
-                    kk = (3, 1, 2, 0)[k] if transpose else k
-                    r = dotf(t[:, dx : dx + L].reshape(4 * EC, W), kern[b, kk, q], dims)
-                    acc = r if acc is None else acc + r
-                ms.append(acc)
-            e = (ms[0] + ms[1] + ms[2]).reshape(4, EC, W)
-            o = (ms[1] - ms[2] - ms[3]).reshape(4, EC, W)
-            for u in range(4):
-                cv[y0 + 2 * u] = e[u]
-                cv[y0 + 2 * u + 1] = o[u]
-            return 0
-
-        lax.fori_loop(0, (hi - lo + 7) >> 3, unit, 0)
-
-    def forward(b, _):
-        deep = b == 3
-        rows_of(jnp.where(deep, 3, b), jnp.where(deep, ER - 3, ER - b), functools.partial(activate, b))
-        conv(b, jnp.where(deep, HR, b + 1), jnp.where(deep, HR + TR, ER - 1 - b), False)
-        return 0
-
-    load.wait()
-    lax.fori_loop(0, BLOCKS, forward, 0)
-
-    def last(y):
-        for ck in range(3):
-            resid(y, ck)
-
-    rows_of(HR, HR + TR, last)
-
-    perm = one_hot(ext_col(iota((EC, 128), 0)) - HC == iota((EC, 128), 1))
-
-    def head(y, _):
-        o = dotf(wht[...], hid[y + HR], NT).astype(BF)
-        fine[y] = dotf(o, perm).astype(BF)[:CIN]
-        return 0
-
-    lax.fori_loop(0, TR, head, 0)
-
-    def send4(y):
-        for ck in range(3):
-            put(y, ck, back[y, ck * CK : (ck + 1) * CK, :])
-
-    rows_of(2, ER - 2, send4)
-
-    def grad(b, y):
-        for ck in range(3):
-            sl = slice(ck * CK, (ck + 1) * CK)
-            u = cv[y, sl] * ds_s[b, y, sl].astype(F32)
-            hs = hs_s[b, y, sl].astype(F32)
-            mean = jnp.mean(u * hs, axis=-1, keepdims=True)
-            new = back[y, sl] + (u - hs * mean)
-            back[y, sl] = new
-            put(y, ck, new)
+        u = cv[y, sl] * ds_s[b, y - 3, sl]
+        hs = hs_s[b, y - 3, sl]
+        old = before[y, 1 + 3 * ck : 4 + 3 * ck].reshape(CK, W)
+        put(act, y, ck, old + (u - hs * over_lanes(lane_mean(u * hs))))
 
     def backward(i, _):
-        b = 3 - i
-        conv(b, HR - b, HR + TR + b, True)
-        rows_of(HR - b, HR + TR + b, functools.partial(grad, b))
-        return 0
-
-    lax.fori_loop(0, BLOCKS, backward, 0)
+        for b, src, dst in ((3 - 2 * i, act_c, act_a), (2 - 2 * i, act_a, act_c)):
+
+            def after(y, ck, b=b, src=src, dst=dst):
+                grad(b, y, ck, src, dst)
+
+            layer(b, HR - b, HR + TR + b, src, True, after)
+        return 0
+
+    lax.fori_loop(0, 2, backward, 0)
 
     e = ext_col(iota((32, EC), 1))
     qq = iota((32, EC), 0)
@@ -410,16 +433,18 @@
     cols_t = jnp.where(own, col_weight(e, j), 0.0).astype(BF)
     gsum[...] = jnp.zeros_like(gsum)
 
-    def gather(y, _):
-        t = dotf(cols_t, back[y + HR].astype(BF))
-        n = 2 * (y + HR) + 5
-        a = n >> 5
-        w = (n & 31).astype(F32) * (1.0 / 32.0)
-        gsum[a] = gsum[a] + (1.0 - w) * t
-        gsum[a + 1] = gsum[a + 1] + w * t
-        return 0
-
-    lax.fori_loop(0, TR, gather, 0)
+    def gather(g, _):
+        for k in range(4):
+            y = 4 * g + k + HR
+            t = dotf(cols_t, act_c[y, 1 : 1 + L].reshape(EC, W))
+            n = 2 * y + 5
+            a = n >> 5
+            w = (n & 31).astype(F32) * (1.0 / 32.0)
+            gsum[a] = gsum[a] + (1.0 - w) * t
+            gsum[a + 1] = gsum[a + 1] + w * t
+        return 0
+
+    lax.fori_loop(0, TR // 4, gather, 0)
     g = jnp.concatenate([gsum[0], gsum[1], gsum[2]], axis=1)
     g_hi = g.astype(BF)
     g_lo = (g - g_hi.astype(F32)).astype(BF)
@@ -445,11 +470,13 @@
         scratch_shapes=[
             pltpu.VMEM((3, EC, 128), F32),
             pltpu.VMEM((ER, EC, W), BF),
+            pltpu.VMEM((ER, EC, W), BF),
             pltpu.VMEM((ER, L + 2, S, W), BF),
-            pltpu.VMEM((ER, EC, W), F32),
-            pltpu.VMEM((BLOCKS, ER, EC, W), BF),
-            pltpu.VMEM((BLOCKS, ER, EC, W), BF),
-            pltpu.VMEM((ER, EC, W), F32),
+            pltpu.VMEM((ER, L + 2, S, W), BF),
+            pltpu.VMEM((ER, L + 2, S, W), BF),
+            pltpu.VMEM((ER, EC, W), BF),
+            pltpu.VMEM((BLOCKS + 1, ER - 6, EC, W), BF),
+            pltpu.VMEM((BLOCKS + 1, ER - 6, EC, W), BF),
             pltpu.VMEM((3, 32, W), F32),
             pltpu.VMEM((BLOCKS, 4, 3, W, W), BF),
             pltpu.SemaphoreType.DMA(()),

time: 128 us -> 113 us (0.88)
  Pallas kernels: 69.8 us -> 54.4 us
    pallas_call x1, Pallas kernels: 57.9 us -> 42.5 us  [main(): pl.pallas_call(main_kernel, out_shape=[jax.ShapeDtypeStruct((TR, CIN, TC)...]
  transfers between devices with their start and end apart: 6 -> 6, of which waited for: 3 -> 2; matrix products, arithmetic and copies ran while one was open for 3% -> 4% of each run, Pallas kernels for 8% -> 9%
where the time goes in v4:
time: 113 us; the launch traced here: 112 us
  Pallas kernels  54.4 us (48%)
  starting transfers between devices  24.7 us (22%)
  waiting for transfers between devices  15.3 us (14%)
  local copies, waits for them, and re-layouts  13.8 us (12%)
  between operations  2.35 us (2%)
  other arithmetic  1.55 us (1%)
    pallas_call x1, Pallas kernels, main(): pl.pallas_call(main_kernel, out_shape=[jax.ShapeDtypeStruct((TR, CIN, TC)...  42.5 us
    unnamed x25, local copies, waits for them, and re-layouts  12.2 us
    all_to_all x1, waiting for transfers between devices, shards(): back = lax.all_to_all(msg, ('sec', 'row', 'col'), 0, 0, tiled=True)  11.7 us
    all_to_all x1, starting transfers between devices, shards(): recv = lax.all_to_all(send, ('sec', 'row', 'col'), 0, 0, tiled=True)  11 us
    all_to_all x1, starting transfers between devices, shards(): back = lax.all_to_all(msg, ('sec', 'row', 'col'), 0, 0, tiled=True)  8.05 us
    all_to_all x1, waiting for transfers between devices, shards(): recv = lax.all_to_all(send, ('sec', 'row', 'col'), 0, 0, tiled=True)  3.58 us
    ppermute x1, starting transfers between devices, shards(): ra = lax.ppermute(pa, 'row', near)  3 us
    pallas_call x1, Pallas kernels, blank(): pl.pallas_call(blank_kernel, out_shape=jax.ShapeDtypeStruct((LAT_DEV, CIN...  2.75 us
  transfers between devices with their start and end apart: 6, of which 2 were waited for; matrix products, arithmetic and copies ran while one was open for 4% of the time, Pallas kernels for 9%

profile of v4, /device:TPU:0, one launch (start us, length us, event | category | flops | bytes accessed | tf_op | source)
XLA Modules:
  0.0 112.2 jit_solution(1010905752571198452)
XLA Ops:
  0.6 0.0 copy-start.9
  0.6 1.1 copy.13.cot
  1.7 0.0 copy-start.5
  1.7 0.7 copy-done.5
  2.4 0.1 own_rows.1
  2.6 0.0 copy-start.10
  2.6 0.7 collective-permute-start.1
  3.3 3.0 %collective-permute-start = (bf16[6,128,128]{2,1,0:T(8,128)(2,1)S(1)}, bf16[6,128,128]{2,1,0:T(8,128)(2,1)S(1)}, u32[]{:S(2)}, u32[]{:S(2)}) collective-permute-start(bf16[6,128,128]{2,1,0:T(8,128)(2,1)S(1)} %get-tuple-element.12.after), channel_id=1, source_target_pairs={{0,4},{4,0},{8,12},{12,8},{16,20},{20,16},{24,28},{28,24},{32,36},... | collective-permute-start | bytes 589832 | tf_op jit(solution)/shard_map/ppermute | solution.py:566
  7.6 0.0 copy-start.4
  7.6 1.5 %copy-done.4 = bf16[45,78,180]{2,1,0:T(8,128)(2,1)S(1)} copy-done((bf16[45,78,180]{2,1,0:T(8,128)(2,1)S(1)}, bf16[45,78,180]{2,1,0:T(8,128)(2,1)}, u32[]{:S(2)}) %copy-start.4) | copy-done | bytes 1263624
  9.1 0.0 copy-start.8
  9.1 2.7 %pack.1 = bf16[128,32,128]{2,1,0:T(8,128)(2,1)} custom-call(s32[1]{0:T(128)S(6)} %copy.24.ro, s32[1]{0:T(128)S(6)} %copy.25.co, bf16[45,78,180]{2,1,0:T(8,128)(2,1)S(1)} %copy-done.4, bf16[6,128,128]{2,1,0:T(8,128)(2,1)S(1)} %get-tuple-element.12.after), custom_call_target="tpu_custom_call" | custom-call | bytes 8388608 | tf_op jit(solution)/shard_map/pack/pallas_call | solution.py:128
  11.8 0.0 collective-permute-done.1.rb
  11.8 0.0 collective-permute-done.ra
  11.8 0.3 edges.1
  12.2 11.0 %all-to-all-start = ((bf16[128,32,128]{2,1,0:T(8,128)(2,1)}), bf16[128,32,128]{2,1,0:T(8,128)(2,1)S(1)}, u32[]{:S(2)}, u32[]{:S(2)}) async-start(bf16[128,32,128]{2,1,0:T(8,128)(2,1)} %pack.1), calls=%async_computation | async-start | bytes 2097152 | tf_op jit(solution)/shard_map/all_to_all | solution.py:575
  23.2 0.0 copy-done.9
  23.2 0.1 copy.14
  23.3 0.5 fusion
  23.9 0.0 copy-done.10
  23.9 0.4 concatenate.18
  24.3 0.8 pad_maximum_fusion.wl
  25.1 1.1 collective-permute-start.2
  26.2 0.8 collective-permute-start.3
  27.1 0.0 copy-done.8
  27.1 0.7 maximum_maximum_fusion.wbig
  27.8 0.6 concatenate.21.wht
  28.4 0.0 copy-start.1
  28.4 2.3 %copy-done.1 = bf16[4,3,3,256,256]{4,3,2,1,0:T(8,128)(2,1)S(1)} copy-done((bf16[4,3,3,256,256]{4,3,2,1,0:T(8,128)(2,1)S(1)}, bf16[4,3,3,256,256]{4,3,2,1,0:T(8,128)(2,1)}, u32[]{:S(2)}) %copy-start.1) | copy-done | bytes 4718616
  30.8 2.5 %pairs.1.kern_hbm = bf16[4,4,3,256,256]{4,3,2,1,0:T(8,128)(2,1)S(1)} custom-call(bf16[4,3,3,256,256]{4,3,2,1,0:T(8,128)(2,1)S(1)} %copy-done.1), custom_call_target="tpu_custom_call" | custom-call | bytes 12582912 | tf_op jit(solution)/shard_map/pairs/pallas_call | solution.py:238
  33.2 0.0 copy-start
  33.3 2.6 %copy-done = bf16[4,4,3,256,256]{4,3,2,1,0:T(8,128)(2,1)} copy-done((bf16[4,4,3,256,256]{4,3,2,1,0:T(8,128)(2,1)}, bf16[4,4,3,256,256]{4,3,2,1,0:T(8,128)(2,1)S(1)}, u32[]{:S(2)}) %copy-start) | copy-done | bytes 6291480
  35.9 0.0 collective-permute-done.2.rc
  35.9 0.0 collective-permute-done.3.rd
  36.0 1.9 %cells.1.ct = bf16[28,144,128]{2,1,0:T(8,128)(2,1)S(1)} custom-call(bf16[16,128,128]{2,1,0:T(8,128)(2,1)S(1)} %get-tuple-element.13.xown, bf16[6,128,128]{2,1,0:T(8,128)(2,1)S(1)} %collective-permute-done.ra, bf16[6,128,128]{2,1,0:T(8,128)(2,1)S(1)} %collective-permute-done.1.rb, bf16[224,128]{1,0:T(8,128)(2,1)S(1)} %collective-permute-done.2.rc, ...), custom_call_target="tpu_custom_call" | custom-call | bytes 8388608 | tf_op jit(solution)/shard_map/cells/pallas_call | solution.py:218
  37.8 0.0 copy-start.2
  37.9 1.0 copy-done.2
  38.8 3.6 %all-to-all-done.recv = bf16[128,32,128]{2,1,0:T(8,128)(2,1)S(1)} async-done(((bf16[128,32,128]{2,1,0:T(8,128)(2,1)}), bf16[128,32,128]{2,1,0:T(8,128)(2,1)S(1)}, u32[]{:S(2)}, u32[]{:S(2)}) %all-to-all-start) | async-done | bytes 1048608 | tf_op jit(solution)/shard_map/all_to_all | solution.py:575
  42.4 0.0 copy-start.6
  42.4 1.0 copy-done.6
  43.4 42.5 %main.1 = (bf16[16,78,128]{2,1,0:T(8,128)(2,1)}, bf16[128,24,128]{2,1,0:T(8,128)(2,1)}) custom-call(bf16[128,32,128]{2,1,0:T(8,128)(2,1)} %copy-done.6, bf16[28,144,128]{2,1,0:T(8,128)(2,1)} %copy-done.2, bf16[256,512]{1,0:T(8,128)(2,1)} %maximum_maximum_fusion.wbig, f32[4,256]{1,0:T(4,128)} %gains.1, bf16[4,4,3,256,256]{4,3,2,1,0:T(8,128)(2,1)} %copy-done, ...), custom_call_target="tpu_custom_call" | custom-call | tf_op jit(solution)/shard_map/main/pallas_call | solution.py:462
  85.9 0.0 copy-start.7
  85.9 8.0 %all-to-all-start.1 = ((bf16[128,24,128]{2,1,0:T(8,128)(2,1)}), bf16[128,24,128]{2,1,0:T(8,128)(2,1)S(1)}, u32[]{:S(2)}, u32[]{:S(2)}) async-start(bf16[128,24,128]{2,1,0:T(8,128)(2,1)} %get-tuple-element.21.after), calls=%async_computation.1 | async-start | bytes 1572864 | tf_op jit(solution)/shard_map/all_to_all | solution.py:593
  94.0 0.0 copy-start.3
  94.0 1.2 %copy-done.3 = bf16[128,24,128]{2,1,0:T(8,128)(2,1)S(1)} copy-done((bf16[128,24,128]{2,1,0:T(8,128)(2,1)S(1)}, bf16[128,24,128]{2,1,0:T(8,128)(2,1)}, u32[]{:S(2)}) %copy-start.3) | copy-done | bytes 786456
  95.1 2.7 %blank.1.zero = f32[45,78,180]{2,1,0:T(8,128)} custom-call(bf16[128,24,128]{2,1,0:T(8,128)(2,1)S(1)} %copy-done.3), custom_call_target="tpu_custom_call" | custom-call | bytes 4194304 | tf_op jit(solution)/shard_map/blank/pallas_call | solution.py:494
  97.9 0.0 copy-done.7
  97.9 0.8 copy.15
  98.7 11.7 %all-to-all-done.1 = bf16[128,24,128]{2,1,0:T(8,128)(2,1)S(1)} async-done(((bf16[128,24,128]{2,1,0:T(8,128)(2,1)}), bf16[128,24,128]{2,1,0:T(8,128)(2,1)S(1)}, u32[]{:S(2)}, u32[]{:S(2)}) %all-to-all-start.1) | async-done | bytes 786464 | tf_op jit(solution)/shard_map/all_to_all | solution.py:593
  110.4 1.6 %place.1 = f32[45,78,180]{2,1,0:T(8,128)} custom-call(s32[1]{0:T(128)S(6)} %copy.24.ro, s32[1]{0:T(128)S(6)} %copy.25.co, bf16[2,16,4,24,128]{4,3,2,1,0:T(8,128)(2,1)S(1)} %bitcast.14, f32[45,78,180]{2,1,0:T(8,128)} %blank.1.zero), custom_call_target="tpu_custom_call", output_to_operand_aliasing={{}: (3, {})} | custom-call | tf_op jit(solution)/shard_map/place/pallas_call | solution.py:550
  (7 shorter events, 0.1 us)
Async XLA Ops:
  0.6 22.6 %copy-start.9 = (bf16[78,256]{1,0:T(8,128)(2,1)S(1)}, bf16[78,256]{1,0:T(8,128)(2,1)}, u32[]{:S(2)}) copy-start(bf16[78,256]{1,0:T(8,128)(2,1)} %param.14) | copy-start | bytes 119812
  1.7 0.7 copy-start.5
  2.6 21.3 %copy-start.10 = (bf16[4,256]{1,0:T(4,128)(2,1)S(1)}, bf16[4,256]{1,0:T(4,128)(2,1)}, u32[]{:S(2)}) copy-start(bf16[4,256]{1,0:T(4,128)(2,1)} %param.15) | copy-start | bytes 6148
  2.6 9.2 %collective-permute-start.1 = (bf16[6,128,128]{2,1,0:T(8,128)(2,1)S(1)}, bf16[6,128,128]{2,1,0:T(8,128)(2,1)S(1)}, u32[]{:S(2)}, u32[]{:S(2)}) collective-permute-start(bf16[6,128,128]{2,1,0:T(8,128)(2,1)S(1)} %get-tuple-element.14), channel_id=1, source_target_pairs={{4,8},{8,4},{12,16},{16,12},{20,24},{24,20},{28,32},{32,28},{36,40... | collective-permute-start | bytes 589832 | tf_op jit(solution)/shard_map/ppermute | solution.py:567
  3.3 8.6 %collective-permute-start = (bf16[6,128,128]{2,1,0:T(8,128)(2,1)S(1)}, bf16[6,128,128]{2,1,0:T(8,128)(2,1)S(1)}, u32[]{:S(2)}, u32[]{:S(2)}) collective-permute-start(bf16[6,128,128]{2,1,0:T(8,128)(2,1)S(1)} %get-tuple-element.12.after), channel_id=1, source_target_pairs={{0,4},{4,0},{8,12},{12,8},{16,20},{20,16},{24,28},{28,24},{32,36},... | collective-permute-start | bytes 589832 | tf_op jit(solution)/shard_map/ppermute | solution.py:566
  7.6 1.5 %copy-start.4 = (bf16[45,78,180]{2,1,0:T(8,128)(2,1)S(1)}, bf16[45,78,180]{2,1,0:T(8,128)(2,1)}, u32[]{:S(2)}) copy-start(bf16[45,78,180]{2,1,0:T(8,128)(2,1)} %coarse.1) | copy-start | bytes 3790804
  9.1 18.0 %copy-start.8 = (bf16[256,78]{0,1:T(8,128)(2,1)S(1)}, bf16[256,78]{0,1:T(8,128)(2,1)}, u32[]{:S(2)}) copy-start(bf16[256,78]{0,1:T(8,128)(2,1)} %param.18) | copy-start | bytes 119812
  12.2 30.2 %all-to-all-start = ((bf16[128,32,128]{2,1,0:T(8,128)(2,1)}), bf16[128,32,128]{2,1,0:T(8,128)(2,1)S(1)}, u32[]{:S(2)}, u32[]{:S(2)}) async-start(bf16[128,32,128]{2,1,0:T(8,128)(2,1)} %pack.1), calls=%async_computation | async-start | bytes 2097152 | tf_op jit(solution)/shard_map/all_to_all | solution.py:575
  25.1 10.8 %collective-permute-start.2 = (bf16[224,128]{1,0:T(8,128)(2,1)S(1)}, bf16[224,128]{1,0:T(8,128)(2,1)S(1)}, u32[]{:S(2)}, u32[]{:S(2)}) collective-permute-start(bf16[224,128]{1,0:T(8,128)(2,1)S(1)} %get-tuple-element.18), channel_id=1, source_target_pairs={{0,1},{1,0},{2,3},{3,2},{64,65},{65,64},{66,67},{67,66},{4,5},{5,4... | collective-permute-start | bytes 172040 | tf_op jit(solution)/shard_map/ppermute | solution.py:573
  26.2 9.7 %collective-permute-start.3 = (bf16[224,128]{1,0:T(8,128)(2,1)S(1)}, bf16[224,128]{1,0:T(8,128)(2,1)S(1)}, u32[]{:S(2)}, u32[]{:S(2)}) collective-permute-start(bf16[224,128]{1,0:T(8,128)(2,1)S(1)} %get-tuple-element.19), channel_id=1, source_target_pairs={{1,2},{2,1},{3,64},{64,3},{65,66},{66,65},{5,6},{6,5},{7,68},{68,7... | collective-permute-start | bytes 172040 | tf_op jit(solution)/shard_map/ppermute | solution.py:574
  28.4 2.3 %copy-start.1 = (bf16[4,3,3,256,256]{4,3,2,1,0:T(8,128)(2,1)S(1)}, bf16[4,3,3,256,256]{4,3,2,1,0:T(8,128)(2,1)}, u32[]{:S(2)}) copy-start(bf16[4,3,3,256,256]{4,3,2,1,0:T(8,128)(2,1)} %kern.1) | copy-start | bytes 14155780
  33.2 2.7 %copy-start = (bf16[4,4,3,256,256]{4,3,2,1,0:T(8,128)(2,1)}, bf16[4,4,3,256,256]{4,3,2,1,0:T(8,128)(2,1)S(1)}, u32[]{:S(2)}) copy-start(bf16[4,4,3,256,256]{4,3,2,1,0:T(8,128)(2,1)S(1)} %pairs.1.kern_hbm) | copy-start | bytes 18874372
  37.8 1.0 copy-start.2
  42.4 1.0 copy-start.6
  85.9 12.0 %copy-start.7 = (bf16[16,78,128]{2,1,0:T(8,128)(2,1)S(1)}, bf16[16,78,128]{2,1,0:T(8,128)(2,1)}, u32[]{:S(2)}) copy-start(bf16[16,78,128]{2,1,0:T(8,128)(2,1)} %get-tuple-element.22) | copy-start | bytes 958468
  85.9 24.5 %all-to-all-start.1 = ((bf16[128,24,128]{2,1,0:T(8,128)(2,1)}), bf16[128,24,128]{2,1,0:T(8,128)(2,1)S(1)}, u32[]{:S(2)}, u32[]{:S(2)}) async-start(bf16[128,24,128]{2,1,0:T(8,128)(2,1)} %get-tuple-element.21.after), calls=%async_computation.1 | async-start | bytes 1572864 | tf_op jit(solution)/shard_map/all_to_all | solution.py:593
  94.0 1.2 %copy-start.3 = (bf16[128,24,128]{2,1,0:T(8,128)(2,1)S(1)}, bf16[128,24,128]{2,1,0:T(8,128)(2,1)}, u32[]{:S(2)}) copy-start(bf16[128,24,128]{2,1,0:T(8,128)(2,1)} %get-tuple-element.21.after) | copy-start | bytes 2359300

commit v5 on v4

--- a/solution.py
+++ b/solution.py
@@ -91,15 +91,13 @@
     start = jnp.clip(first_row, 0, LAT_DEV - 18)
     copy = pltpu.make_async_copy(coarse.at[pl.ds(start, 18)], xs, sem)
     copy.start()
-    lj = iota((272, LON_DEV), 1)
-    q = iota((272, LON_DEV), 0)
+    lj = iota((144, LON_DEV), 1)
+    q = iota((144, LON_DEV), 0)
     tail = q - 80
-    k = tail >> 6
-    c = (tail & 63) >> 3
-    s = (tail & 7) - 2 * k
-    j_tail = jnp.where((s >= 0) & (s < 2), 8 * c + 8 + s, -100000)
+    j_tail = jnp.where((tail & 7) < 4, 8 * (tail >> 3) + 8 + (tail & 1), -100000)
     j = jnp.where(q < 80, jnp.where(q < 66, q, -100000), j_tail)
     sel = one_hot(lj == off + j)
+    prod[...] = jnp.zeros_like(prod)
     copy.wait()
 
     def rows(g, _):
@@ -111,14 +109,24 @@
         return 0
 
     lax.fori_loop(0, 3, rows, 0)
+    lane = iota((144, 128), 1)
+    is_0 = lane < 40
+    is_1 = lane < 80
+    low = iota((64, 128), 0)
+    low = (low & 7) < 2
 
     def dest(r, _):
-        tails = prod[r, 80:144] + prod[r + 1, 144:208] + prod[r + 2, 208:272]
+        p0 = prod[r]
+        p1 = prod[r + 1]
+        p2 = prod[r + 2]
+        up = pltpu.roll(p1, 40, 1)
+        m0 = jnp.where(is_0, p0, jnp.where(is_1, up, pltpu.roll(p2, 80, 1)))
+        m1 = jnp.where(is_0, pltpu.roll(p0, 88, 1), jnp.where(is_1, p1, pltpu.roll(p2, 40, 1)))
+        tails = jnp.where(low, m0[80:], m1[80:])
         for cc in range(8):
             d = (cc // 4) * 64 + r * 4 + cc % 4
             sl = slice(8 * cc, 8 * cc + 8)
-            msg = jnp.concatenate([prod[r, sl], prod[r + 1, sl], prod[r + 2, sl], tails[sl]], axis=0)
-            send[d] = msg.astype(BF)
+            send[d] = jnp.concatenate([m0[sl], m1[sl], tails[sl]], axis=0).astype(BF)
         return 0
 
     lax.fori_loop(0, 16, dest, 0)
@@ -127,12 +135,12 @@
 def pack(ro, co, coarse, after):
     return pl.pallas_call(
         pack_kernel,
-        out_shape=jax.ShapeDtypeStruct((128, 32, 128), BF),
+        out_shape=jax.ShapeDtypeStruct((128, 24, 128), BF),
         in_specs=[SM, SM, pl.BlockSpec(memory_space=pltpu.HBM), pl.BlockSpec(memory_space=pl.ANY)],
         out_specs=VM,
         scratch_shapes=[
             pltpu.VMEM((18, CIN, LON_DEV), BF),
-            pltpu.VMEM((18, 272, 128), F32),
+            pltpu.VMEM((18, 144, 128), F32),
             pltpu.SemaphoreType.DMA(()),
         ],
         cost_estimate=pl.CostEstimate(flops=0, bytes_accessed=8 * MB, transcendentals=0),
@@ -226,46 +234,28 @@
     )(xown, ra, rb, rc, rd)
 
 
-def pairs_kernel(kern, out):
-    k0, k1, k2 = (kern[p].astype(F32) for p in range(3))
-    out[0] = kern[0]
-    out[1] = (0.5 * (k0 + k1 + k2)).astype(BF)
-    out[2] = (0.5 * (k0 - k1 + k2)).astype(BF)
-    out[3] = kern[2]
-
-
-def pairs(kern):
-    return pl.pallas_call(
-        pairs_kernel,
-        out_shape=jax.ShapeDtypeStruct((BLOCKS, 4, 3, W, W), BF),
-        grid=(BLOCKS, 3),
-        in_specs=[pl.BlockSpec((None, 3, None, W, W), lambda b, q: (b, 0, q, 0, 0))],
-        out_specs=pl.BlockSpec((None, 4, None, W, W), lambda b, q: (b, 0, q, 0, 0)),
-        cost_estimate=pl.CostEstimate(flops=0, bytes_accessed=12 * MB, transcendentals=0),
-        compiler_params=pltpu.CompilerParams(vmem_limit_bytes=8 * MB),
-        name="pairs",
-    )(kern)
-
-
 def main_kernel(
-    recv, ct, wbig, gains, kern_hbm, wht, wl, fine, msg,
-    vup, hid_a, hid_b, act_a, act_b, act_c, cv, hs_s, ds_s, gsum, kern, sem,
+    recv, ct, wbig, gains, kern_hbm, wl, deep_out, msg,
+    vup, hid_a, hid_b, act_a, act_b, act_c, cv, hs_s, ds_s, gsum, kern, pair, sem,
 ):
     ri = lax.axis_index("row")
     ci = col_place()
-    load = pltpu.make_async_copy(kern_hbm, kern, sem)
+    load = pltpu.make_async_copy(kern_hbm, kern, sem.at[0])
     load.start()
 
     win = jnp.sum(recv[...].astype(F32), axis=0)
-    win = jnp.where(iota((32, 128), 1) < CIN, win, 0.0).astype(BF)
-    m = iota((EC, 32), 0)
-    q = iota((EC, 32), 1)
+    m = iota((EC, 48), 0)
+    q = iota((EC, 48), 1)
+    j0 = jnp.where(q < 8, q, jnp.where((q == 16) | (q == 17), q - 8, -10))
+    q1 = q - 24
+    j1 = jnp.where((q1 >= 8) & (q1 < 16), q1 - 8, jnp.where((q1 == 18) | (q1 == 19), q1 - 10, -10))
+    coef = col_weight(ext_col(m), jnp.where(q < 24, j0, j1)).astype(BF)
+    lane = iota((24, 128), 1)
     for k in range(3):
-        tail = q - 24 - 2 * k
-        j = jnp.where((q >= 8 * k) & (q < 8 * k + 8), q - 8 * k, -10)
-        j = jnp.where((tail >= 0) & (tail < 2), tail + 8, j)
-        coef = col_weight(ext_col(m), j).astype(BF)
-        vup[k] = dotf(coef, win)
+        w0 = jnp.where(lane < 40, pltpu.roll(win, (128 - 40 * k) % 128, 1) if k else win, 0.0)
+        w1 = pltpu.roll(win, (168 - 40 * k) % 128, 1) if k != 1 else win
+        w1 = jnp.where((lane >= 40) & (lane < CIN), w1, 0.0)
+        vup[k] = dotf(coef, jnp.concatenate([w0, w1], axis=0).astype(BF))
 
     CK = 48
     col_ok = []
@@ -329,12 +319,27 @@
             for ck in range(3):
                 activate(0, g * 4 + k, ck, None, hid_a, act_a)
 
+    def pair_kernels(i):
+        i = jnp.minimum(i, 3 * BLOCKS - 1)
+        b = i // 3
+        q = i - 3 * b
+        for c in range(0, W, 64):
+            sl = slice(c, c + 64)
+            k0, k1, k2 = (kern[b, p, q, sl].astype(F32) for p in range(3))
+            both = 0.5 * (k0 + k2)
+            mid = 0.5 * k1
+            pair[b, 0, q, sl] = (both + mid).astype(BF)
+            pair[b, 1, q, sl] = (both - mid).astype(BF)
+
     def lift_on(g, _):
         start4(g - 1)
         lift(jnp.minimum(g, ER // 4 - 1))
+        pair_kernels(2 * g - 2)
+        pair_kernels(2 * g - 1)
         return 0
 
     lift(jnp.int32(0))
+    load.wait()
     lax.fori_loop(1, ER // 4 + 1, lift_on, 0)
 
     def conv(b, act, y0, transpose, between=()):
@@ -350,8 +355,11 @@
             acc = None
             for q in range(3):
                 dx = 2 - q if transpose else q
-                kk = (3, 1, 2, 0)[k] if transpose else k
-                r = dotf(t[:, dx : dx + L].reshape(4 * EC, W), kern[b, kk, q], dims)
+                if k == 1 or k == 2:
+                    kk = pair[b, k - 1, q]
+                else:
+                    kk = kern[b, 0 if (k == 3) == transpose else 2, q]
+                r = dotf(t[:, dx : dx + L].reshape(4 * EC, W), kk, dims)
                 acc = r if acc is None else acc + r
                 for job in between[:2]:
                     job()
@@ -381,8 +389,6 @@
         for job in rest(n - 1):
             job()
 
-    load.wait()
-
     def forward(i, _):
         for b, src, dst in ((2 * i, (hid_a, act_a), (hid_b, act_b)), (2 * i + 1, (hid_b, act_b), (hid_a, act_a))):
             deep = b == 3
@@ -397,16 +403,8 @@
 
     lax.fori_loop(0, 2, forward, 0)
 
-    perm = one_hot(ext_col(iota((EC, 128), 0)) - HC == iota((EC, 128), 1))
-
-    def head(g, _):
-        for k in range(4):
-            y = 4 * g + k
-            o = dotf(wht[...], hid_a[y + HR], NT).astype(BF)
-            fine[y] = dotf(o, perm).astype(BF)[:CIN]
-        return 0
-
-    lax.fori_loop(0, TR // 4, head, 0)
+    save = pltpu.make_async_copy(hid_a.at[pl.ds(HR, TR)], deep_out, sem.at[1])
+    save.start()
 
     def grad(b, y, ck, before, act):
         sl = slice(ck * CK, (ck + 1) * CK)
@@ -452,21 +450,23 @@
     o = jnp.where(iota((32, 128), 0) < 10, o[:, :128], o[:, 128:]).astype(BF)[:24]
 
     def spread(d, _):
-        msg[d] = o
-        return 0
-
-    lax.fori_loop(0, 128, spread, 0)
-
-
-def main(recv, ct, wbig, gains, kern, wht, wl):
+        for k in range(8):
+            msg[8 * d + k] = o
+        return 0
+
+    lax.fori_loop(0, 16, spread, 0)
+    save.wait()
+
+
+def main(recv, ct, wbig, gains, kern, wl):
     return pl.pallas_call(
         main_kernel,
         out_shape=[
-            jax.ShapeDtypeStruct((TR, CIN, TC), BF),
+            jax.ShapeDtypeStruct((TR, EC, W), BF),
             jax.ShapeDtypeStruct((128, 24, 128), BF),
         ],
-        in_specs=[VM] * 4 + [pl.BlockSpec(memory_space=pltpu.HBM)] + [VM] * 2,
-        out_specs=[VM] * 2,
+        in_specs=[VM] * 4 + [pl.BlockSpec(memory_space=pl.ANY), VM],
+        out_specs=[pl.BlockSpec(memory_space=pltpu.HBM), VM],
         scratch_shapes=[
             pltpu.VMEM((3, EC, 128), F32),
             pltpu.VMEM((ER, EC, W), BF),
@@ -478,12 +478,34 @@
             pltpu.VMEM((BLOCKS + 1, ER - 6, EC, W), BF),
             pltpu.VMEM((BLOCKS + 1, ER - 6, EC, W), BF),
             pltpu.VMEM((3, 32, W), F32),
-            pltpu.VMEM((BLOCKS, 4, 3, W, W), BF),
-            pltpu.SemaphoreType.DMA(()),
+            pltpu.VMEM((BLOCKS, 3, 3, W, W), BF),
+            pltpu.VMEM((BLOCKS, 2, 3, W, W), BF),
+            pltpu.SemaphoreType.DMA((2,)),
         ],
-        compiler_params=pltpu.CompilerParams(vmem_limit_bytes=58 * MB),
+        compiler_params=pltpu.CompilerParams(vmem_limit_bytes=48 * MB),
         name="main",
-    )(recv, ct, wbig, gains, kern, wht, wl)
+    )(recv, ct, wbig, gains, kern, wl)
+
+
+def head_kernel(hid, wht, after, fine, mixed):
+    perm = one_hot(ext_col(iota((EC, TC), 0)) - HC == iota((EC, TC), 1))
+    for y in range(TR):
+        mixed[y] = dotf(wht[...], hid[y], NT).astype(BF)
+    out = dotf(mixed[...].reshape(TR * 80, EC), perm).astype(BF).reshape(TR, 80, TC)
+    fine[...] = out[:, :CIN]
+
+
+def head(hid, wht, after):
+    return pl.pallas_call(
+        head_kernel,
+        out_shape=jax.ShapeDtypeStruct((TR, CIN, TC), BF),
+        in_specs=[VM, VM, pl.BlockSpec(memory_space=pl.ANY)],
+        out_specs=VM,
+        scratch_shapes=[pltpu.VMEM((TR, 80, EC), BF)],
+        cost_estimate=pl.CostEstimate(flops=0, bytes_accessed=6 * MB, transcendentals=0),
+        compiler_params=pltpu.CompilerParams(vmem_limit_bytes=8 * MB),
+        name="head",
+    )(hid, wht, after)
 
 
 def blank_kernel(after, out):
@@ -589,9 +611,9 @@
     wl = jnp.concatenate(
         [jnp.pad(wl, ((0, 0), (0, 0), (40 * k, 88 - 40 * k))).reshape(W, 256) for k in range(3)], 0
     )
-    fine, msg = main(recv, ct, wbig, gains, pairs(kern), wht80, wl)
+    deep, msg = main(recv, ct, wbig, gains, kern, wl)
     back = lax.all_to_all(msg, ("sec", "row", "col"), 0, 0, tiled=True)
-    return fine, place(ro, co, back.reshape(2, 16, 4, 24, 128), blank(msg))
+    return head(deep, wht80, msg), place(ro, co, back.reshape(2, 16, 4, 24, 128), blank(msg))
 
 
 def solution(mesh):

time: 113 us -> 108 us (0.956)
  waiting for transfers between devices: 15.3 us -> 23.5 us
  local copies, waits for them, and re-layouts: 13.8 us -> 6.2 us
  Pallas kernels: 54.4 us -> 51.8 us
  other arithmetic: 1.55 us -> 0.05 us
  starting transfers between devices: 24.7 us -> 23.3 us
    unnamed x25 -> x19, local copies, waits for them, and re-layouts: 12.2 us -> 5.17 us
    ppermute x1, waiting for transfers between devices: 0.05 us -> 6.37 us  [shards(): rc = lax.ppermute(pc, ('sec', 'col'), near)]
    pallas_call x3, Pallas kernels: 47.7 us -> 45.1 us  [the longest x1 40.6 us: main(): pl.pallas_call(main_kernel, out_shape=[jax.ShapeDtypeStruct((TR, EC, W),...]
    all_to_all x1, waiting for transfers between devices: 3.58 us -> 4.95 us  [shards(): recv = lax.all_to_all(send, ('sec', 'row', 'col'), 0, 0, tiled=True)]
    all_to_all x1, starting transfers between devices: 8.05 us -> 6.73 us  [shards(): back = lax.all_to_all(msg, ('sec', 'row', 'col'), 0, 0, tiled=True)]
  transfers between devices with their start and end apart: 6 -> 6, of which waited for: 2 -> 3; matrix products, arithmetic and copies ran while one was open for 4% -> 2% of each run, Pallas kernels for 9% -> 9%
where the time goes in v5:
time: 108 us; the launch traced here: 107 us
  Pallas kernels  51.8 us (48%)
  waiting for transfers between devices  23.5 us (22%)
  starting transfers between devices  23.3 us (22%)
  local copies, waits for them, and re-layouts  6.2 us (6%)
  between operations  2.34 us (2%)
    pallas_call x1, Pallas kernels, main(): pl.pallas_call(main_kernel, out_shape=[jax.ShapeDtypeStruct((TR, EC, W),...  40.6 us
    all_to_all x1, waiting for transfers between devices, shards(): back = lax.all_to_all(msg, ('sec', 'row', 'col'), 0, 0, tiled=True)  12.1 us
    all_to_all x1, starting transfers between devices, shards(): recv = lax.all_to_all(send, ('sec', 'row', 'col'), 0, 0, tiled=True)  10.9 us
    all_to_all x1, starting transfers between devices, shards(): back = lax.all_to_all(msg, ('sec', 'row', 'col'), 0, 0, tiled=True)  6.73 us
    ppermute x1, waiting for transfers between devices, shards(): rc = lax.ppermute(pc, ('sec', 'col'), near)  6.37 us
    unnamed x19, local copies, waits for them, and re-layouts  5.17 us
    all_to_all x1, waiting for transfers between devices, shards(): recv = lax.all_to_all(send, ('sec', 'row', 'col'), 0, 0, tiled=True)  4.95 us
    pallas_call x1, Pallas kernels, pack(): pl.pallas_call(pack_kernel, out_shape=jax.ShapeDtypeStruct((128, 24, 128)...  3.76 us
  transfers between devices with their start and end apart: 6, of which 3 were waited for; matrix products, arithmetic and copies ran while one was open for 2% of the time, Pallas kernels for 9%

profile of v5, /device:TPU:0, one launch (start us, length us, event | category | flops | bytes accessed | tf_op | source)
XLA Modules:
  0.0 107.1 jit_solution(5552166431990285131)
XLA Ops:
  0.6 0.0 copy-start.6
  0.6 0.0 copy-start.7
  0.7 1.1 copy.13.cot
  1.7 0.0 copy-start.3
  1.7 0.7 copy-done.3
  2.4 0.1 own_rows.1
  2.6 0.7 collective-permute-start.1
  3.3 3.0 %collective-permute-start = (bf16[6,128,128]{2,1,0:T(8,128)(2,1)S(1)}, bf16[6,128,128]{2,1,0:T(8,128)(2,1)S(1)}, u32[]{:S(2)}, u32[]{:S(2)}) collective-permute-start(bf16[6,128,128]{2,1,0:T(8,128)(2,1)S(1)} %get-tuple-element.12.after), channel_id=1, source_target_pairs={{0,4},{4,0},{8,12},{12,8},{16,20},{20,16},{24,28},{28,24},{32,36},... | collective-permute-start | bytes 589832 | tf_op jit(solution)/shard_map/ppermute | solution.py:588
  7.6 0.0 copy-start
  7.6 1.5 %copy-done = bf16[45,78,180]{2,1,0:T(8,128)(2,1)S(1)} copy-done((bf16[45,78,180]{2,1,0:T(8,128)(2,1)S(1)}, bf16[45,78,180]{2,1,0:T(8,128)(2,1)}, u32[]{:S(2)}) %copy-start) | copy-done | bytes 1263624
  9.1 0.0 copy-start.5
  9.1 3.8 %pack.1 = bf16[128,24,128]{2,1,0:T(8,128)(2,1)} custom-call(s32[1]{0:T(128)S(6)} %copy.24.ro, s32[1]{0:T(128)S(6)} %copy.25.co, bf16[45,78,180]{2,1,0:T(8,128)(2,1)S(1)} %copy-done, bf16[6,128,128]{2,1,0:T(8,128)(2,1)S(1)} %get-tuple-element.12.after), custom_call_target="tpu_custom_call" | custom-call | bytes 8388608 | tf_op jit(solution)/shard_map/pack/pallas_call | solution.py:136
  12.8 0.0 collective-permute-done.1.rb
  12.8 0.0 collective-permute-done.ra
  12.9 0.3 edges.1
  13.2 0.0 copy-start.4
  13.2 10.9 %all-to-all-start = ((bf16[128,24,128]{2,1,0:T(8,128)(2,1)}), bf16[128,24,128]{2,1,0:T(8,128)(2,1)S(1)}, u32[]{:S(2)}, u32[]{:S(2)}) async-start(bf16[128,24,128]{2,1,0:T(8,128)(2,1)} %pack.1), calls=%async_computation | async-start | bytes 1572864 | tf_op jit(solution)/shard_map/all_to_all | solution.py:597
  24.1 0.0 copy-done.6
  24.1 0.1 copy.14
  24.2 0.5 fusion
  24.8 0.0 copy-done.7
  24.8 0.4 concatenate.18
  25.2 1.2 %collective-permute-start.2 = (bf16[224,128]{1,0:T(8,128)(2,1)S(1)}, bf16[224,128]{1,0:T(8,128)(2,1)S(1)}, u32[]{:S(2)}, u32[]{:S(2)}) collective-permute-start(bf16[224,128]{1,0:T(8,128)(2,1)S(1)} %get-tuple-element.18), channel_id=1, source_target_pairs={{0,1},{1,0},{2,3},{3,2},{64,65},{65,64},{66,67},{67,66},{4,5},{5,4... | collective-permute-start | bytes 172040 | tf_op jit(solution)/shard_map/ppermute | solution.py:595
  26.4 0.8 collective-permute-start.3
  27.3 0.0 copy-done.5
  27.3 6.4 %collective-permute-done.2.rc = bf16[224,128]{1,0:T(8,128)(2,1)S(1)} collective-permute-done((bf16[224,128]{1,0:T(8,128)(2,1)S(1)}, bf16[224,128]{1,0:T(8,128)(2,1)S(1)}, u32[]{:S(2)}, u32[]{:S(2)}) %collective-permute-start.2) | collective-permute-done | bytes 57376 | tf_op jit(solution)/shard_map/ppermute | solution.py:595
  33.7 0.0 collective-permute-done.3.rd
  33.7 1.9 %cells.1.ct = bf16[28,144,128]{2,1,0:T(8,128)(2,1)S(1)} custom-call(bf16[16,128,128]{2,1,0:T(8,128)(2,1)S(1)} %get-tuple-element.13.xown, bf16[6,128,128]{2,1,0:T(8,128)(2,1)S(1)} %collective-permute-done.ra, bf16[6,128,128]{2,1,0:T(8,128)(2,1)S(1)} %collective-permute-done.1.rb, bf16[224,128]{1,0:T(8,128)(2,1)S(1)} %collective-permute-done.2.rc, ...), custom_call_target="tpu_custom_call" | custom-call | bytes 8388608 | tf_op jit(solution)/shard_map/cells/pallas_call | solution.py:226
  35.6 5.0 %all-to-all-done.recv = bf16[128,24,128]{2,1,0:T(8,128)(2,1)S(1)} async-done(((bf16[128,24,128]{2,1,0:T(8,128)(2,1)}), bf16[128,24,128]{2,1,0:T(8,128)(2,1)S(1)}, u32[]{:S(2)}, u32[]{:S(2)}) %all-to-all-start) | async-done | bytes 786464 | tf_op jit(solution)/shard_map/all_to_all | solution.py:597
  40.5 0.0 copy-done.4
  40.5 40.6 %main.1 = (bf16[16,144,256]{2,1,0:T(8,128)(2,1)S(1)}, bf16[128,24,128]{2,1,0:T(8,128)(2,1)}) custom-call(bf16[128,24,128]{2,1,0:T(8,128)(2,1)S(1)} %all-to-all-done.recv, bf16[28,144,128]{2,1,0:T(8,128)(2,1)S(1)} %cells.1.ct, bf16[256,512]{1,0:T(8,128)(2,1)S(1)} %maximum_maximum_fusion.wbig, f32[4,256]{1,0:T(4,128)S(1)} %copy-done.4, ...), custom_call_target="tpu_custom_call" | custom-call | tf_op jit(solution)/shard_map/main/pallas_call | solution.py:462
  81.1 0.0 copy-start.1
  81.1 1.0 copy-done.1
  82.2 0.0 copy-start.2
  82.2 6.7 %all-to-all-start.1 = ((bf16[128,24,128]{2,1,0:T(8,128)(2,1)}), bf16[128,24,128]{2,1,0:T(8,128)(2,1)S(1)}, u32[]{:S(2)}, u32[]{:S(2)}) async-start(bf16[128,24,128]{2,1,0:T(8,128)(2,1)} %get-tuple-element.21.after), calls=%async_computation.1 | async-start | bytes 1572864 | tf_op jit(solution)/shard_map/all_to_all | solution.py:615
  88.9 2.8 %blank.1.zero = f32[45,78,180]{2,1,0:T(8,128)} custom-call(bf16[128,24,128]{2,1,0:T(8,128)(2,1)} %get-tuple-element.21.after), custom_call_target="tpu_custom_call" | custom-call | bytes 4194304 | tf_op jit(solution)/shard_map/blank/pallas_call | solution.py:516
  91.7 0.0 copy-done.2
  91.7 0.7 head.1
  92.4 0.8 copy.15
  93.2 12.1 %all-to-all-done.1 = bf16[128,24,128]{2,1,0:T(8,128)(2,1)S(1)} async-done(((bf16[128,24,128]{2,1,0:T(8,128)(2,1)}), bf16[128,24,128]{2,1,0:T(8,128)(2,1)S(1)}, u32[]{:S(2)}, u32[]{:S(2)}) %all-to-all-start.1) | async-done | bytes 786464 | tf_op jit(solution)/shard_map/all_to_all | solution.py:615
  105.3 1.6 %place.1 = f32[45,78,180]{2,1,0:T(8,128)} custom-call(s32[1]{0:T(128)S(6)} %copy.24.ro, s32[1]{0:T(128)S(6)} %copy.25.co, bf16[2,16,4,24,128]{4,3,2,1,0:T(8,128)(2,1)S(1)} %bitcast.14, f32[45,78,180]{2,1,0:T(8,128)} %blank.1.zero), custom_call_target="tpu_custom_call", output_to_operand_aliasing={{}: (3, {})} | custom-call | tf_op jit(solution)/shard_map/place/pallas_call | solution.py:572
  (10 shorter events, 0.1 us)
Async XLA Ops:
  0.6 23.5 %copy-start.6 = (bf16[78,256]{1,0:T(8,128)(2,1)S(1)}, bf16[78,256]{1,0:T(8,128)(2,1)}, u32[]{:S(2)}) copy-start(bf16[78,256]{1,0:T(8,128)(2,1)} %param.14) | copy-start | bytes 119812
  0.6 24.1 %copy-start.7 = (bf16[4,256]{1,0:T(4,128)(2,1)S(1)}, bf16[4,256]{1,0:T(4,128)(2,1)}, u32[]{:S(2)}) copy-start(bf16[4,256]{1,0:T(4,128)(2,1)} %param.15) | copy-start | bytes 6148
  1.7 0.7 copy-start.3
  2.6 10.3 %collective-permute-start.1 = (bf16[6,128,128]{2,1,0:T(8,128)(2,1)S(1)}, bf16[6,128,128]{2,1,0:T(8,128)(2,1)S(1)}, u32[]{:S(2)}, u32[]{:S(2)}) collective-permute-start(bf16[6,128,128]{2,1,0:T(8,128)(2,1)S(1)} %get-tuple-element.14), channel_id=1, source_target_pairs={{4,8},{8,4},{12,16},{16,12},{20,24},{24,20},{28,32},{32,28},{36,40... | collective-permute-start | bytes 589832 | tf_op jit(solution)/shard_map/ppermute | solution.py:589
  3.3 9.6 %collective-permute-start = (bf16[6,128,128]{2,1,0:T(8,128)(2,1)S(1)}, bf16[6,128,128]{2,1,0:T(8,128)(2,1)S(1)}, u32[]{:S(2)}, u32[]{:S(2)}) collective-permute-start(bf16[6,128,128]{2,1,0:T(8,128)(2,1)S(1)} %get-tuple-element.12.after), channel_id=1, source_target_pairs={{0,4},{4,0},{8,12},{12,8},{16,20},{20,16},{24,28},{28,24},{32,36},... | collective-permute-start | bytes 589832 | tf_op jit(solution)/shard_map/ppermute | solution.py:588
  7.6 1.5 %copy-start = (bf16[45,78,180]{2,1,0:T(8,128)(2,1)S(1)}, bf16[45,78,180]{2,1,0:T(8,128)(2,1)}, u32[]{:S(2)}) copy-start(bf16[45,78,180]{2,1,0:T(8,128)(2,1)} %coarse.1) | copy-start | bytes 3790804
  9.1 18.2 %copy-start.5 = (bf16[256,78]{0,1:T(8,128)(2,1)S(1)}, bf16[256,78]{0,1:T(8,128)(2,1)}, u32[]{:S(2)}) copy-start(bf16[256,78]{0,1:T(8,128)(2,1)} %param.18) | copy-start | bytes 119812
  13.2 27.3 %copy-start.4 = (f32[4,256]{1,0:T(4,128)S(1)}, f32[4,256]{1,0:T(4,128)}, u32[]{:S(2)}) copy-start(f32[4,256]{1,0:T(4,128)} %gains.1) | copy-start | bytes 12292
  13.2 27.3 %all-to-all-start = ((bf16[128,24,128]{2,1,0:T(8,128)(2,1)}), bf16[128,24,128]{2,1,0:T(8,128)(2,1)S(1)}, u32[]{:S(2)}, u32[]{:S(2)}) async-start(bf16[128,24,128]{2,1,0:T(8,128)(2,1)} %pack.1), calls=%async_computation | async-start | bytes 1572864 | tf_op jit(solution)/shard_map/all_to_all | solution.py:597
  25.2 8.4 %collective-permute-start.2 = (bf16[224,128]{1,0:T(8,128)(2,1)S(1)}, bf16[224,128]{1,0:T(8,128)(2,1)S(1)}, u32[]{:S(2)}, u32[]{:S(2)}) collective-permute-start(bf16[224,128]{1,0:T(8,128)(2,1)S(1)} %get-tuple-element.18), channel_id=1, source_target_pairs={{0,1},{1,0},{2,3},{3,2},{64,65},{65,64},{66,67},{67,66},{4,5},{5,4... | collective-permute-start | bytes 172040 | tf_op jit(solution)/shard_map/ppermute | solution.py:595
  26.4 7.3 %collective-permute-start.3 = (bf16[224,128]{1,0:T(8,128)(2,1)S(1)}, bf16[224,128]{1,0:T(8,128)(2,1)S(1)}, u32[]{:S(2)}, u32[]{:S(2)}) collective-permute-start(bf16[224,128]{1,0:T(8,128)(2,1)S(1)} %get-tuple-element.19), channel_id=1, source_target_pairs={{1,2},{2,1},{3,64},{64,3},{65,66},{66,65},{5,6},{6,5},{7,68},{68,7... | collective-permute-start | bytes 172040 | tf_op jit(solution)/shard_map/ppermute | solution.py:596
  81.1 1.0 copy-start.1
  82.2 9.5 %copy-start.2 = (bf16[16,144,256]{2,1,0:T(8,128)(2,1)S(1)}, bf16[16,144,256]{2,1,0:T(8,128)(2,1)}, u32[]{:S(2)}) copy-start(bf16[16,144,256]{2,1,0:T(8,128)(2,1)} %copy-done.1) | copy-start | bytes 3538948
  82.2 23.2 %all-to-all-start.1 = ((bf16[128,24,128]{2,1,0:T(8,128)(2,1)}), bf16[128,24,128]{2,1,0:T(8,128)(2,1)S(1)}, u32[]{:S(2)}, u32[]{:S(2)}) async-start(bf16[128,24,128]{2,1,0:T(8,128)(2,1)} %get-tuple-element.21.after), calls=%async_computation.1 | async-start | bytes 1572864 | tf_op jit(solution)/shard_map/all_to_all | solution.py:615

commit v6 on v5

--- a/solution.py
+++ b/solution.py
@@ -94,10 +94,10 @@
     lj = iota((144, LON_DEV), 1)
     q = iota((144, LON_DEV), 0)
     tail = q - 80
-    j_tail = jnp.where((tail & 7) < 4, 8 * (tail >> 3) + 8 + (tail & 1), -100000)
+    j_tail = jnp.where((tail & 7) < 6, 8 * (tail >> 3) + 8 + (tail & 1), -100000)
     j = jnp.where(q < 80, jnp.where(q < 66, q, -100000), j_tail)
     sel = one_hot(lj == off + j)
-    prod[...] = jnp.zeros_like(prod)
+    prod[:, :, CIN:] = jnp.zeros((18, 144, 128 - CIN), F32)
     copy.wait()
 
     def rows(g, _):
@@ -109,33 +109,36 @@
         return 0
 
     lax.fori_loop(0, 3, rows, 0)
-    lane = iota((144, 128), 1)
-    is_0 = lane < 40
-    is_1 = lane < 80
-    low = iota((64, 128), 0)
-    low = (low & 7) < 2
-
-    def dest(r, _):
-        p0 = prod[r]
-        p1 = prod[r + 1]
-        p2 = prod[r + 2]
-        up = pltpu.roll(p1, 40, 1)
-        m0 = jnp.where(is_0, p0, jnp.where(is_1, up, pltpu.roll(p2, 80, 1)))
-        m1 = jnp.where(is_0, pltpu.roll(p0, 88, 1), jnp.where(is_1, p1, pltpu.roll(p2, 40, 1)))
-        tails = jnp.where(low, m0[80:], m1[80:])
+    part = iota((144, 128), 1) >> 5
+    low = iota((64, 128), 0) & 7
+
+    def dest(r):
+        ms = []
+        for h in range(3):
+            m = None
+            for k in range(4):
+                p = prod[2 * r + k]
+                p = p if k == h else pltpu.roll(p, 32 * (k - h) % 128, 1)
+                m = p if m is None else jnp.where(part == k, p, m)
+            ms.append(m)
+        tails = jnp.where(low < 2, ms[0][80:], jnp.where(low < 4, ms[1][80:], ms[2][80:]))
         for cc in range(8):
-            d = (cc // 4) * 64 + r * 4 + cc % 4
+            d = (cc // 4) * 32 + r * 4 + cc % 4
             sl = slice(8 * cc, 8 * cc + 8)
-            send[d] = jnp.concatenate([m0[sl], m1[sl], tails[sl]], axis=0).astype(BF)
-        return 0
-
-    lax.fori_loop(0, 16, dest, 0)
+            send[d] = jnp.concatenate([m[sl] for m in ms] + [tails[sl]], axis=0).astype(BF)
+
+    def dests(g, _):
+        for k in range(2):
+            dest(2 * g + k)
+        return 0
+
+    lax.fori_loop(0, 4, dests, 0)
 
 
 def pack(ro, co, coarse, after):
     return pl.pallas_call(
         pack_kernel,
-        out_shape=jax.ShapeDtypeStruct((128, 24, 128), BF),
+        out_shape=jax.ShapeDtypeStruct((64, 32, 128), BF),
         in_specs=[SM, SM, pl.BlockSpec(memory_space=pltpu.HBM), pl.BlockSpec(memory_space=pl.ANY)],
         out_specs=VM,
         scratch_shapes=[
@@ -144,7 +147,7 @@
             pltpu.SemaphoreType.DMA(()),
         ],
         cost_estimate=pl.CostEstimate(flops=0, bytes_accessed=8 * MB, transcendentals=0),
-        compiler_params=pltpu.CompilerParams(vmem_limit_bytes=16 * MB),
+        compiler_params=pltpu.CompilerParams(vmem_limit_bytes=57 * MB),
         name="pack",
     )(ro, co, coarse, after)
 
@@ -234,8 +237,40 @@
     )(xown, ra, rb, rc, rd)
 
 
+def fold_kernel(recv, out):
+    out[...] = jnp.sum(recv[...].astype(F32), axis=0).astype(BF)
+
+
+def fold(recv):
+    return pl.pallas_call(
+        fold_kernel,
+        out_shape=jax.ShapeDtypeStruct((32, 128), BF),
+        in_specs=[VM],
+        out_specs=VM,
+        compiler_params=pltpu.CompilerParams(vmem_limit_bytes=4 * MB),
+        name="fold",
+    )(recv)
+
+
+def spread_kernel(mine, other, out):
+    o = (mine[...] + other[...]).astype(BF)
+    for d in range(64):
+        out[d] = o
+
+
+def spread(mine, other):
+    return pl.pallas_call(
+        spread_kernel,
+        out_shape=jax.ShapeDtypeStruct((64, 32, 128), BF),
+        in_specs=[VM] * 2,
+        out_specs=VM,
+        compiler_params=pltpu.CompilerParams(vmem_limit_bytes=4 * MB),
+        name="spread",
+    )(mine, other)
+
+
 def main_kernel(
-    recv, ct, wbig, gains, kern_hbm, wl, deep_out, msg,
+    win_a, win_b, ct, wbig, gains, kern_hbm, wl, deep_out, msg,
     vup, hid_a, hid_b, act_a, act_b, act_c, cv, hs_s, ds_s, gsum, kern, pair, sem,
 ):
     ri = lax.axis_index("row")
@@ -243,19 +278,22 @@
     load = pltpu.make_async_copy(kern_hbm, kern, sem.at[0])
     load.start()
 
-    win = jnp.sum(recv[...].astype(F32), axis=0)
-    m = iota((EC, 48), 0)
-    q = iota((EC, 48), 1)
-    j0 = jnp.where(q < 8, q, jnp.where((q == 16) | (q == 17), q - 8, -10))
-    q1 = q - 24
-    j1 = jnp.where((q1 >= 8) & (q1 < 16), q1 - 8, jnp.where((q1 == 18) | (q1 == 19), q1 - 10, -10))
-    coef = col_weight(ext_col(m), jnp.where(q < 24, j0, j1)).astype(BF)
-    lane = iota((24, 128), 1)
+    win = win_a[...].astype(F32) + win_b[...].astype(F32)
+    odd = (ri & 1) == 1
+    win = jnp.where(odd, pltpu.roll(win, 96, 1), win)
+    m = iota((EC, 96), 0)
+    q = iota((EC, 96), 1)
+    h = q >> 5
+    q = q & 31
+    j = jnp.where((q >> 3) == h, q & 7, jnp.where((q >> 1) == 12 + h, 8 + (q & 1), -10))
+    coef = col_weight(ext_col(m), j).astype(BF)
+    lane = iota((32, 128), 1)
     for k in range(3):
-        w0 = jnp.where(lane < 40, pltpu.roll(win, (128 - 40 * k) % 128, 1) if k else win, 0.0)
-        w1 = pltpu.roll(win, (168 - 40 * k) % 128, 1) if k != 1 else win
-        w1 = jnp.where((lane >= 40) & (lane < CIN), w1, 0.0)
-        vup[k] = dotf(coef, jnp.concatenate([w0, w1], axis=0).astype(BF))
+        parts = []
+        for h in range(3):
+            w = win if h == k else pltpu.roll(win, 32 * (h - k) % 128, 1)
+            parts.append(jnp.where(((lane >> 5) == h) & (lane < CIN), w, 0.0))
+        vup[k] = dotf(coef, jnp.concatenate(parts, axis=0).astype(BF))
 
     CK = 48
     col_ok = []
@@ -426,7 +464,7 @@
 
     e = ext_col(iota((32, EC), 1))
     qq = iota((32, EC), 0)
-    j = jnp.where(qq < 10, qq, jnp.where(qq < 20, qq - 10, -10))
+    j = jnp.where(qq < 10, qq, jnp.where(qq < 20, qq - 10, jnp.where(qq < 30, qq - 20, -10)))
     own = (e >= HC) & (e < HC + TC)
     cols_t = jnp.where(own, col_weight(e, j), 0.0).astype(BF)
     gsum[...] = jnp.zeros_like(gsum)
@@ -447,25 +485,20 @@
     g_hi = g.astype(BF)
     g_lo = (g - g_hi.astype(F32)).astype(BF)
     o = dotf(g_hi, wl[...]) + dotf(g_lo, wl[...])
-    o = jnp.where(iota((32, 128), 0) < 10, o[:, :128], o[:, 128:]).astype(BF)[:24]
-
-    def spread(d, _):
-        for k in range(8):
-            msg[8 * d + k] = o
-        return 0
-
-    lax.fori_loop(0, 16, spread, 0)
+    row = iota((32, 128), 0)
+    o = jnp.where(row < 10, o[:, :128], jnp.where(row < 20, o[:, 128:256], o[:, 256:]))
+    msg[...] = jnp.where(odd, pltpu.roll(o, 32, 1), o)
     save.wait()
 
 
-def main(recv, ct, wbig, gains, kern, wl):
+def main(win_a, win_b, ct, wbig, gains, kern, wl):
     return pl.pallas_call(
         main_kernel,
         out_shape=[
             jax.ShapeDtypeStruct((TR, EC, W), BF),
-            jax.ShapeDtypeStruct((128, 24, 128), BF),
+            jax.ShapeDtypeStruct((32, 128), F32),
         ],
-        in_specs=[VM] * 4 + [pl.BlockSpec(memory_space=pl.ANY), VM],
+        in_specs=[VM] * 5 + [pl.BlockSpec(memory_space=pl.ANY), VM],
         out_specs=[pl.BlockSpec(memory_space=pltpu.HBM), VM],
         scratch_shapes=[
             pltpu.VMEM((3, EC, 128), F32),
@@ -482,9 +515,9 @@
             pltpu.VMEM((BLOCKS, 2, 3, W, W), BF),
             pltpu.SemaphoreType.DMA((2,)),
         ],
-        compiler_params=pltpu.CompilerParams(vmem_limit_bytes=48 * MB),
+        compiler_params=pltpu.CompilerParams(vmem_limit_bytes=50 * MB),
         name="main",
-    )(recv, ct, wbig, gains, kern, wl)
+    )(win_a, win_b, ct, wbig, gains, kern, wl)
 
 
 def head_kernel(hid, wht, after, fine, mixed):
@@ -528,26 +561,26 @@
 def place_kernel(ro, co, recv, zero, out, acc, sem):
     first_row = ro[0] - 1 - LAT_DEV * lax.axis_index("row")
     off = co[0] - 1 - LON_DEV * col_place()
-    q = iota((192, 512), 0)
-    lane = iota((192, 512), 1)
-    h = lane >> 8
+    q = iota((256, 768), 0)
+    lane = iota((256, 768), 1)
     lj = lane & 255
-    c = q // 24
-    j = q - c * 24 - 10 * h
-    sel = one_hot((j >= 0) & (j < 10) & (lj == off + 8 * c + j) & (lj < LON_DEV))
+    j = (q & 31) - 10 * (lane >> 8)
+    sel = one_hot((j >= 0) & (j < 10) & (lj == off + 8 * (q >> 5) + j) & (lj < LON_DEV))
     acc[...] = jnp.zeros_like(acc)
 
     def rows(g, _):
         for u in range(4):
             r = 4 * g + u
-            a = recv[:, r].astype(F32).reshape(192, 128).astype(BF)
-            o = dotf(a, sel, TN)
-            for k in range(3):
-                acc[r + k, :40] = acc[r + k, :40] + o[40 * k : 40 * k + 40, :LON_DEV]
-                acc[r + k, 40:] = acc[r + k, 40:] + o[40 * k : 40 * k + 38, 256 : 256 + LON_DEV]
-        return 0
-
-    lax.fori_loop(0, 4, rows, 0)
+            o = dotf(recv[:, r].reshape(256, 128), sel, TN)
+            for k in range(4):
+                for h in range(3):
+                    n = min(32, CIN - 32 * h)
+                    sl = slice(32 * h, 32 * h + n)
+                    part = o[32 * k : 32 * k + n, 256 * h : 256 * h + LON_DEV]
+                    acc[2 * r + k, sl] = acc[2 * r + k, sl] + part
+        return 0
+
+    lax.fori_loop(0, 2, rows, 0)
     lo = jnp.clip(-first_row, 0, 18)
     hi = jnp.clip(LAT_DEV - first_row, lo, 18)
 
@@ -594,7 +627,17 @@
     send, pc, pd = lax.optimization_barrier((send, pc, pd))
     rc = lax.ppermute(pc, ("sec", "col"), near)
     rd = lax.ppermute(pd, ("sec", "col"), far)
-    recv = lax.all_to_all(send, ("sec", "row", "col"), 0, 0, tiled=True)
+    groups = [
+        [sec * 64 + row * 4 + col for sec in range(2) for row in range(core, 16, 2) for col in range(4)]
+        for core in range(2)
+    ]
+
+    def swap(x):
+        return lax.all_to_all(x, ("sec", "row", "col"), 0, 0, axis_index_groups=groups, tiled=True)
+
+    mates = [(i, i ^ 1) for i in range(16)]
+    win_a = fold(swap(send))
+    win_b = lax.ppermute(win_a, "row", mates)
     ct = cells(xown, ra, rb, rc, rd)
 
     wht = w_head.T
@@ -607,13 +650,14 @@
         1,
     )
     wht80 = jnp.concatenate([wht, zero((2, W), BF)], 0)
-    wl = jnp.concatenate([w_lift, zero((2, W), BF)], 0).reshape(2, 40, W).transpose(2, 0, 1)
+    wl = jnp.concatenate([w_lift, zero((18, W), BF)], 0).reshape(3, 32, W).transpose(2, 0, 1)
     wl = jnp.concatenate(
-        [jnp.pad(wl, ((0, 0), (0, 0), (40 * k, 88 - 40 * k))).reshape(W, 256) for k in range(3)], 0
+        [jnp.pad(wl, ((0, 0), (0, 0), (32 * k, 96 - 32 * k))).reshape(W, 384) for k in range(3)], 0
     )
-    deep, msg = main(recv, ct, wbig, gains, kern, wl)
-    back = lax.all_to_all(msg, ("sec", "row", "col"), 0, 0, tiled=True)
-    return head(deep, wht80, msg), place(ro, co, back.reshape(2, 16, 4, 24, 128), blank(msg))
+    deep, own = main(win_a, win_b, ct, wbig, gains, kern, wl)
+    msg = spread(own, lax.ppermute(own, "row", mates))
+    back = swap(msg)
+    return head(deep, wht80, msg), place(ro, co, back.reshape(2, 8, 4, 32, 128), blank(msg))
 
 
 def solution(mesh):

time: 108 us -> 103 us (0.954)
  waiting for transfers between devices: 23.5 us -> 20.5 us
  local copies, waits for them, and re-layouts: 6.2 us -> 3.57 us
  starting transfers between devices: 23.3 us -> 24.8 us
    ppermute x1, waiting for transfers between devices: 6.37 us -> 0.01 us  [shards(): rc = lax.ppermute(pc, ('sec', 'col'), near)]
    all_to_all x2, waiting for transfers between devices: 17.1 us -> 19.6 us  [swap(): lax.all_to_all(x, ('sec', 'row', 'col'), 0, 0, axis_index_groups=groups,...]
    unnamed x19 -> x14, local copies, waits for them, and re-layouts: 5.17 us -> 2.66 us
    pallas_call x1 -> x3, Pallas kernels: 3.76 us -> 4.57 us  [the longest x1 3.65 us: pack(): pl.pallas_call(pack_kernel, out_shape=jax.ShapeDtypeStruct((64, 32, 128),...]
  transfers between devices with their start and end apart: 6 -> 8, of which waited for: 3 -> 3; matrix products, arithmetic and copies ran while one was open for 2% -> 2% of each run, Pallas kernels for 9% -> 9%
where the time goes in v6:
time: 103 us; the launch traced here: 102 us
  Pallas kernels  51.1 us (50%)
  starting transfers between devices  24.8 us (24%)
  waiting for transfers between devices  20.5 us (20%)
  local copies, waits for them, and re-layouts  3.57 us (3%)
  between operations  2.38 us (2%)
    pallas_call x1, Pallas kernels, main(): pl.pallas_call(main_kernel, out_shape=[jax.ShapeDtypeStruct((TR, EC, W),...  39.6 us
    all_to_all x2, waiting for transfers between devices, swap(): lax.all_to_all(x, ('sec', 'row', 'col'), 0, 0, axis_index_groups=groups,...  19.6 us
    all_to_all x2, starting transfers between devices, swap(): lax.all_to_all(x, ('sec', 'row', 'col'), 0, 0, axis_index_groups=groups,...  18 us
    pallas_call x1, Pallas kernels, pack(): pl.pallas_call(pack_kernel, out_shape=jax.ShapeDtypeStruct((64, 32, 128),...  3.65 us
    ppermute x1, starting transfers between devices, shards(): ra = lax.ppermute(pa, 'row', near)  3 us
    pallas_call x1, Pallas kernels, blank(): pl.pallas_call(blank_kernel, out_shape=jax.ShapeDtypeStruct((LAT_DEV, CIN...  2.76 us
    unnamed x14, local copies, waits for them, and re-layouts  2.66 us
  transfers between devices with their start and end apart: 8, of which 3 were waited for; matrix products, arithmetic and copies ran while one was open for 2% of the time, Pallas kernels for 9%

profile of v6, /device:TPU:0, one launch (start us, length us, event | category | flops | bytes accessed | tf_op | source)
XLA Modules:
  0.0 102.4 jit_solution(3859146134568040875)
XLA Ops:
  0.6 1.1 %copy.16.cot = bf16[16,78,128]{2,1,0:T(8,128)(2,1)S(1)} copy(bf16[16,78,128]{2,0,1:T(8,128)(2,1)} %param.19) | data formatting | bytes 638976 | tf_op args[9]
  1.7 0.0 copy-start.1
  1.7 0.7 copy-done.1
  2.4 0.1 own_rows.1
  2.5 0.0 copy-start
  2.6 0.7 collective-permute-start.1
  3.2 3.0 %collective-permute-start = (bf16[6,128,128]{2,1,0:T(8,128)(2,1)S(1)}, bf16[6,128,128]{2,1,0:T(8,128)(2,1)S(1)}, u32[]{:S(2)}, u32[]{:S(2)}) collective-permute-start(bf16[6,128,128]{2,1,0:T(8,128)(2,1)S(1)} %get-tuple-element.12.after), channel_id=1, source_target_pairs={{0,4},{4,0},{8,12},{12,8},{16,20},{20,16},{24,28},{28,24},{32,36},... | collective-permute-start | bytes 589832 | tf_op jit(solution)/shard_map/ppermute | solution.py:621
  7.5 0.0 copy-done
  7.5 3.6 %pack.1 = bf16[64,32,128]{2,1,0:T(8,128)(2,1)} custom-call(s32[1]{0:T(128)S(6)} %copy.22.ro, s32[1]{0:T(128)S(6)} %copy.23.co, bf16[45,78,180]{2,1,0:T(8,128)(2,1)} %coarse.1, bf16[6,128,128]{2,1,0:T(8,128)(2,1)} %copy-done), custom_call_target="tpu_custom_call" | custom-call | bytes 8388608 | tf_op jit(solution)/shard_map/pack/pallas_call | solution.py:139
  11.2 0.0 copy-start.4
  11.2 0.0 collective-permute-done.1.rb
  11.2 0.0 collective-permute-done.ra
  11.2 0.3 edges.1
  11.6 11.9 %all-to-all-start = ((bf16[64,32,128]{2,1,0:T(8,128)(2,1)}), bf16[64,32,128]{2,1,0:T(8,128)(2,1)S(1)}, u32[]{:S(2)}, u32[]{:S(2)}) async-start(bf16[64,32,128]{2,1,0:T(8,128)(2,1)} %pack.1), calls=%async_computation | async-start | bytes 1048576 | tf_op jit(solution)/shard_map/all_to_all | solution.py:636
  23.5 0.0 copy-done.4
  23.5 0.0 copy-start.5
  23.6 0.2 copy.17
  23.8 0.2 copy.19
  24.0 0.0 copy-start.3
  24.0 0.2 copy.18
  24.2 0.1 copy-done.5
  24.2 0.3 concatenate.18
  24.6 0.1 pad_maximum_fusion.wl
  24.6 1.6 %collective-permute-start.3 = (bf16[224,128]{1,0:T(8,128)(2,1)S(1)}, bf16[224,128]{1,0:T(8,128)(2,1)S(1)}, u32[]{:S(2)}, u32[]{:S(2)}) collective-permute-start(bf16[224,128]{1,0:T(8,128)(2,1)S(1)} %get-tuple-element.18), channel_id=1, source_target_pairs={{0,1},{1,0},{2,3},{3,2},{64,65},{65,64},{66,67},{67,66},{4,5},{5,4... | collective-permute-start | bytes 172040 | tf_op jit(solution)/shard_map/ppermute | solution.py:628
  26.3 0.7 collective-permute-start.4
  27.0 10.3 %all-to-all-done.recv = bf16[64,32,128]{2,1,0:T(8,128)(2,1)S(1)} async-done(((bf16[64,32,128]{2,1,0:T(8,128)(2,1)}), bf16[64,32,128]{2,1,0:T(8,128)(2,1)S(1)}, u32[]{:S(2)}, u32[]{:S(2)}) %all-to-all-start) | async-done | bytes 524320 | tf_op jit(solution)/shard_map/all_to_all | solution.py:636
  37.3 0.1 fold.1.win_a
  37.3 0.3 collective-permute-start.2
  37.6 0.0 copy-done.3
  37.6 0.0 copy-start.2
  37.7 0.0 collective-permute-done.3.rc
  37.7 0.0 collective-permute-done.4.rd
  37.7 1.9 %cells.1.ct = bf16[28,144,128]{2,1,0:T(8,128)(2,1)S(1)} custom-call(bf16[16,128,128]{2,1,0:T(8,128)(2,1)S(1)} %get-tuple-element.13.xown, bf16[6,128,128]{2,1,0:T(8,128)(2,1)S(1)} %collective-permute-done.ra, bf16[6,128,128]{2,1,0:T(8,128)(2,1)S(1)} %collective-permute-done.1.rb, bf16[224,128]{1,0:T(8,128)(2,1)S(1)} %collective-permute-done.3.rc, ...), custom_call_target="tpu_custom_call" | custom-call | bytes 8388608 | tf_op jit(solution)/shard_map/cells/pallas_call | solution.py:229
  39.6 0.0 collective-permute-done.2.win_b
  39.6 0.0 copy-done.2
  39.6 39.6 %main.1 = (bf16[16,144,256]{2,1,0:T(8,128)(2,1)S(1)}, f32[32,128]{1,0:T(8,128)S(1)}) custom-call(bf16[32,128]{1,0:T(8,128)(2,1)S(1)} %fold.1.win_a, bf16[32,128]{1,0:T(8,128)(2,1)S(1)} %collective-permute-done.2.win_b, bf16[28,144,128]{2,1,0:T(8,128)(2,1)S(1)} %cells.1.ct, bf16[256,512]{1,0:T(8,128)(2,1)S(1)} %maximum_maximum_fusion.wbig, ...), custom_call_target="tpu_custom_call" | custom-call | tf_op jit(solution)/shard_map/main/pallas_call | solution.py:495
  79.2 0.6 collective-permute-start.5
  79.7 0.8 collective-permute-done.5.other
  80.6 0.8 spread.1.after
  81.4 6.0 %all-to-all-start.1 = ((bf16[64,32,128]{2,1,0:T(8,128)(2,1)}), bf16[64,32,128]{2,1,0:T(8,128)(2,1)S(1)}, u32[]{:S(2)}, u32[]{:S(2)}) async-start(bf16[64,32,128]{2,1,0:T(8,128)(2,1)} %spread.1.after), calls=%async_computation.1 | async-start | bytes 1048576 | tf_op jit(solution)/shard_map/all_to_all | solution.py:636
  87.4 2.8 %blank.1.zero = f32[45,78,180]{2,1,0:T(8,128)} custom-call(bf16[64,32,128]{2,1,0:T(8,128)(2,1)} %spread.1.after), custom_call_target="tpu_custom_call" | custom-call | bytes 4194304 | tf_op jit(solution)/shard_map/blank/pallas_call | solution.py:549
  90.2 0.7 head.1
  90.9 0.8 copy.20
  91.7 9.3 %all-to-all-done.1 = bf16[64,32,128]{2,1,0:T(8,128)(2,1)S(1)} async-done(((bf16[64,32,128]{2,1,0:T(8,128)(2,1)}), bf16[64,32,128]{2,1,0:T(8,128)(2,1)S(1)}, u32[]{:S(2)}, u32[]{:S(2)}) %all-to-all-start.1) | async-done | bytes 524320 | tf_op jit(solution)/shard_map/all_to_all | solution.py:636
  101.1 1.2 %place.1 = f32[45,78,180]{2,1,0:T(8,128)} custom-call(s32[1]{0:T(128)S(6)} %copy.22.ro, s32[1]{0:T(128)S(6)} %copy.23.co, bf16[2,8,4,32,128]{4,3,2,1,0:T(8,128)(2,1)S(1)} %bitcast.8, f32[45,78,180]{2,1,0:T(8,128)} %blank.1.zero), custom_call_target="tpu_custom_call", output_to_operand_aliasing={{}: (3, {})} | custom-call | tf_op jit(solution)/shard_map/place/pallas_call | solution.py:605
  (8 shorter events, 0.1 us)
Async XLA Ops:
  1.7 0.7 copy-start.1
  2.5 5.0 %copy-start = (bf16[6,128,128]{2,1,0:T(8,128)(2,1)}, bf16[6,128,128]{2,1,0:T(8,128)(2,1)S(1)}, u32[]{:S(2)}) copy-start(bf16[6,128,128]{2,1,0:T(8,128)(2,1)S(1)} %get-tuple-element.12.after) | copy-start | bytes 589828
  2.6 8.7 %collective-permute-start.1 = (bf16[6,128,128]{2,1,0:T(8,128)(2,1)S(1)}, bf16[6,128,128]{2,1,0:T(8,128)(2,1)S(1)}, u32[]{:S(2)}, u32[]{:S(2)}) collective-permute-start(bf16[6,128,128]{2,1,0:T(8,128)(2,1)S(1)} %get-tuple-element.14), channel_id=1, source_target_pairs={{4,8},{8,4},{12,16},{16,12},{20,24},{24,20},{28,32},{32,28},{36,40... | collective-permute-start | bytes 589832 | tf_op jit(solution)/shard_map/ppermute | solution.py:622
  3.2 8.0 %collective-permute-start = (bf16[6,128,128]{2,1,0:T(8,128)(2,1)S(1)}, bf16[6,128,128]{2,1,0:T(8,128)(2,1)S(1)}, u32[]{:S(2)}, u32[]{:S(2)}) collective-permute-start(bf16[6,128,128]{2,1,0:T(8,128)(2,1)S(1)} %get-tuple-element.12.after), channel_id=1, source_target_pairs={{0,4},{4,0},{8,12},{12,8},{16,20},{20,16},{24,28},{28,24},{32,36},... | collective-permute-start | bytes 589832 | tf_op jit(solution)/shard_map/ppermute | solution.py:621
  11.2 12.3 %copy-start.4 = (bf16[78,256]{1,0:T(8,128)(2,1)S(1)}, bf16[78,256]{1,0:T(8,128)(2,1)}, u32[]{:S(2)}) copy-start(bf16[78,256]{1,0:T(8,128)(2,1)} %param.14) | copy-start | bytes 119812
  11.6 25.7 %all-to-all-start = ((bf16[64,32,128]{2,1,0:T(8,128)(2,1)}), bf16[64,32,128]{2,1,0:T(8,128)(2,1)S(1)}, u32[]{:S(2)}, u32[]{:S(2)}) async-start(bf16[64,32,128]{2,1,0:T(8,128)(2,1)} %pack.1), calls=%async_computation | async-start | bytes 1048576 | tf_op jit(solution)/shard_map/all_to_all | solution.py:636
  23.5 0.7 copy-start.5
  24.0 13.7 %copy-start.3 = (bf16[256,78]{0,1:T(8,128)(2,1)S(1)}, bf16[256,78]{0,1:T(8,128)(2,1)}, u32[]{:S(2)}) copy-start(bf16[256,78]{0,1:T(8,128)(2,1)} %param.18) | copy-start | bytes 119812
  24.6 13.0 %collective-permute-start.3 = (bf16[224,128]{1,0:T(8,128)(2,1)S(1)}, bf16[224,128]{1,0:T(8,128)(2,1)S(1)}, u32[]{:S(2)}, u32[]{:S(2)}) collective-permute-start(bf16[224,128]{1,0:T(8,128)(2,1)S(1)} %get-tuple-element.18), channel_id=1, source_target_pairs={{0,1},{1,0},{2,3},{3,2},{64,65},{65,64},{66,67},{67,66},{4,5},{5,4... | collective-permute-start | bytes 172040 | tf_op jit(solution)/shard_map/ppermute | solution.py:628
  26.3 11.4 %collective-permute-start.4 = (bf16[224,128]{1,0:T(8,128)(2,1)S(1)}, bf16[224,128]{1,0:T(8,128)(2,1)S(1)}, u32[]{:S(2)}, u32[]{:S(2)}) collective-permute-start(bf16[224,128]{1,0:T(8,128)(2,1)S(1)} %get-tuple-element.19), channel_id=1, source_target_pairs={{1,2},{2,1},{3,64},{64,3},{65,66},{66,65},{5,6},{6,5},{7,68},{68,7... | collective-permute-start | bytes 172040 | tf_op jit(solution)/shard_map/ppermute | solution.py:629
  37.3 2.3 %collective-permute-start.2 = (bf16[32,128]{1,0:T(8,128)(2,1)S(1)}, bf16[32,128]{1,0:T(8,128)(2,1)S(1)}, u32[]{:S(2)}, u32[]{:S(2)}) collective-permute-start(bf16[32,128]{1,0:T(8,128)(2,1)S(1)} %fold.1.win_a), channel_id=1, source_target_pairs={{0,4},{4,0},{8,12},{12,8},{16,20},{20,16},{24,28},{28,24},{32,36},... | collective-permute-start | bytes 24584 | tf_op jit(solution)/shard_map/ppermute | solution.py:640
  37.6 2.0 %copy-start.2 = (f32[4,256]{1,0:T(4,128)S(1)}, f32[4,256]{1,0:T(4,128)}, u32[]{:S(2)}) copy-start(f32[4,256]{1,0:T(4,128)} %gains.1) | copy-start | bytes 12292
  79.2 1.4 %collective-permute-start.5 = (f32[32,128]{1,0:T(8,128)S(1)}, f32[32,128]{1,0:T(8,128)S(1)}, u32[]{:S(2)}, u32[]{:S(2)}) collective-permute-start(f32[32,128]{1,0:T(8,128)S(1)} %get-tuple-element.21.mine), channel_id=1, source_target_pairs={{0,4},{4,0},{8,12},{12,8},{16,20},{20,16},{24,28},{28,24},{32,36},... | collective-permute-start | bytes 49160 | tf_op jit(solution)/shard_map/ppermute | solution.py:658
  81.4 19.6 %all-to-all-start.1 = ((bf16[64,32,128]{2,1,0:T(8,128)(2,1)}), bf16[64,32,128]{2,1,0:T(8,128)(2,1)S(1)}, u32[]{:S(2)}, u32[]{:S(2)}) async-start(bf16[64,32,128]{2,1,0:T(8,128)(2,1)} %spread.1.after), calls=%async_computation.1 | async-start | bytes 1048576 | tf_op jit(solution)/shard_map/all_to_all | solution.py:636

commit v7 on v6

--- a/solution.py
+++ b/solution.py
@@ -380,12 +380,12 @@
     load.wait()
     lax.fori_loop(1, ER // 4 + 1, lift_on, 0)
 
-    def conv(b, act, y0, transpose, between=()):
+    def conv(b, act, y0, transpose, between=(), count=4):
         between = list(between)
         dims = NT if transpose else NN
 
         def rows(k):
-            return jnp.concatenate([act[pl.ds(y0 - 1 + k + 2 * u, 1)] for u in range(4)], axis=0)
+            return jnp.concatenate([act[pl.ds(y0 - 1 + k + 2 * u, 1)] for u in range(count)], axis=0)
 
         d0, d1, d2, d3 = rows(0), rows(1), rows(2), rows(3)
         ms = []
@@ -397,21 +397,23 @@
                     kk = pair[b, k - 1, q]
                 else:
                     kk = kern[b, 0 if (k == 3) == transpose else 2, q]
-                r = dotf(t[:, dx : dx + L].reshape(4 * EC, W), kk, dims)
+                r = dotf(t[:, dx : dx + L].reshape(count * EC, W), kk, dims)
                 acc = r if acc is None else acc + r
                 for job in between[:2]:
                     job()
                 between = between[2:]
             ms.append(acc)
-        e = (ms[0] + ms[1] + ms[2]).reshape(4, EC, W)
-        o = (ms[1] - ms[2] - ms[3]).reshape(4, EC, W)
-        for u in range(4):
+        e = (ms[0] + ms[1] + ms[2]).reshape(count, EC, W)
+        o = (ms[1] - ms[2] - ms[3]).reshape(count, EC, W)
+        for u in range(count):
             cv[y0 + 2 * u] = e[u].astype(BF)
             cv[y0 + 2 * u + 1] = o[u].astype(BF)
 
-    def layer(b, lo, hi, act, transpose, after):
+    def layer(b, lo, hi, act, transpose, after, short):
+        back = 2 if short else 0
+
         def place(i):
-            return jnp.minimum(lo + 8 * i, hi - 8)
+            return jnp.minimum(lo + jnp.maximum(8 * i - back, 0), hi - 8)
 
         def rest(i):
             y0 = place(i)
@@ -421,8 +423,8 @@
             conv(b, act, place(i), transpose, rest(i - 1))
             return 0
 
-        n = (hi - lo + 7) >> 3
-        conv(b, act, place(0), transpose)
+        n = (hi - lo + back + 7) >> 3
+        conv(b, act, lo, transpose, (), 3 if short else 4)
         lax.fori_loop(1, n, unit, 0)
         for job in rest(n - 1):
             job()
@@ -436,7 +438,7 @@
             def after(y, ck, b=b, src=src, dst=dst):
                 activate(b + 1, y, ck, src[0], *dst)
 
-            layer(b, lo, hi, src[1], False, after)
+            layer(b, lo, hi, src[1], False, after, dst[0] is hid_b)
         return 0
 
     lax.fori_loop(0, 2, forward, 0)
@@ -457,7 +459,7 @@
             def after(y, ck, b=b, src=src, dst=dst):
                 grad(b, y, ck, src, dst)
 
-            layer(b, HR - b, HR + TR + b, src, True, after)
+            layer(b, HR - b, HR + TR + b, src, True, after, dst is act_a)
         return 0
 
     lax.fori_loop(0, 2, backward, 0)

time: 103 us -> 102 us (level)
  no operation moved by 1% of the time
where the time goes in v7:
time: 102 us; the launch traced here: 101 us
  Pallas kernels  50.2 us (49%)
  starting transfers between devices  24.8 us (24%)
  waiting for transfers between devices  20.5 us (20%)
  local copies, waits for them, and re-layouts  3.57 us (4%)
  between operations  2.38 us (2%)
    pallas_call x1, Pallas kernels, main(): pl.pallas_call(main_kernel, out_shape=[jax.ShapeDtypeStruct((TR, EC, W),...  38.6 us
    all_to_all x2, waiting for transfers between devices, swap(): lax.all_to_all(x, ('sec', 'row', 'col'), 0, 0, axis_index_groups=groups,...  19.6 us
    all_to_all x2, starting transfers between devices, swap(): lax.all_to_all(x, ('sec', 'row', 'col'), 0, 0, axis_index_groups=groups,...  18 us
    pallas_call x1, Pallas kernels, pack(): pl.pallas_call(pack_kernel, out_shape=jax.ShapeDtypeStruct((64, 32, 128),...  3.65 us
    ppermute x1, starting transfers between devices, shards(): ra = lax.ppermute(pa, 'row', near)  3 us
    pallas_call x1, Pallas kernels, blank(): pl.pallas_call(blank_kernel, out_shape=jax.ShapeDtypeStruct((LAT_DEV, CIN...  2.76 us
    unnamed x14, local copies, waits for them, and re-layouts  2.66 us
  transfers between devices with their start and end apart: 8, of which 3 were waited for; matrix products, arithmetic and copies ran while one was open for 2% of the time, Pallas kernels for 9%

profile of v7, /device:TPU:0, one launch (start us, length us, event | category | flops | bytes accessed | tf_op | source)
XLA Modules:
  0.0 101.5 jit_solution(16607223032068738400)
XLA Ops:
  0.6 1.1 %copy.16.cot = bf16[16,78,128]{2,1,0:T(8,128)(2,1)S(1)} copy(bf16[16,78,128]{2,0,1:T(8,128)(2,1)} %param.19) | data formatting | bytes 638976 | tf_op args[9]
  1.7 0.0 copy-start.1
  1.7 0.7 copy-done.1
  2.4 0.1 own_rows.1
  2.5 0.0 copy-start
  2.6 0.7 collective-permute-start.1
  3.2 3.0 %collective-permute-start = (bf16[6,128,128]{2,1,0:T(8,128)(2,1)S(1)}, bf16[6,128,128]{2,1,0:T(8,128)(2,1)S(1)}, u32[]{:S(2)}, u32[]{:S(2)}) collective-permute-start(bf16[6,128,128]{2,1,0:T(8,128)(2,1)S(1)} %get-tuple-element.12.after), channel_id=1, source_target_pairs={{0,4},{4,0},{8,12},{12,8},{16,20},{20,16},{24,28},{28,24},{32,36},... | collective-permute-start | bytes 589832 | tf_op jit(solution)/shard_map/ppermute | solution.py:623
  7.5 0.0 copy-done
  7.5 3.6 %pack.1 = bf16[64,32,128]{2,1,0:T(8,128)(2,1)} custom-call(s32[1]{0:T(128)S(6)} %copy.22.ro, s32[1]{0:T(128)S(6)} %copy.23.co, bf16[45,78,180]{2,1,0:T(8,128)(2,1)} %coarse.1, bf16[6,128,128]{2,1,0:T(8,128)(2,1)} %copy-done), custom_call_target="tpu_custom_call" | custom-call | bytes 8388608 | tf_op jit(solution)/shard_map/pack/pallas_call | solution.py:139
  11.2 0.0 copy-start.4
  11.2 0.0 collective-permute-done.1.rb
  11.2 0.0 collective-permute-done.ra
  11.2 0.3 edges.1
  11.6 11.9 %all-to-all-start = ((bf16[64,32,128]{2,1,0:T(8,128)(2,1)}), bf16[64,32,128]{2,1,0:T(8,128)(2,1)S(1)}, u32[]{:S(2)}, u32[]{:S(2)}) async-start(bf16[64,32,128]{2,1,0:T(8,128)(2,1)} %pack.1), calls=%async_computation | async-start | bytes 1048576 | tf_op jit(solution)/shard_map/all_to_all | solution.py:638
  23.5 0.0 copy-done.4
  23.5 0.0 copy-start.5
  23.6 0.2 copy.17
  23.8 0.2 copy.19
  24.0 0.0 copy-start.3
  24.0 0.2 copy.18
  24.2 0.1 copy-done.5
  24.2 0.3 concatenate.18
  24.6 0.1 pad_maximum_fusion.wl
  24.6 1.6 %collective-permute-start.3 = (bf16[224,128]{1,0:T(8,128)(2,1)S(1)}, bf16[224,128]{1,0:T(8,128)(2,1)S(1)}, u32[]{:S(2)}, u32[]{:S(2)}) collective-permute-start(bf16[224,128]{1,0:T(8,128)(2,1)S(1)} %get-tuple-element.18), channel_id=1, source_target_pairs={{0,1},{1,0},{2,3},{3,2},{64,65},{65,64},{66,67},{67,66},{4,5},{5,4... | collective-permute-start | bytes 172040 | tf_op jit(solution)/shard_map/ppermute | solution.py:630
  26.3 0.7 collective-permute-start.4
  27.0 10.3 %all-to-all-done.recv = bf16[64,32,128]{2,1,0:T(8,128)(2,1)S(1)} async-done(((bf16[64,32,128]{2,1,0:T(8,128)(2,1)}), bf16[64,32,128]{2,1,0:T(8,128)(2,1)S(1)}, u32[]{:S(2)}, u32[]{:S(2)}) %all-to-all-start) | async-done | bytes 524320 | tf_op jit(solution)/shard_map/all_to_all | solution.py:638
  37.3 0.1 fold.1.win_a
  37.3 0.3 collective-permute-start.2
  37.6 0.0 copy-done.3
  37.6 0.0 copy-start.2
  37.7 0.0 collective-permute-done.3.rc
  37.7 0.0 collective-permute-done.4.rd
  37.7 1.9 %cells.1.ct = bf16[28,144,128]{2,1,0:T(8,128)(2,1)S(1)} custom-call(bf16[16,128,128]{2,1,0:T(8,128)(2,1)S(1)} %get-tuple-element.13.xown, bf16[6,128,128]{2,1,0:T(8,128)(2,1)S(1)} %collective-permute-done.ra, bf16[6,128,128]{2,1,0:T(8,128)(2,1)S(1)} %collective-permute-done.1.rb, bf16[224,128]{1,0:T(8,128)(2,1)S(1)} %collective-permute-done.3.rc, ...), custom_call_target="tpu_custom_call" | custom-call | bytes 8388608 | tf_op jit(solution)/shard_map/cells/pallas_call | solution.py:229
  39.6 0.0 collective-permute-done.2.win_b
  39.6 0.0 copy-done.2
  39.6 38.6 %main.1 = (bf16[16,144,256]{2,1,0:T(8,128)(2,1)S(1)}, f32[32,128]{1,0:T(8,128)S(1)}) custom-call(bf16[32,128]{1,0:T(8,128)(2,1)S(1)} %fold.1.win_a, bf16[32,128]{1,0:T(8,128)(2,1)S(1)} %collective-permute-done.2.win_b, bf16[28,144,128]{2,1,0:T(8,128)(2,1)S(1)} %cells.1.ct, bf16[256,512]{1,0:T(8,128)(2,1)S(1)} %maximum_maximum_fusion.wbig, ...), custom_call_target="tpu_custom_call" | custom-call | tf_op jit(solution)/shard_map/main/pallas_call | solution.py:497
  78.2 0.6 collective-permute-start.5
  78.8 0.8 collective-permute-done.5.other
  79.6 0.8 spread.1.after
  80.5 6.0 %all-to-all-start.1 = ((bf16[64,32,128]{2,1,0:T(8,128)(2,1)}), bf16[64,32,128]{2,1,0:T(8,128)(2,1)S(1)}, u32[]{:S(2)}, u32[]{:S(2)}) async-start(bf16[64,32,128]{2,1,0:T(8,128)(2,1)} %spread.1.after), calls=%async_computation.1 | async-start | bytes 1048576 | tf_op jit(solution)/shard_map/all_to_all | solution.py:638
  86.5 2.8 %blank.1.zero = f32[45,78,180]{2,1,0:T(8,128)} custom-call(bf16[64,32,128]{2,1,0:T(8,128)(2,1)} %spread.1.after), custom_call_target="tpu_custom_call" | custom-call | bytes 4194304 | tf_op jit(solution)/shard_map/blank/pallas_call | solution.py:551
  89.3 0.7 head.1
  90.0 0.8 copy.20
  90.8 9.3 %all-to-all-done.1 = bf16[64,32,128]{2,1,0:T(8,128)(2,1)S(1)} async-done(((bf16[64,32,128]{2,1,0:T(8,128)(2,1)}), bf16[64,32,128]{2,1,0:T(8,128)(2,1)S(1)}, u32[]{:S(2)}, u32[]{:S(2)}) %all-to-all-start.1) | async-done | bytes 524320 | tf_op jit(solution)/shard_map/all_to_all | solution.py:638
  100.1 1.2 %place.1 = f32[45,78,180]{2,1,0:T(8,128)} custom-call(s32[1]{0:T(128)S(6)} %copy.22.ro, s32[1]{0:T(128)S(6)} %copy.23.co, bf16[2,8,4,32,128]{4,3,2,1,0:T(8,128)(2,1)S(1)} %bitcast.8, f32[45,78,180]{2,1,0:T(8,128)} %blank.1.zero), custom_call_target="tpu_custom_call", output_to_operand_aliasing={{}: (3, {})} | custom-call | tf_op jit(solution)/shard_map/place/pallas_call | solution.py:607
  (8 shorter events, 0.1 us)
Async XLA Ops:
  1.7 0.7 copy-start.1
  2.5 5.0 %copy-start = (bf16[6,128,128]{2,1,0:T(8,128)(2,1)}, bf16[6,128,128]{2,1,0:T(8,128)(2,1)S(1)}, u32[]{:S(2)}) copy-start(bf16[6,128,128]{2,1,0:T(8,128)(2,1)S(1)} %get-tuple-element.12.after) | copy-start | bytes 589828
  2.6 8.7 %collective-permute-start.1 = (bf16[6,128,128]{2,1,0:T(8,128)(2,1)S(1)}, bf16[6,128,128]{2,1,0:T(8,128)(2,1)S(1)}, u32[]{:S(2)}, u32[]{:S(2)}) collective-permute-start(bf16[6,128,128]{2,1,0:T(8,128)(2,1)S(1)} %get-tuple-element.14), channel_id=1, source_target_pairs={{4,8},{8,4},{12,16},{16,12},{20,24},{24,20},{28,32},{32,28},{36,40... | collective-permute-start | bytes 589832 | tf_op jit(solution)/shard_map/ppermute | solution.py:624
  3.2 8.0 %collective-permute-start = (bf16[6,128,128]{2,1,0:T(8,128)(2,1)S(1)}, bf16[6,128,128]{2,1,0:T(8,128)(2,1)S(1)}, u32[]{:S(2)}, u32[]{:S(2)}) collective-permute-start(bf16[6,128,128]{2,1,0:T(8,128)(2,1)S(1)} %get-tuple-element.12.after), channel_id=1, source_target_pairs={{0,4},{4,0},{8,12},{12,8},{16,20},{20,16},{24,28},{28,24},{32,36},... | collective-permute-start | bytes 589832 | tf_op jit(solution)/shard_map/ppermute | solution.py:623
  11.2 12.3 %copy-start.4 = (bf16[78,256]{1,0:T(8,128)(2,1)S(1)}, bf16[78,256]{1,0:T(8,128)(2,1)}, u32[]{:S(2)}) copy-start(bf16[78,256]{1,0:T(8,128)(2,1)} %param.14) | copy-start | bytes 119812
  11.6 25.7 %all-to-all-start = ((bf16[64,32,128]{2,1,0:T(8,128)(2,1)}), bf16[64,32,128]{2,1,0:T(8,128)(2,1)S(1)}, u32[]{:S(2)}, u32[]{:S(2)}) async-start(bf16[64,32,128]{2,1,0:T(8,128)(2,1)} %pack.1), calls=%async_computation | async-start | bytes 1048576 | tf_op jit(solution)/shard_map/all_to_all | solution.py:638
  23.5 0.7 copy-start.5
  24.0 13.7 %copy-start.3 = (bf16[256,78]{0,1:T(8,128)(2,1)S(1)}, bf16[256,78]{0,1:T(8,128)(2,1)}, u32[]{:S(2)}) copy-start(bf16[256,78]{0,1:T(8,128)(2,1)} %param.18) | copy-start | bytes 119812
  24.6 13.0 %collective-permute-start.3 = (bf16[224,128]{1,0:T(8,128)(2,1)S(1)}, bf16[224,128]{1,0:T(8,128)(2,1)S(1)}, u32[]{:S(2)}, u32[]{:S(2)}) collective-permute-start(bf16[224,128]{1,0:T(8,128)(2,1)S(1)} %get-tuple-element.18), channel_id=1, source_target_pairs={{0,1},{1,0},{2,3},{3,2},{64,65},{65,64},{66,67},{67,66},{4,5},{5,4... | collective-permute-start | bytes 172040 | tf_op jit(solution)/shard_map/ppermute | solution.py:630
  26.3 11.4 %collective-permute-start.4 = (bf16[224,128]{1,0:T(8,128)(2,1)S(1)}, bf16[224,128]{1,0:T(8,128)(2,1)S(1)}, u32[]{:S(2)}, u32[]{:S(2)}) collective-permute-start(bf16[224,128]{1,0:T(8,128)(2,1)S(1)} %get-tuple-element.19), channel_id=1, source_target_pairs={{1,2},{2,1},{3,64},{64,3},{65,66},{66,65},{5,6},{6,5},{7,68},{68,7... | collective-permute-start | bytes 172040 | tf_op jit(solution)/shard_map/ppermute | solution.py:631
  37.3 2.3 %collective-permute-start.2 = (bf16[32,128]{1,0:T(8,128)(2,1)S(1)}, bf16[32,128]{1,0:T(8,128)(2,1)S(1)}, u32[]{:S(2)}, u32[]{:S(2)}) collective-permute-start(bf16[32,128]{1,0:T(8,128)(2,1)S(1)} %fold.1.win_a), channel_id=1, source_target_pairs={{0,4},{4,0},{8,12},{12,8},{16,20},{20,16},{24,28},{28,24},{32,36},... | collective-permute-start | bytes 24584 | tf_op jit(solution)/shard_map/ppermute | solution.py:642
  37.6 2.0 %copy-start.2 = (f32[4,256]{1,0:T(4,128)S(1)}, f32[4,256]{1,0:T(4,128)}, u32[]{:S(2)}) copy-start(f32[4,256]{1,0:T(4,128)} %gains.1) | copy-start | bytes 12292
  78.2 1.4 %collective-permute-start.5 = (f32[32,128]{1,0:T(8,128)S(1)}, f32[32,128]{1,0:T(8,128)S(1)}, u32[]{:S(2)}, u32[]{:S(2)}) collective-permute-start(f32[32,128]{1,0:T(8,128)S(1)} %get-tuple-element.21.mine), channel_id=1, source_target_pairs={{0,4},{4,0},{8,12},{12,8},{16,20},{20,16},{24,28},{28,24},{32,36},... | collective-permute-start | bytes 49160 | tf_op jit(solution)/shard_map/ppermute | solution.py:660
  80.5 19.6 %all-to-all-start.1 = ((bf16[64,32,128]{2,1,0:T(8,128)(2,1)}), bf16[64,32,128]{2,1,0:T(8,128)(2,1)S(1)}, u32[]{:S(2)}, u32[]{:S(2)}) async-start(bf16[64,32,128]{2,1,0:T(8,128)(2,1)} %spread.1.after), calls=%async_computation.1 | async-start | bytes 1048576 | tf_op jit(solution)/shard_map/all_to_all | solution.py:638
